TPU v7x, 1024 devices: a whole 4x4x32 slice. The times are simulated.
1024 devices in a mesh: row: 8 (over x, core), col: 128 (over y, z).
Axes of the slice: x: 4, y: 4, z: 32, core: 2. Of those that a mesh axis runs over, the one named last changes fastest.
Arguments:
- rhs: bfloat16 [8, 1048576], P(None, ('row', 'col')), may hold values from -6 to 6
- points: float32 [3, 1048576], P(None, ('row', 'col')), may hold values from 0 to 128
- basis: bfloat16 [4096, 256, 64], P(('row', 'col')), may hold values from -0.375 to 0.375
- transfer: bfloat16 [4096, 64, 64], P(('row', 'col')), may hold values from -0.75 to 0.75
- leaf_coupling: bfloat16 [4096, 16, 64, 64], P(('row', 'col')), may hold values from -0.1875 to 0.1875
- coupling_list: int32 [4096, 16], P(('row', 'col')), may hold values from 0 to 4095, as said below
- coupling_count: int32 [4096], P(('row', 'col')), may hold values from 1 to 16
- coarse_coupling: bfloat16 [1024, 16, 64, 64], P(('row', 'col')), may hold values from -0.09375 to 0.09375
- coarse_list: int32 [1024, 16], P(('row', 'col')), may hold values from 0 to 1023
- coarse_count: int32 [1024], P(('row', 'col')), may hold values from 1 to 16
- owner: int32 [1024], replicated, may hold values from 0 to 1023, each once
- near_list: int32 [4096, 8], P(('row', 'col')), may hold values from 0 to 4095, as said below
- near_count: int32 [4096], P(('row', 'col')), may hold values from 1 to 8
Outputs:
- product: bfloat16 [8, 1048576], P(None, ('row', 'col'))
Inputs may be any that keep to these rules, and one draw needn't show every extreme that they name: coupling_list[t, j] is a leaf whose box corner differs from t's by at most 3 in each coordinate and by 2 or 3 in at least one, each coordinate then clipped to the grid of boxes; slots at or past coupling_count[t] are padding and hold such leaves too. near_list[t, 0] is t itself; every entry is a leaf whose box touches or equals t's box, each coordinate clipped to the grid of boxes, repeats allowed; slots at or past near_count[t] are padding. `owner`: each device number appears once.
All inputs are finite; a program needn't handle non-finite values.
Results may differ from a plain program's by a relative error of at most 0.0048.
Values may be sent and summed in bfloat16 or wider, within the bound.
No kernel may reach another device: no remote copies, remote signals or barrier semaphores. Data moves between devices by JAX's collectives and lax.ppermute only.
A program may use at most 64 MiB of HBM per device.

v0:
```python
import jax
import jax.numpy as jnp
from jax import lax
from jax.sharding import PartitionSpec as P

FOUR_PI = 12.566370614359172
SOFTEN = 0.0025


def with_halo(block, sides, width):
    for axis, dim in sides:
        count = lax.axis_size(axis)
        forward = [(i, i + 1) for i in range(count - 1)]
        backward = [(target, source) for source, target in forward]
        low = lax.ppermute(
            lax.slice_in_dim(block, block.shape[dim] - width, None, axis=dim), axis, forward
        )
        high = lax.ppermute(lax.slice_in_dim(block, 0, width, axis=dim), axis, backward)
        block = jnp.concatenate([low, block, high], axis=dim)
    return block


def kernel_tile(target_points, source_points):
    gap = target_points[:, :, :, None] - source_points[:, :, None, :]
    dist_sq = gap[0] * gap[0] + gap[1] * gap[1] + gap[2] * gap[2]
    return 1.0 / (FOUR_PI * jnp.sqrt(dist_sq + SOFTEN))


def keep_edges(padded, span, axis_id):
    lower = lax.slice_in_dim(padded, 0, 1, axis=axis_id)
    middle = lax.slice_in_dim(padded, span, 2 * span, axis=axis_id)
    upper = lax.slice_in_dim(padded, 3 * span - 1, 3 * span, axis=axis_id)
    return jnp.concatenate([lower, middle, upper], axis=axis_id)


def widen_coeff(flat_coeff):
    grown = flat_coeff
    for layer in range(3):
        span = grown.shape[0]
        padded = with_halo(grown, (("row", 0), ("col", 1)), span)
        grown = keep_edges(keep_edges(padded, span, 0), span, 1)
    return grown


def per_device(
    rhs,
    points,
    basis,
    transfer,
    leaf_coupling,
    coupling_list,
    coupling_count,
    coarse_coupling,
    coarse_list,
    coarse_count,
    owner,
    near_list,
    near_count,
):
    leaf_dev = basis.shape[0]
    leaf_size = basis.shape[1]
    basis_rank = basis.shape[2]
    num_sides = rhs.shape[0]
    coarse_slots = coarse_coupling.shape[1]
    coupling_slots = coupling_list.shape[1]
    col_count = lax.axis_size("col")
    my_first = lax.axis_index("row")
    my_second = lax.axis_index("col")

    def place(leaf_ids, reach):
        device_ids = leaf_ids // leaf_dev
        first_rel = device_ids // col_count - my_first + reach
        second_rel = device_ids % col_count - my_second + reach
        block_ids = first_rel * (2 * reach + 1) + second_rel
        return (block_ids, leaf_ids % leaf_dev)

    rhs_leaf = rhs.reshape(num_sides, leaf_dev, leaf_size)
    leaf_coeff = jnp.einsum(
        "lpk,rlp->lrk", basis, rhs_leaf, preferred_element_type=jnp.float32
    ).astype(jnp.bfloat16)
    flat_coeff = leaf_coeff.reshape(1, 1, leaf_dev, num_sides * basis_rank)
    own_points = points.reshape(3, leaf_dev, leaf_size)
    near_data = jnp.concatenate([own_points, rhs_leaf.astype(jnp.float32)], axis=0)[None, None]
    widened = with_halo(near_data, (("row", 0), ("col", 1)), 1)
    widened = widened.reshape(9, 3 + num_sides, leaf_dev, leaf_size)
    wide_points = widened[:, :3]
    wide_rhs = widened[:, 3:].astype(jnp.bfloat16)
    wide_coeff = widen_coeff(flat_coeff)
    wide_coeff = wide_coeff.reshape(49 * leaf_dev, num_sides * basis_rank)
    cluster = jnp.einsum(
        "ljk,lrj->rk", transfer, leaf_coeff, preferred_element_type=jnp.float32
    ).astype(jnp.bfloat16)
    cluster = cluster.reshape(1, num_sides * basis_rank)
    coarse_live = jnp.arange(coarse_slots) < coarse_count[0]
    targets = owner[coarse_list[0]]
    all_clusters = lax.all_gather(cluster, ("row", "col"), axis=0, tiled=True)
    sources = all_clusters[targets].reshape(coarse_slots, num_sides, basis_rank)
    sources = jnp.where(coarse_live[:, None, None], sources, jnp.zeros((), jnp.bfloat16))
    coarse_field = jnp.einsum(
        "jkm,jrm->rk", coarse_coupling[0], sources, preferred_element_type=jnp.float32
    )
    coup_block, coup_leaf = place(coupling_list, 3)
    source_rows = coup_block * leaf_dev + coup_leaf
    picked = wide_coeff[source_rows].reshape(leaf_dev, coupling_slots, num_sides, basis_rank)
    live_mask = jnp.arange(coupling_slots)[None, :] < coupling_count[:, None]
    picked = jnp.where(live_mask[:, :, None, None], picked, jnp.zeros((), jnp.bfloat16))
    far_local = jnp.einsum(
        "tjkm,tjrm->trk", leaf_coupling, picked, preferred_element_type=jnp.float32
    )
    pushed = jnp.einsum(
        "tjk,rk->trj", transfer.astype(jnp.float32), coarse_field, precision=lax.Precision.HIGHEST
    )
    local_exp = (far_local + pushed).astype(jnp.bfloat16)
    far_part = jnp.einsum("tpj,trj->rtp", basis, local_exp, preferred_element_type=jnp.float32)
    near_block, near_leaf = place(near_list, 1)
    near_part = jnp.zeros((num_sides, leaf_dev, leaf_size), jnp.float32)
    for near_slot in range(near_list.shape[1]):
        block_ids = near_block[:, near_slot]
        leaf_ids = near_leaf[:, near_slot]
        source_points = jnp.moveaxis(wide_points[block_ids, :, leaf_ids], 1, 0)
        source_rhs = wide_rhs[block_ids, :, leaf_ids]
        tile_vals = kernel_tile(own_points, source_points)
        tile_vals = jnp.where(
            (near_slot < near_count)[:, None, None], tile_vals, jnp.float32(0.0)
        ).astype(jnp.bfloat16)
        near_part = near_part + jnp.einsum(
            "lpq,lrq->rlp", tile_vals, source_rhs, preferred_element_type=jnp.float32
        )
    product = (near_part + far_part).astype(jnp.bfloat16)
    return product.reshape(num_sides, leaf_dev * leaf_size)


def solution(mesh):
    in_specs = (
        P(None, ("row", "col")),
        P(None, ("row", "col")),
        P(("row", "col"), None, None),
        P(("row", "col"), None, None),
        P(("row", "col"), None, None, None),
        P(("row", "col"), None),
        P(("row", "col")),
        P(("row", "col"), None, None, None),
        P(("row", "col"), None),
        P(("row", "col")),
        P(),
        P(("row", "col"), None),
        P(("row", "col")),
    )
    out_specs = P(None, ("row", "col"))
    return jax.shard_map(
        per_device, mesh=mesh, in_specs=in_specs, out_specs=out_specs, check_vma=False
    )
```

profile of v0, /device:TPU:1, one launch (start us, length us, event | category | flops | bytes accessed | tf_op | source)
XLA Modules:
  0.0 362.2 jit_solution(17642115299744955216)
XLA Ops:
  6.5 1.1 convolution_convert_fusion
  7.8 16.1 %collective-permute-start.5 = (bf16[1,1,4,512]{3,2,1,0:T(4,128)(2,1)S(1)}, bf16[1,1,4,512]{3,2,1,0:T(4,128)(2,1)S(1)}, u32[]{:S(2)}, u32[]{:S(2)}) collective-permute-start(bf16[1,1,4,512]{3,2,1,0:T(4,128)(2,1)S(1)} %reshape.189), channel_id=1, source_target_pairs={{128,0},{256,128},{384,256},{512,384},{640,512},{768,640},{896,768... | collective-permute-start | bytes 12296 | tf_op jit(solution)/shard_map/ppermute | solution.py:18
  23.8 1.9 collective-permute-start.4
  25.8 0.7 convert_element_type.41
  26.5 0.7 maximum_bitcast_fusion
  27.2 2.4 collective-permute-start.1
  29.6 3.2 collective-permute-start
  32.8 1.0 fusion.3
  33.8 0.7 reshape.357
  34.5 0.7 iota_compare_fusion.8
  35.3 0.7 fusion.216
  35.9 0.7 compare_select_fusion
  36.7 0.7 fusion.151
  37.4 0.7 broadcast_compare_fusion.1
  38.1 1.3 gather_fusion.17
  39.8 1.3 collective-permute-start.7
  41.1 4.0 %collective-permute-start.6 = (bf16[3,1,4,512]{3,2,1,0:T(4,128)(2,1)S(1)}, bf16[3,1,4,512]{3,2,1,0:T(4,128)(2,1)S(1)}, u32[]{:S(2)}, u32[]{:S(2)}) collective-permute-start(bf16[3,1,4,512]{3,2,1,0:T(4,128)(2,1)S(1)} %constant_dynamic-update-slice_fusion), channel_id=1, source_target_pairs={{0,1},{1,2},{2,3},{3,4},{4,5},{5,6},{6,7},{7,8},{8,9},{9,10},{10,1... | collective-permute-start | bytes 36872 | tf_op jit(solution)/shard_map/ppermute | solution.py:15
  46.0 2.3 collective-permute-start.9
  48.3 3.3 collective-permute-start.8
  51.6 0.7 reshape.186
  52.7 1.3 collective-permute-start.11
  54.0 4.7 %collective-permute-start.10 = (bf16[9,3,4,512]{3,2,1,0:T(4,128)(2,1)S(1)}, bf16[9,3,4,512]{3,2,1,0:T(4,128)(2,1)S(1)}, u32[]{:S(2)}, u32[]{:S(2)}) collective-permute-start(bf16[9,3,4,512]{3,2,1,0:T(4,128)(2,1)S(1)} %pad_maximum_fusion.8), channel_id=1, source_target_pairs={{0,1},{1,2},{2,3},{3,4},{4,5},{5,6},{6,7},{7,8},{8,9},{9,10},{10,1... | collective-permute-start | bytes 331784 | tf_op jit(solution)/shard_map/ppermute | solution.py:15
  58.7 1.3 collective-permute-start.3
  60.0 4.0 %collective-permute-start.2 = (f32[3,1,11,4,256]{4,2,3,1,0:T(8,128)S(1)}, f32[3,1,11,4,256]{4,2,3,1,0:T(8,128)S(1)}, u32[]{:S(2)}, u32[]{:S(2)}) collective-permute-start(f32[3,1,11,4,256]{4,2,3,1,0:T(8,128)S(1)} %pad_maximum_fusion.5), channel_id=1, source_target_pairs={{0,1},{1,2},{2,3},{3,4},{4,5},{5,6},{6,7},{7,8},{8,9},{9,10},{10,1... | collective-permute-start | bytes 405512 | tf_op jit(solution)/shard_map/ppermute | solution.py:15
  64.3 1.9 collective-permute-start.13
  66.2 5.1 %collective-permute-start.12 = (bf16[5,5,4,512]{3,2,1,0:T(4,128)(2,1)S(1)}, bf16[5,5,4,512]{3,2,1,0:T(4,128)(2,1)S(1)}, u32[]{:S(2)}, u32[]{:S(2)}) collective-permute-start(bf16[5,5,4,512]{3,2,1,0:T(4,128)(2,1)S(1)} %pad_maximum_fusion.9), channel_id=1, source_target_pairs={{0,128},{128,256},{256,384},{384,512},{512,640},{640,768},{768,896... | collective-permute-start | bytes 307208 | tf_op jit(solution)/shard_map/ppermute | solution.py:15
  72.0 0.6 gather_fusion.13
  73.1 0.6 gather_fusion.11
  74.3 0.6 gather_fusion.9
  79.5 0.6 gather_fusion.15
  80.1 3.7 %broadcast_subtract_fusion = (f32[3,4,256,256]{3,2,1,0:T(8,128)}, f32[3,4,256,256]{3,2,1,0:T(8,128)S(1)}, f32[3,4,256,256]{3,2,1,0:T(8,128)S(1)}, f32[3,4,256,25...) fusion(f32[3,4,256]{2,1,0:T(4,128)S(1)} %copy.51, ...), kind=kLoop, calls=%fused_computation.19 | loop fusion | flops 6291456 | bytes 25276416 | tf_op jit(solution)/shard_map/sub | solution.py:24
  83.8 0.6 fusion.98
  84.4 0.7 convolution_add_fusion.7
  85.1 0.7 convolution_add_fusion.6
  85.8 0.7 convolution_add_fusion.5
  86.4 0.7 convolution_add_fusion.4
  87.1 0.7 convolution_add_fusion.3
  87.7 0.7 convolution_add_fusion.2
  89.2 1.3 collective-permute-start.15
  90.5 4.3 %collective-permute-start.14 = (bf16[15,5,4,512]{3,2,1,0:T(4,128)(2,1)S(1)}, bf16[15,5,4,512]{3,2,1,0:T(4,128)(2,1)S(1)}, u32[]{:S(2)}, u32[]{:S(2)}) collective-permute-start(bf16[15,5,4,512]{3,2,1,0:T(4,128)(2,1)S(1)} %pad_maximum_fusion.3), channel_id=1, source_target_pairs={{0,1},{1,2},{2,3},{3,4},{4,5},{5,6},{6,7},{7,8},{8,9},{9,10},{10,1... | collective-permute-start | bytes 921608 | tf_op jit(solution)/shard_map/ppermute | solution.py:15
  94.8 2.5 convolution_add_fusion.1
  97.3 1.6 collective-permute-done.15
  98.9 1.8 collective-permute-done.14
  101.2 0.7 gather_fusion.16
  102.5 249.0 %all-gather.3.cloned.1.call-done = bf16[1024,1,512]{2,1,0:T(2,128)(2,1)} async-done(((bf16[1,1,512]{2,1,0:T(2,128)(2,1)}), bf16[1024,1,512]{2,1,0:T(2,128)(2,1)}) %all-gather.3.cloned.1.call-update) | async-done | bytes 1048592 | tf_op jit(solution)/shard_map/all_gather | solution.py:96
  351.5 1.9 copy.55
  353.4 0.6 gather_fusion.18
  354.6 0.8 fusion
  (76 shorter events, 10.2 us)
Async XLA Ops:
  6.5 95.5 %copy-start = (bf16[4,16,64,64]{3,2,1,0:T(8,128)(2,1)S(1)}, bf16[4,16,64,64]{3,2,1,0:T(8,128)(2,1)}, u32[]{:S(2)}) copy-start(bf16[4,16,64,64]{3,2,1,0:T(8,128)(2,1)} %param.17) | copy-start | bytes 1572868
  6.5 345.0 %all-gather.3.cloned.1.call-start = ((), (), s32[]{:S(2)}) async-start(), calls=%async_computation | async-start | bytes 2099200 | tf_op jit(solution)/shard_map/all_gather | solution.py:96
  7.8 32.0 %collective-permute-start.5 = (bf16[1,1,4,512]{3,2,1,0:T(4,128)(2,1)S(1)}, bf16[1,1,4,512]{3,2,1,0:T(4,128)(2,1)S(1)}, u32[]{:S(2)}, u32[]{:S(2)}) collective-permute-start(bf16[1,1,4,512]{3,2,1,0:T(4,128)(2,1)S(1)} %reshape.189), channel_id=1, source_target_pairs={{128,0},{256,128},{384,256},{512,384},{640,512},{768,640},{896,768... | collective-permute-start | bytes 12296 | tf_op jit(solution)/shard_map/ppermute | solution.py:18
  23.8 15.9 %collective-permute-start.4 = (bf16[1,1,4,512]{3,2,1,0:T(4,128)(2,1)S(1)}, bf16[1,1,4,512]{3,2,1,0:T(4,128)(2,1)S(1)}, u32[]{:S(2)}, u32[]{:S(2)}) collective-permute-start(bf16[1,1,4,512]{3,2,1,0:T(4,128)(2,1)S(1)} %reshape.189), channel_id=1, source_target_pairs={{0,128},{128,256},{256,384},{384,512},{512,640},{640,768},{768,896... | collective-permute-start | bytes 12296 | tf_op jit(solution)/shard_map/ppermute | solution.py:15
  27.2 31.4 %collective-permute-start.1 = (f32[1,1,11,4,256]{4,2,3,1,0:T(8,128)S(1)}, f32[1,1,11,4,256]{4,2,3,1,0:T(8,128)S(1)}, u32[]{:S(2)}, u32[]{:S(2)}) collective-permute-start(f32[1,1,11,4,256]{4,2,3,1,0:T(8,128)S(1)} %maximum_bitcast_fusion), channel_id=1, source_target_pairs={{128,0},{256,128},{384,256},{512,384},{640,512},{768,640},{896,768... | collective-permute-start | bytes 135176 | tf_op jit(solution)/shard_map/ppermute | solution.py:18
  29.6 29.0 %collective-permute-start = (f32[1,1,11,4,256]{4,2,3,1,0:T(8,128)S(1)}, f32[1,1,11,4,256]{4,2,3,1,0:T(8,128)S(1)}, u32[]{:S(2)}, u32[]{:S(2)}) collective-permute-start(f32[1,1,11,4,256]{4,2,3,1,0:T(8,128)S(1)} %maximum_bitcast_fusion), channel_id=1, source_target_pairs={{0,128},{128,256},{256,384},{384,512},{512,640},{640,768},{768,896... | collective-permute-start | bytes 135176 | tf_op jit(solution)/shard_map/ppermute | solution.py:15
  39.8 6.0 %collective-permute-start.7 = (bf16[3,1,4,512]{3,2,1,0:T(4,128)(2,1)S(1)}, bf16[3,1,4,512]{3,2,1,0:T(4,128)(2,1)S(1)}, u32[]{:S(2)}, u32[]{:S(2)}) collective-permute-start(bf16[3,1,4,512]{3,2,1,0:T(4,128)(2,1)S(1)} %constant_dynamic-update-slice_fusion), channel_id=1, source_target_pairs={{1,0},{2,1},{3,2},{4,3},{5,4},{6,5},{7,6},{8,7},{9,8},{10,9},{11,1... | collective-permute-start | bytes 36872 | tf_op jit(solution)/shard_map/ppermute | solution.py:18
  41.1 4.8 %collective-permute-start.6 = (bf16[3,1,4,512]{3,2,1,0:T(4,128)(2,1)S(1)}, bf16[3,1,4,512]{3,2,1,0:T(4,128)(2,1)S(1)}, u32[]{:S(2)}, u32[]{:S(2)}) collective-permute-start(bf16[3,1,4,512]{3,2,1,0:T(4,128)(2,1)S(1)} %constant_dynamic-update-slice_fusion), channel_id=1, source_target_pairs={{0,1},{1,2},{2,3},{3,4},{4,5},{5,6},{6,7},{7,8},{8,9},{9,10},{10,1... | collective-permute-start | bytes 36872 | tf_op jit(solution)/shard_map/ppermute | solution.py:15
  46.0 6.3 %collective-permute-start.9 = (bf16[3,3,4,512]{3,2,1,0:T(4,128)(2,1)S(1)}, bf16[3,3,4,512]{3,2,1,0:T(4,128)(2,1)S(1)}, u32[]{:S(2)}, u32[]{:S(2)}) collective-permute-start(bf16[3,3,4,512]{3,2,1,0:T(4,128)(2,1)S(1)} %pad_maximum_fusion.10), channel_id=1, source_target_pairs={{128,0},{256,128},{384,256},{512,384},{640,512},{768,640},{896,768... | collective-permute-start | bytes 110600 | tf_op jit(solution)/shard_map/ppermute | solution.py:18
  48.3 4.3 %collective-permute-start.8 = (bf16[3,3,4,512]{3,2,1,0:T(4,128)(2,1)S(1)}, bf16[3,3,4,512]{3,2,1,0:T(4,128)(2,1)S(1)}, u32[]{:S(2)}, u32[]{:S(2)}) collective-permute-start(bf16[3,3,4,512]{3,2,1,0:T(4,128)(2,1)S(1)} %pad_maximum_fusion.10), channel_id=1, source_target_pairs={{0,128},{128,256},{256,384},{384,512},{512,640},{640,768},{768,896... | collective-permute-start | bytes 110600 | tf_op jit(solution)/shard_map/ppermute | solution.py:15
  52.7 11.3 %collective-permute-start.11 = (bf16[9,3,4,512]{3,2,1,0:T(4,128)(2,1)S(1)}, bf16[9,3,4,512]{3,2,1,0:T(4,128)(2,1)S(1)}, u32[]{:S(2)}, u32[]{:S(2)}) collective-permute-start(bf16[9,3,4,512]{3,2,1,0:T(4,128)(2,1)S(1)} %pad_maximum_fusion.8), channel_id=1, source_target_pairs={{1,0},{2,1},{3,2},{4,3},{5,4},{6,5},{7,6},{8,7},{9,8},{10,9},{11,1... | collective-permute-start | bytes 331784 | tf_op jit(solution)/shard_map/ppermute | solution.py:18
  54.0 10.0 %collective-permute-start.10 = (bf16[9,3,4,512]{3,2,1,0:T(4,128)(2,1)S(1)}, bf16[9,3,4,512]{3,2,1,0:T(4,128)(2,1)S(1)}, u32[]{:S(2)}, u32[]{:S(2)}) collective-permute-start(bf16[9,3,4,512]{3,2,1,0:T(4,128)(2,1)S(1)} %pad_maximum_fusion.8), channel_id=1, source_target_pairs={{0,1},{1,2},{2,3},{3,4},{4,5},{5,6},{6,7},{7,8},{8,9},{9,10},{10,1... | collective-permute-start | bytes 331784 | tf_op jit(solution)/shard_map/ppermute | solution.py:15
  58.7 12.6 %collective-permute-start.3 = (f32[3,1,11,4,256]{4,2,3,1,0:T(8,128)S(1)}, f32[3,1,11,4,256]{4,2,3,1,0:T(8,128)S(1)}, u32[]{:S(2)}, u32[]{:S(2)}) collective-permute-start(f32[3,1,11,4,256]{4,2,3,1,0:T(8,128)S(1)} %pad_maximum_fusion.5), channel_id=1, source_target_pairs={{1,0},{2,1},{3,2},{4,3},{5,4},{6,5},{7,6},{8,7},{9,8},{10,9},{11,1... | collective-permute-start | bytes 405512 | tf_op jit(solution)/shard_map/ppermute | solution.py:18
  60.0 11.3 %collective-permute-start.2 = (f32[3,1,11,4,256]{4,2,3,1,0:T(8,128)S(1)}, f32[3,1,11,4,256]{4,2,3,1,0:T(8,128)S(1)}, u32[]{:S(2)}, u32[]{:S(2)}) collective-permute-start(f32[3,1,11,4,256]{4,2,3,1,0:T(8,128)S(1)} %pad_maximum_fusion.5), channel_id=1, source_target_pairs={{0,1},{1,2},{2,3},{3,4},{4,5},{5,6},{6,7},{7,8},{8,9},{9,10},{10,1... | collective-permute-start | bytes 405512 | tf_op jit(solution)/shard_map/ppermute | solution.py:15
  64.3 24.7 %collective-permute-start.13 = (bf16[5,5,4,512]{3,2,1,0:T(4,128)(2,1)S(1)}, bf16[5,5,4,512]{3,2,1,0:T(4,128)(2,1)S(1)}, u32[]{:S(2)}, u32[]{:S(2)}) collective-permute-start(bf16[5,5,4,512]{3,2,1,0:T(4,128)(2,1)S(1)} %pad_maximum_fusion.9), channel_id=1, source_target_pairs={{128,0},{256,128},{384,256},{512,384},{640,512},{768,640},{896,768... | collective-permute-start | bytes 307208 | tf_op jit(solution)/shard_map/ppermute | solution.py:18
  66.2 22.8 %collective-permute-start.12 = (bf16[5,5,4,512]{3,2,1,0:T(4,128)(2,1)S(1)}, bf16[5,5,4,512]{3,2,1,0:T(4,128)(2,1)S(1)}, u32[]{:S(2)}, u32[]{:S(2)}) collective-permute-start(bf16[5,5,4,512]{3,2,1,0:T(4,128)(2,1)S(1)} %pad_maximum_fusion.9), channel_id=1, source_target_pairs={{0,128},{128,256},{256,384},{384,512},{512,640},{640,768},{768,896... | collective-permute-start | bytes 307208 | tf_op jit(solution)/shard_map/ppermute | solution.py:15
  89.2 9.7 %collective-permute-start.15 = (bf16[15,5,4,512]{3,2,1,0:T(4,128)(2,1)S(1)}, bf16[15,5,4,512]{3,2,1,0:T(4,128)(2,1)S(1)}, u32[]{:S(2)}, u32[]{:S(2)}) collective-permute-start(bf16[15,5,4,512]{3,2,1,0:T(4,128)(2,1)S(1)} %pad_maximum_fusion.3), channel_id=1, source_target_pairs={{1,0},{2,1},{3,2},{4,3},{5,4},{6,5},{7,6},{8,7},{9,8},{10,9},{11,1... | collective-permute-start | bytes 921608 | tf_op jit(solution)/shard_map/ppermute | solution.py:18
  90.5 10.1 %collective-permute-start.14 = (bf16[15,5,4,512]{3,2,1,0:T(4,128)(2,1)S(1)}, bf16[15,5,4,512]{3,2,1,0:T(4,128)(2,1)S(1)}, u32[]{:S(2)}, u32[]{:S(2)}) collective-permute-start(bf16[15,5,4,512]{3,2,1,0:T(4,128)(2,1)S(1)} %pad_maximum_fusion.3), channel_id=1, source_target_pairs={{0,1},{1,2},{2,3},{3,4},{4,5},{5,6},{6,7},{7,8},{8,9},{9,10},{10,1... | collective-permute-start | bytes 921608 | tf_op jit(solution)/shard_map/ppermute | solution.py:15
  100.9 253.2 %copy-start.2 = (bf16[1,16,64,64]{3,2,1,0:T(8,128)(2,1)S(1)}, bf16[1,16,64,64]{3,2,1,0:T(8,128)(2,1)}, u32[]{:S(2)}) copy-start(bf16[1,16,64,64]{3,2,1,0:T(8,128)(2,1)} %param.20) | copy-start | bytes 393220
  101.1 253.2 %copy-start.3 = (bf16[4,64,64]{2,1,0:T(8,128)(2,1)S(1)}, bf16[4,64,64]{2,1,0:T(8,128)(2,1)}, u32[]{:S(2)}) copy-start(bf16[4,64,64]{2,1,0:T(8,128)(2,1)} %param.16) | copy-start | bytes 98308
  101.2 253.4 %copy-start.1 = (bf16[4,256,64]{1,2,0:T(8,128)(2,1)S(1)}, bf16[4,256,64]{1,2,0:T(8,128)(2,1)}, u32[]{:S(2)}) copy-start(bf16[4,256,64]{1,2,0:T(8,128)(2,1)} %param.15) | copy-start | bytes 393220
Sparse Core Ops, SparseCore 0:
  34.6 316.8 all-gather.2
where the time goes:
time: 363 us; the launch traced here: 362 us
  waiting for transfers between devices  253 us (70%)
  starting transfers between devices  58.2 us (16%)
  local copies, waits for them, and re-layouts  15.7 us (4%)
  between operations  14.6 us (4%)
  matrix products  10.9 us (3%)
  other arithmetic  10 us (3%)
    all_gather x1, waiting for transfers between devices, per_device(): all_clusters = lax.all_gather(cluster, ('row', 'col'), axis=0, tiled=True)  249 us
    ppermute x8, starting transfers between devices, with_halo(): lax.ppermute(lax.slice_in_dim(block, block.shape[dim] - width, None, axis...  30.3 us
    ppermute x8, starting transfers between devices, with_halo(): lax.ppermute(lax.slice_in_dim(block, 0, width, axis=dim), axis, backward)  27.9 us
  transfers between devices with their start and end apart: 17, of which 5 were waited for; matrix products, arithmetic and copies ran while one was open for 9% of the time, Pallas kernels for 0%

commit v1 on v0

v1 whole, which is shorter than its diff:
```python
import functools

import jax
import jax.numpy as jnp
from jax import lax
from jax.experimental import pallas as pl
from jax.experimental.pallas import tpu as pltpu
from jax.sharding import Mesh, PartitionSpec as P

FOUR_PI = 12.566370614359172
SOFTEN = 0.0025
F32 = jnp.float32
BF16 = jnp.bfloat16
NT = (((1,), (1,)), ((), ()))

BLOCK = 10
SHARE = BLOCK + 2 * BLOCK + 4


def pack_kernel(rhs_ref, points_ref, basis_ref, transfer_ref, block_ref, cluster_ref):
    points = points_ref[...]
    part_hi = points.astype(BF16).astype(F32)
    rest = points - part_hi
    part_mid = rest.astype(BF16).astype(F32)
    part_lo = rest - part_mid
    parts = jnp.concatenate([part_hi, part_mid, part_lo[:2]], axis=0)
    cluster = jnp.zeros((8, 64), F32)
    coeffs = []
    last_rows = []
    for leaf in range(4):
        low = slice(leaf * 256, leaf * 256 + 128)
        high = slice(leaf * 256 + 128, leaf * 256 + 256)
        sides = rhs_ref[:, leaf * 256 : leaf * 256 + 256]
        coeff = jnp.dot(sides, basis_ref[leaf], preferred_element_type=F32).astype(BF16)
        cluster = cluster + jnp.dot(coeff, transfer_ref[leaf], preferred_element_type=F32)
        coeffs.append(coeff.astype(F32))
        wide = sides.astype(F32)
        block_ref[leaf] = jnp.concatenate([wide[:, :128], wide[:, 128:]], axis=0).astype(BF16)
        block_ref[4 + leaf] = jnp.concatenate([parts[:, low], parts[:, high]], axis=0).astype(BF16)
        last_rows += [part_lo[2:3, low], part_lo[2:3, high]]
    block_ref[8] = jnp.concatenate(last_rows + [jnp.zeros((8, 128), F32)], axis=0).astype(BF16)
    block_ref[9] = jnp.concatenate(
        [jnp.concatenate(coeffs[:2], axis=1), jnp.concatenate(coeffs[2:], axis=1)], axis=0
    ).astype(BF16)
    packed = jnp.concatenate([cluster[:4], cluster[4:]], axis=1).astype(BF16)
    cluster_ref[...] = jnp.broadcast_to(packed[None], cluster_ref.shape)


def locate(leaf_id, cols, my_col):
    device = lax.shift_right_logical(leaf_id, 2)
    row = device // cols
    gap = device - row * cols - my_col
    side = (row - lax.rem(row, 2) + jnp.where(gap < 0, 1, 0)) * SHARE
    return row, gap, side, lax.rem(leaf_id, 4)


def near_kernel(cols, pos_ref, list_ref, count_ref, points_ref, share_ref, near_ref, wide_ref):
    my_col = pos_ref[1]
    scale = F32(FOUR_PI * FOUR_PI)
    floor = F32(FOUR_PI * FOUR_PI * SOFTEN)
    row_ids = lax.broadcasted_iota(jnp.int32, (8, 128), 0)
    for leaf in range(4):
        own = points_ref[:, leaf * 256 : leaf * 256 + 256]
        own = jnp.concatenate([own, jnp.zeros((5, 256), F32)], axis=0).T
        for axis in range(3):
            wide_ref[axis] = jnp.broadcast_to(own[:, axis : axis + 1], (256, 128))

        def slot_step(slot, total):
            row, gap, side, source = locate(list_ref[leaf, slot], cols, my_col)
            base = jnp.where(gap == 0, row * SHARE, side + BLOCK + lax.rem(row, 2) * BLOCK)
            sides = share_ref[base + source].astype(F32)
            parts = share_ref[base + 4 + source].astype(F32)
            last = share_ref[base + 8].astype(F32)[:8]
            tiles = []
            for half in range(2):
                part = parts[half * 8 : half * 8 + 8]
                tail = jnp.sum(
                    jnp.where(row_ids == source * 2 + half, last, 0.0), axis=0, keepdims=True
                )
                first = wide_ref[0] - (part[0:1] + part[3:4] + part[6:7])
                second = wide_ref[1] - (part[1:2] + part[4:5] + part[7:8])
                third = wide_ref[2] - (part[2:3] + part[5:6] + tail)
                dist_sq = first * first + second * second + third * third
                tiles.append(lax.rsqrt(dist_sq * scale + floor).astype(BF16))
            tile = jnp.concatenate(tiles, axis=1)
            sides = jnp.concatenate([sides[:8], sides[8:]], axis=1).astype(BF16)
            return total + lax.dot_general(tile, sides, NT, preferred_element_type=F32)

        total = lax.fori_loop(0, count_ref[leaf], slot_step, jnp.zeros((256, 8), F32))
        near_ref[:, leaf * 256 : leaf * 256 + 256] = total.T


def couple(matrices, sources):
    slots = matrices.shape[0]
    products = lax.dot_general(
        matrices.reshape(slots * 64, 64), sources.astype(BF16), NT, preferred_element_type=F32
    )
    group = lax.broadcasted_iota(jnp.int32, (64, 128), 1) // 8
    total = jnp.zeros((64, 128), F32)
    for slot in range(slots):
        total = jnp.where(group == slot, products[slot * 64 : slot * 64 + 64], total)
    for shift in (64, 32, 16, 8):
        total = total + pltpu.roll(total, shift, 1)
    return total


def far_kernel(
    cols,
    ys,
    zs,
    pos_ref,
    coupling_list_ref,
    coupling_count_ref,
    coarse_list_ref,
    coarse_count_ref,
    owner_ref,
    share_ref,
    same_ref,
    other_ref,
    leaf_coupling_ref,
    coarse_coupling_ref,
    transfer_ref,
    basis_ref,
    near_ref,
    out_ref,
    source_ref,
):
    my_row = pos_ref[0]
    my_col = pos_ref[1]
    for slot in range(16):
        device = owner_ref[coarse_list_ref[0, slot]]
        row = device // cols
        col = device - row * cols
        tile_id = (row // 2) * (ys * zs // 4) + col // 4
        mine = lax.rem(row, 2) == lax.rem(my_row, 2)
        tile = jnp.where(mine, same_ref[tile_id], other_ref[tile_id]).astype(F32)
        place = lax.rem(col, 4)
        picked = tile[0:4]
        for step in range(1, 4):
            picked = jnp.where(place == step, tile[step * 4 : step * 4 + 4], picked)
        picked = jnp.where(slot < coarse_count_ref[0], picked, 0.0)
        source_ref[slot * 8 : slot * 8 + 8, :] = jnp.concatenate(
            [picked[:, :64], picked[:, 64:]], axis=0
        )
    coarse_field = couple(coarse_coupling_ref[0], source_ref[...])
    for leaf in range(4):
        for slot in range(16):
            row, gap, side, source = locate(coupling_list_ref[leaf, slot], cols, my_col)
            odd = lax.rem(row, 2)
            far = jnp.abs(gap)
            tile_id = jnp.where(
                far == 0,
                row * SHARE + 9,
                side + jnp.where(far == 1, 19 + odd * BLOCK, 28 + odd * 2 + far),
            )
            tile = share_ref[tile_id].astype(F32)
            half = jnp.where(source >= 2, tile[8:], tile[:8])
            half = jnp.where(lax.rem(source, 2) == 1, half[:, 64:], half[:, :64])
            live = slot < coupling_count_ref[leaf]
            source_ref[slot * 8 : slot * 8 + 8, :] = jnp.where(live, half, 0.0)
        local = couple(leaf_coupling_ref[leaf], source_ref[...])
        local = local + jnp.dot(
            transfer_ref[leaf].astype(F32),
            coarse_field,
            precision=lax.Precision.HIGHEST,
            preferred_element_type=F32,
        )
        local = local.T[:8].astype(BF16)
        far_part = lax.dot_general(local, basis_ref[leaf], NT, preferred_element_type=F32)
        span = slice(leaf * 256, leaf * 256 + 256)
        out_ref[:, span] = (near_ref[:, span] + far_part).astype(BF16)


def per_device(
    xs,
    ys,
    zs,
    rhs,
    points,
    basis,
    transfer,
    leaf_coupling,
    coupling_list,
    coupling_count,
    coarse_coupling,
    coarse_list,
    coarse_count,
    owner,
    near_list,
    near_count,
):
    cols = ys * zs
    vmem = pl.BlockSpec(memory_space=pltpu.VMEM)
    smem = pl.BlockSpec(memory_space=pltpu.SMEM)
    row_axes = ("x", "core")
    my_row = lax.axis_index(row_axes)
    my_col = lax.axis_index(("y", "z"))
    pos = jnp.stack([my_row, my_col]).astype(jnp.int32)

    block, cluster = pl.pallas_call(
        pack_kernel,
        out_shape=(
            jax.ShapeDtypeStruct((BLOCK, 16, 128), BF16),
            jax.ShapeDtypeStruct((zs, 4, 128), BF16),
        ),
        in_specs=[vmem] * 4,
        out_specs=(vmem, vmem),
        name="pack",
    )(rhs, points, basis, transfer)

    def beside(step):
        pairs = []
        for core in range(2):
            for col in range(cols):
                source = col + step if core == 0 else col - step
                if 0 <= source < cols:
                    pairs.append((core * cols + source, core * cols + col))
        return pairs

    chip = lax.all_gather(block, "core", axis=0, tiled=False)
    first = lax.ppermute(chip, ("core", "y", "z"), beside(1))
    coeffs = jnp.concatenate([chip[:, 9:], first[:, 9:]], axis=1)
    second = lax.ppermute(coeffs, ("core", "y", "z"), beside(2))
    share = jnp.concatenate(
        [block, first.reshape(2 * BLOCK, 16, 128), second.reshape(4, 16, 128)], axis=0
    )
    share, cluster = lax.optimization_barrier((share, cluster))
    shares = lax.all_gather(share, row_axes, axis=0, tiled=True)

    line = lax.all_to_all(cluster, "z", 0, 0, tiled=True).reshape(zs // 4, 16, 128)
    line = jnp.broadcast_to(line[None], (xs * ys,) + line.shape)
    same = lax.all_to_all(line, ("x", "y"), 0, 0, tiled=True).reshape(xs * cols // 4, 16, 128)
    other = lax.ppermute(same, "core", [(0, 1), (1, 0)])

    near = pl.pallas_call(
        functools.partial(near_kernel, cols),
        out_shape=jax.ShapeDtypeStruct((8, 1024), F32),
        in_specs=[smem] * 3 + [vmem] * 2,
        out_specs=vmem,
        scratch_shapes=[pltpu.VMEM((3, 256, 128), F32)],
        name="near",
        cost_estimate=pl.CostEstimate(flops=20_000_000, bytes_accessed=1_200_000, transcendentals=0),
    )(pos, near_list, near_count, points, shares)

    return pl.pallas_call(
        functools.partial(far_kernel, cols, ys, zs),
        out_shape=jax.ShapeDtypeStruct((8, 1024), BF16),
        in_specs=[smem] * 6 + [vmem] * 8,
        out_specs=vmem,
        scratch_shapes=[pltpu.VMEM((128, 64), F32)],
        name="far",
    )(
        pos,
        coupling_list,
        coupling_count,
        coarse_list,
        coarse_count,
        owner,
        shares,
        same,
        other,
        leaf_coupling,
        coarse_coupling,
        transfer,
        basis,
        near,
    )


def solution(mesh):
    rows, cols = mesh.devices.shape
    xs, ys = rows // 2, 4
    zs = cols // ys
    axes = ("x", "core", "y", "z")
    fine = Mesh(mesh.devices.reshape(xs, 2, ys, zs), axes)
    in_specs = (
        P(None, axes),
        P(None, axes),
        P(axes, None, None),
        P(axes, None, None),
        P(axes, None, None, None),
        P(axes, None),
        P(axes),
        P(axes, None, None, None),
        P(axes, None),
        P(axes),
        P(),
        P(axes, None),
        P(axes),
    )
    return jax.shard_map(
        functools.partial(per_device, xs, ys, zs),
        mesh=fine,
        in_specs=in_specs,
        out_specs=P(None, axes),
        check_vma=False,
    )
```

time: 363 us -> 123 us (0.34)
  waiting for transfers between devices: 253 us -> 2.33 us
  blocking collectives: 0 us -> 77.3 us
  starting transfers between devices: 58.2 us -> 8.63 us
  Pallas kernels: 0 us -> 15.7 us
  local copies, waits for them, and re-layouts: 15.7 us -> 2.63 us
  matrix products: 10.9 us -> 0 us
  other arithmetic: 10 us -> 2.11 us
    all_gather x1, waiting for transfers between devices: 249 us -> 0.01 us  [per_device(): shares = lax.all_gather(share, row_axes, axis=0, tiled=True)]
    all_to_all x0 -> x2, blocking collectives: none -> 61.4 us  [the longest x1 45.9 us: per_device(): lax.all_to_all(cluster, 'z', 0, 0, tiled=True).reshape(zs // 4, 16, 128)]
    ppermute x16 -> x3, starting transfers between devices: 58.2 us -> 8.63 us  [the longest x1 6.07 us: per_device(): other = lax.ppermute(same, 'core', [(0, 1), (1, 0)])]
    all_gather x0 -> x1, blocking collectives: none -> 15.9 us  [per_device(): chip = lax.all_gather(block, 'core', axis=0, tiled=False)]
    pallas_call x0 -> x3, Pallas kernels: none -> 15.7 us  [the longest x1 8.02 us: per_device(): pl.pallas_call(functools.partial(near_kernel, cols), out_shape=jax.ShapeD...]
    gather x19 -> x0, local copies, waits for them, and re-layouts: 11.7 us -> none  [the longest x8 4.64 us: per_device(): source_points = jnp.moveaxis(wide_points[block_ids, :, leaf_ids], 1, 0)]
    dot_general x14 -> x0, matrix products: 10.9 us -> none  [the longest x8 7.09 us: per_device(): jnp.einsum('lpq,lrq->rlp', tile_vals, source_rhs, preferred_element_type=...]
    sub x1 -> x0, other arithmetic: 3.72 us -> none  [kernel_tile(): gap = target_points[:, :, :, None] - source_points[:, :, None, :]]
  transfers between devices with their start and end apart: 17 -> 4, of which waited for: 5 -> 2; matrix products, arithmetic and copies ran while one was open for 9% -> 1% of each run, Pallas kernels for 0% -> 7%
where the time goes in v1:
time: 123 us
  blocking collectives  77.3 us (63%)
  Pallas kernels  15.7 us (13%)
  between operations  14.1 us (11%)
  starting transfers between devices  8.63 us (7%)
  local copies, waits for them, and re-layouts  2.63 us (2%)
  waiting for transfers between devices  2.33 us (2%)
  other arithmetic  2.11 us (2%)
    all_to_all x1, blocking collectives, per_device(): lax.all_to_all(cluster, 'z', 0, 0, tiled=True).reshape(zs // 4, 16, 128)  45.9 us
    all_gather x1, blocking collectives, per_device(): chip = lax.all_gather(block, 'core', axis=0, tiled=False)  15.9 us
    all_to_all x1, blocking collectives, per_device(): lax.all_to_all(line, ('x', 'y'), 0, 0, tiled=True)  15.5 us
    pallas_call x1, Pallas kernels, per_device(): pl.pallas_call(functools.partial(near_kernel, cols), out_shape=jax.ShapeD...  8.02 us
    ppermute x1, starting transfers between devices, per_device(): other = lax.ppermute(same, 'core', [(0, 1), (1, 0)])  6.07 us
    pallas_call x1, Pallas kernels, per_device(): pl.pallas_call(functools.partial(far_kernel, cols, ys, zs), out_shape=jax...  5.74 us
    unnamed x5, local copies, waits for them, and re-layouts  2.54 us
  transfers between devices with their start and end apart: 4, of which 2 were waited for; matrix products, arithmetic and copies ran while one was open for 1% of the time, Pallas kernels for 7%

profile of v1, /device:TPU:1, one launch (start us, length us, event | category | flops | bytes accessed | tf_op | source)
XLA Modules:
  0.0 122.8 jit_solution(836888762948132010)
XLA Ops:
  6.5 0.0 all-gather.3.cloned.1.call-start
  6.5 1.7 %copy.16.basis_ref = bf16[4,256,64]{2,1,0:T(8,128)(2,1)} copy(bf16[4,256,64]{1,2,0:T(8,128)(2,1)} %param.15) | data formatting | bytes 262144 | tf_op args[2]
  8.3 2.0 %pack.1 = (bf16[10,16,128]{2,1,0:T(8,128)(2,1)}, bf16[32,4,128]{2,1,0:T(4,128)(2,1)}) custom-call(bf16[8,1024]{1,0:T(8,128)(2,1)} %rhs_ref.1, f32[3,1024]{1,0:T(4,128)} %points_ref.3, bf16[4,256,64]{2,1,0:T(8,128)(2,1)} %copy.16.basis_ref, bf16[4,64,64]{2,1,0:T(8,128)(2,1)} %transfer_ref.3), custom_call_target="tpu_custom_call" | custom-call | tf_op jit(solution)/shard_map/pack/pallas_call | solution.py:200
  10.2 15.9 %all-gather = bf16[20,16,128]{2,1,0:T(8,128)(2,1)S(1)} all-gather(bf16[10,16,128]{2,1,0:T(8,128)(2,1)} %get-tuple-element.9), channel_id=2, replica_groups=mesh['x'=4,'core'=2,'y'=4,'z'=32] {'core'}, dimensions={0}, use_global_device_ids=true | all-gather | bytes 122880 | tf_op jit(solution)/shard_map/all_gather | solution.py:220
  26.1 1.3 %collective-permute-start = (bf16[2,10,16,128]{3,2,1,0:T(8,128)(2,1)S(1)}, bf16[2,10,16,128]{3,2,1,0:T(8,128)(2,1)S(1)}, u32[]{:S(2)}, u32[]{:S(2)}) collective-permute-start(bf16[2,10,16,128]{3,2,1,0:T(8,128)(2,1)S(1)} %bitcast.10), channel_id=1, source_target_pairs={{1,0},{2,1},{3,2},{4,3},{5,4},{6,5},{7,6},{8,7},{9,8},{10,9},{11,1... | collective-permute-start | bytes 245768 | tf_op jit(solution)/shard_map/ppermute | solution.py:221
  27.4 1.5 %collective-permute-done = bf16[2,10,16,128]{3,2,1,0:T(8,128)(2,1)S(1)} collective-permute-done((bf16[2,10,16,128]{3,2,1,0:T(8,128)(2,1)S(1)}, bf16[2,10,16,128]{3,2,1,0:T(8,128)(2,1)S(1)}, u32[]{:S(2)}, u32[]{:S(2)}) %collective-permute-start) | collective-permute-done | bytes 81952 | tf_op jit(solution)/shard_map/ppermute | solution.py:221
  28.9 1.3 %collective-permute-start.1 = (bf16[2,2,16,128]{3,2,1,0:T(8,128)(2,1)S(1)}, bf16[2,2,16,128]{3,2,1,0:T(8,128)(2,1)S(1)}, u32[]{:S(2)}, u32[]{:S(2)}) collective-permute-start(bf16[2,2,16,128]{3,2,1,0:T(8,128)(2,1)S(1)} %pad_maximum_fusion.1), channel_id=1, source_target_pairs={{2,0},{3,1},{4,2},{5,3},{6,4},{7,5},{8,6},{9,7},{10,8},{11,9},{12,... | collective-permute-start | bytes 49160 | tf_op jit(solution)/shard_map/ppermute | solution.py:223
  30.1 0.9 collective-permute-done.1
  31.0 1.4 %pad_maximum_fusion = bf16[34,16,128]{2,1,0:T(8,128)(2,1)} fusion(bf16[4,16,128]{2,1,0:T(8,128)(2,1)S(1)} %bitcast.13, bf16[20,16,128]{2,1,0:T(8,128)(2,1)S(1)} %bitcast.12, bf16[10,16,128]{2,1,0:T(8,128)(2,1)} %get-tuple-element.9), kind=kLoop, calls=%fused_computation | loop fusion | flops 139264 | bytes 278528 | tf_op jit(solution)/shard_map/concatenate | solution.py:224
  32.4 0.0 all-gather.3.cloned.1.call-update
  32.5 45.9 %all_to_all.10 = bf16[32,4,128]{2,1,0:T(4,128)(2,1)S(1)} all-to-all(bf16[32,4,128]{2,1,0:T(4,128)(2,1)} %get-tuple-element.12), channel_id=1, replica_groups=mesh['x'=4,'core'=2,'y'=4,'z'=32] {'z'}, dimensions={0} | all-to-all | bytes 65536 | tf_op jit(solution)/shard_map/all_to_all | solution.py:230
  78.3 0.1 broadcast_in_dim.8
  78.5 15.5 %all_to_all.11 = bf16[16,8,16,128]{3,2,1,0:T(8,128)(2,1)S(1)} all-to-all(bf16[16,8,16,128]{3,2,1,0:T(8,128)(2,1)S(1)} %broadcast_in_dim.8), channel_id=1, replica_groups=mesh['x'=4,'core'=2,'y'=4,'z'=32] {'x','y'}, dimensions={0} | all-to-all | bytes 1048576 | tf_op jit(solution)/shard_map/all_to_all | solution.py:232
  94.0 0.0 copy-start
  94.0 6.1 %collective-permute-start.2 = (bf16[128,16,128]{2,1,0:T(8,128)(2,1)S(1)}, bf16[128,16,128]{2,1,0:T(8,128)(2,1)S(1)}, u32[]{:S(2)}, u32[]{:S(2)}) collective-permute-start(bf16[128,16,128]{2,1,0:T(8,128)(2,1)S(1)} %bitcast.7), channel_id=1, source_target_pairs={{0,128},{128,0},{1,129},{129,1},{2,130},{130,2},{3,131},{131,3},{4... | collective-permute-start | bytes 1572872 | tf_op jit(solution)/shard_map/ppermute | solution.py:233
  100.7 0.7 pad_add_fusion.pos_ref
  101.3 0.0 all-gather.3.cloned.1.call-done.share_ref
  101.4 8.0 %near.1.near_ref = f32[8,1024]{1,0:T(8,128)} custom-call(s32[2]{0:T(128)} %pad_add_fusion.pos_ref, s32[4,8]{1,0:T(4,128)} %list_ref.1, s32[4]{0:T(128)} %count_ref.1, f32[3,1024]{1,0:T(4,128)} %points_ref.3, bf16[272,16,128]{2,1,0:T(8,128)(2,1)} %all-gather.3.cloned.1.call-done.share_ref), custom_call_target="tpu_custom_call" | custom-call | flops 20000000 | bytes 1200000 | tf_op jit(solution)/shard_map/near/pallas_call | solution.py:235
  109.4 0.0 collective-permute-done.2.other_ref
  109.4 0.0 copy-done
  109.4 0.0 copy-start.1
  109.4 0.8 copy-done.1
  110.2 5.7 %far.1 = bf16[8,1024]{1,0:T(8,128)(2,1)} custom-call(s32[2]{0:T(128)} %pad_add_fusion.pos_ref, s32[4,16]{1,0:T(4,128)} %coupling_list_ref.1, s32[4]{0:T(128)} %coupling_count_ref.1, s32[1,16]{1,0:T(1,128)} %coarse_list_ref.1, s32[1]{0:T(128)S(6)} %copy.18.coarse_count_ref, s32[1024]{0:T(1024)} %owner_ref.1, ...), custom_call_target="tpu_custom_call" | custom-call | tf_op jit(solution)/shard_map/far/pallas_call | solution.py:245
  (3 shorter events, 0.0 us)
Async XLA Ops:
  6.5 94.8 %all-gather.3.cloned.1.call-start = ((), (), s32[]{:S(2)}) async-start(), calls=%async_computation.2 | async-start | bytes 1253376 | tf_op jit(solution)/shard_map/all_gather | solution.py:228
  26.1 2.8 %collective-permute-start = (bf16[2,10,16,128]{3,2,1,0:T(8,128)(2,1)S(1)}, bf16[2,10,16,128]{3,2,1,0:T(8,128)(2,1)S(1)}, u32[]{:S(2)}, u32[]{:S(2)}) collective-permute-start(bf16[2,10,16,128]{3,2,1,0:T(8,128)(2,1)S(1)} %bitcast.10), channel_id=1, source_target_pairs={{1,0},{2,1},{3,2},{4,3},{5,4},{6,5},{7,6},{8,7},{9,8},{10,9},{11,1... | collective-permute-start | bytes 245768 | tf_op jit(solution)/shard_map/ppermute | solution.py:221
  28.9 2.1 %collective-permute-start.1 = (bf16[2,2,16,128]{3,2,1,0:T(8,128)(2,1)S(1)}, bf16[2,2,16,128]{3,2,1,0:T(8,128)(2,1)S(1)}, u32[]{:S(2)}, u32[]{:S(2)}) collective-permute-start(bf16[2,2,16,128]{3,2,1,0:T(8,128)(2,1)S(1)} %pad_maximum_fusion.1), channel_id=1, source_target_pairs={{2,0},{3,1},{4,2},{5,3},{6,4},{7,5},{8,6},{9,7},{10,8},{11,9},{12,... | collective-permute-start | bytes 49160 | tf_op jit(solution)/shard_map/ppermute | solution.py:223
  94.0 15.4 %copy-start = (bf16[16,8,16,128]{3,2,1,0:T(8,128)(2,1)}, bf16[16,8,16,128]{3,2,1,0:T(8,128)(2,1)S(1)}, u32[]{:S(2)}) copy-start(bf16[16,8,16,128]{3,2,1,0:T(8,128)(2,1)S(1)} %all_to_all.11) | copy-start | bytes 1572868
  94.0 15.4 %collective-permute-start.2 = (bf16[128,16,128]{2,1,0:T(8,128)(2,1)S(1)}, bf16[128,16,128]{2,1,0:T(8,128)(2,1)S(1)}, u32[]{:S(2)}, u32[]{:S(2)}) collective-permute-start(bf16[128,16,128]{2,1,0:T(8,128)(2,1)S(1)} %bitcast.7), channel_id=1, source_target_pairs={{0,128},{128,0},{1,129},{129,1},{2,130},{130,2},{3,131},{131,3},{4... | collective-permute-start | bytes 1572872 | tf_op jit(solution)/shard_map/ppermute | solution.py:233
  109.4 0.8 copy-start.1
Sparse Core Ops, SparseCore 0:
  32.6 45.3 all-gather.2

commit v2 on v1

--- a/solution.py
+++ b/solution.py
@@ -11,10 +11,10 @@
 SOFTEN = 0.0025
 F32 = jnp.float32
 BF16 = jnp.bfloat16
+NN = (((1,), (0,)), ((), ()))
 NT = (((1,), (1,)), ((), ()))
 
 BLOCK = 10
-SHARE = BLOCK + 2 * BLOCK + 4
 
 
 def pack_kernel(rhs_ref, points_ref, basis_ref, transfer_ref, block_ref, cluster_ref):
@@ -31,7 +31,8 @@
         low = slice(leaf * 256, leaf * 256 + 128)
         high = slice(leaf * 256 + 128, leaf * 256 + 256)
         sides = rhs_ref[:, leaf * 256 : leaf * 256 + 256]
-        coeff = jnp.dot(sides, basis_ref[leaf], preferred_element_type=F32).astype(BF16)
+        coeff = lax.dot_general(sides, basis_ref[leaf], NT, preferred_element_type=F32)
+        coeff = coeff.astype(BF16)
         cluster = cluster + jnp.dot(coeff, transfer_ref[leaf], preferred_element_type=F32)
         coeffs.append(coeff.astype(F32))
         wide = sides.astype(F32)
@@ -46,16 +47,25 @@
     cluster_ref[...] = jnp.broadcast_to(packed[None], cluster_ref.shape)
 
 
-def locate(leaf_id, cols, my_col):
+def locate(leaf_id, cols):
     device = lax.shift_right_logical(leaf_id, 2)
     row = device // cols
-    gap = device - row * cols - my_col
-    side = (row - lax.rem(row, 2) + jnp.where(gap < 0, 1, 0)) * SHARE
-    return row, gap, side, lax.rem(leaf_id, 4)
-
-
-def near_kernel(cols, pos_ref, list_ref, count_ref, points_ref, share_ref, near_ref, wide_ref):
-    my_col = pos_ref[1]
+    gap = device - row * cols - lax.axis_index(("y", "z"))
+    fetched_here = (gap > 0) == (lax.axis_index("core") == 0)
+    return row, gap, fetched_here, lax.rem(leaf_id, 4)
+
+
+def near_kernel(
+    cols,
+    list_ref,
+    count_ref,
+    points_ref,
+    own_ref,
+    first_ref,
+    first_mate_ref,
+    near_ref,
+    wide_ref,
+):
     scale = F32(FOUR_PI * FOUR_PI)
     floor = F32(FOUR_PI * FOUR_PI * SOFTEN)
     row_ids = lax.broadcasted_iota(jnp.int32, (8, 128), 0)
@@ -66,11 +76,15 @@
             wide_ref[axis] = jnp.broadcast_to(own[:, axis : axis + 1], (256, 128))
 
         def slot_step(slot, total):
-            row, gap, side, source = locate(list_ref[leaf, slot], cols, my_col)
-            base = jnp.where(gap == 0, row * SHARE, side + BLOCK + lax.rem(row, 2) * BLOCK)
-            sides = share_ref[base + source].astype(F32)
-            parts = share_ref[base + 4 + source].astype(F32)
-            last = share_ref[base + 8].astype(F32)[:8]
+            row, gap, here, source = locate(list_ref[leaf, slot], cols)
+
+            def fetch(place):
+                beside = jnp.where(here, first_ref[row, place], first_mate_ref[row, place])
+                return jnp.where(gap == 0, own_ref[row, place], beside).astype(F32)
+
+            sides = fetch(source)
+            parts = fetch(4 + source)
+            last = fetch(8)[:8]
             tiles = []
             for half in range(2):
                 part = parts[half * 8 : half * 8 + 8]
@@ -105,18 +119,18 @@
 
 
 def far_kernel(
+    groups,
     cols,
-    ys,
-    zs,
-    pos_ref,
     coupling_list_ref,
     coupling_count_ref,
     coarse_list_ref,
     coarse_count_ref,
     owner_ref,
-    share_ref,
-    same_ref,
-    other_ref,
+    own_ref,
+    first_ref,
+    first_mate_ref,
+    last_ref,
+    last_mate_ref,
     leaf_coupling_ref,
     coarse_coupling_ref,
     transfer_ref,
@@ -125,15 +139,14 @@
     out_ref,
     source_ref,
 ):
-    my_row = pos_ref[0]
-    my_col = pos_ref[1]
+    my_core = lax.axis_index("core")
     for slot in range(16):
         device = owner_ref[coarse_list_ref[0, slot]]
         row = device // cols
         col = device - row * cols
-        tile_id = (row // 2) * (ys * zs // 4) + col // 4
-        mine = lax.rem(row, 2) == lax.rem(my_row, 2)
-        tile = jnp.where(mine, same_ref[tile_id], other_ref[tile_id]).astype(F32)
+        tile_id = (row // 2) * (cols // 4) + col // 4
+        mine = lax.rem(row, 2) == my_core
+        tile = jnp.where(mine, last_ref[tile_id], last_mate_ref[tile_id]).astype(F32)
         place = lax.rem(col, 4)
         picked = tile[0:4]
         for step in range(1, 4):
@@ -145,15 +158,13 @@
     coarse_field = couple(coarse_coupling_ref[0], source_ref[...])
     for leaf in range(4):
         for slot in range(16):
-            row, gap, side, source = locate(coupling_list_ref[leaf, slot], cols, my_col)
-            odd = lax.rem(row, 2)
+            row, gap, here, source = locate(coupling_list_ref[leaf, slot], cols)
             far = jnp.abs(gap)
-            tile_id = jnp.where(
-                far == 0,
-                row * SHARE + 9,
-                side + jnp.where(far == 1, 19 + odd * BLOCK, 28 + odd * 2 + far),
-            )
-            tile = share_ref[tile_id].astype(F32)
+            beyond = groups + row * 2 + jnp.where(far == 3, 1, 0)
+            one = jnp.where(here, first_ref[row, 9], first_mate_ref[row, 9])
+            more = jnp.where(here, last_ref[beyond], last_mate_ref[beyond])
+            tile = jnp.where(far == 0, own_ref[row, 9], jnp.where(far == 1, one, more))
+            tile = tile.astype(F32)
             half = jnp.where(source >= 2, tile[8:], tile[:8])
             half = jnp.where(lax.rem(source, 2) == 1, half[:, 64:], half[:, :64])
             live = slot < coupling_count_ref[leaf]
@@ -166,7 +177,7 @@
             preferred_element_type=F32,
         )
         local = local.T[:8].astype(BF16)
-        far_part = lax.dot_general(local, basis_ref[leaf], NT, preferred_element_type=F32)
+        far_part = lax.dot_general(local, basis_ref[leaf], NN, preferred_element_type=F32)
         span = slice(leaf * 256, leaf * 256 + 256)
         out_ref[:, span] = (near_ref[:, span] + far_part).astype(BF16)
 
@@ -189,13 +200,14 @@
     near_list,
     near_count,
 ):
+    rows = 2 * xs
     cols = ys * zs
     vmem = pl.BlockSpec(memory_space=pltpu.VMEM)
     smem = pl.BlockSpec(memory_space=pltpu.SMEM)
     row_axes = ("x", "core")
-    my_row = lax.axis_index(row_axes)
-    my_col = lax.axis_index(("y", "z"))
-    pos = jnp.stack([my_row, my_col]).astype(jnp.int32)
+    swap = [(0, 1), (1, 0)]
+    groups = xs * cols // 4
+    basis = jnp.swapaxes(basis, 1, 2)
 
     block, cluster = pl.pallas_call(
         pack_kernel,
@@ -217,48 +229,49 @@
                     pairs.append((core * cols + source, core * cols + col))
         return pairs
 
-    chip = lax.all_gather(block, "core", axis=0, tiled=False)
-    first = lax.ppermute(chip, ("core", "y", "z"), beside(1))
-    coeffs = jnp.concatenate([chip[:, 9:], first[:, 9:]], axis=1)
+    own = jnp.broadcast_to(block[None], (rows,) + block.shape)
+    own = lax.all_to_all(own, row_axes, 0, 0, tiled=True)
+    first = lax.ppermute(own, ("core", "y", "z"), beside(1))
+    own, cluster = lax.optimization_barrier((own, cluster))
+    line = lax.all_to_all(cluster, "z", 0, 0, tiled=True).reshape(zs // 4, 16, 128)
+    first, line = lax.optimization_barrier((first, line))
+    coeffs = jnp.concatenate([own[:, 9:], first[:, 9:]], axis=1)
     second = lax.ppermute(coeffs, ("core", "y", "z"), beside(2))
-    share = jnp.concatenate(
-        [block, first.reshape(2 * BLOCK, 16, 128), second.reshape(4, 16, 128)], axis=0
-    )
-    share, cluster = lax.optimization_barrier((share, cluster))
-    shares = lax.all_gather(share, row_axes, axis=0, tiled=True)
-
-    line = lax.all_to_all(cluster, "z", 0, 0, tiled=True).reshape(zs // 4, 16, 128)
+    first_mate = lax.ppermute(first, "core", swap)
     line = jnp.broadcast_to(line[None], (xs * ys,) + line.shape)
-    same = lax.all_to_all(line, ("x", "y"), 0, 0, tiled=True).reshape(xs * cols // 4, 16, 128)
-    other = lax.ppermute(same, "core", [(0, 1), (1, 0)])
+    line, coeffs = lax.optimization_barrier((line, coeffs))
+    same = lax.all_to_all(line, ("x", "y"), 0, 0, tiled=True).reshape(groups, 16, 128)
+    last = jnp.concatenate([same, second.reshape(rows * 2, 16, 128)], axis=0)
+    last_mate = lax.ppermute(last, "core", swap)
 
     near = pl.pallas_call(
         functools.partial(near_kernel, cols),
         out_shape=jax.ShapeDtypeStruct((8, 1024), F32),
-        in_specs=[smem] * 3 + [vmem] * 2,
+        in_specs=[smem] * 2 + [vmem] * 4,
         out_specs=vmem,
         scratch_shapes=[pltpu.VMEM((3, 256, 128), F32)],
         name="near",
         cost_estimate=pl.CostEstimate(flops=20_000_000, bytes_accessed=1_200_000, transcendentals=0),
-    )(pos, near_list, near_count, points, shares)
+    )(near_list, near_count, points, own, first, first_mate)
 
     return pl.pallas_call(
-        functools.partial(far_kernel, cols, ys, zs),
+        functools.partial(far_kernel, groups, cols),
         out_shape=jax.ShapeDtypeStruct((8, 1024), BF16),
-        in_specs=[smem] * 6 + [vmem] * 8,
+        in_specs=[smem] * 5 + [vmem] * 10,
         out_specs=vmem,
         scratch_shapes=[pltpu.VMEM((128, 64), F32)],
         name="far",
     )(
-        pos,
         coupling_list,
         coupling_count,
         coarse_list,
         coarse_count,
         owner,
-        shares,
-        same,
-        other,
+        own,
+        first,
+        first_mate,
+        last,
+        last_mate,
         leaf_coupling,
         coarse_coupling,
         transfer,

time: 123 us -> 109 us (0.89)
  blocking collectives: 77.3 us -> 24 us
  waiting for transfers between devices: 2.33 us -> 30.1 us
  starting transfers between devices: 8.63 us -> 34.5 us
  between operations: 14.1 us -> 0.76 us
  other arithmetic: 2.11 us -> 0.06 us
    all_to_all x2 -> x1, blocking collectives: 61.4 us -> 24 us  [per_device(): own = lax.all_to_all(own, row_axes, 0, 0, tiled=True)]
    all_to_all x0 -> x2, waiting for transfers between devices: none -> 27.8 us  [the longest x1 22 us: per_device(): lax.all_to_all(cluster, 'z', 0, 0, tiled=True).reshape(zs // 4, 16, 128)]
    all_to_all x0 -> x2, starting transfers between devices: none -> 23.8 us  [the longest x1 18.9 us: per_device(): lax.all_to_all(cluster, 'z', 0, 0, tiled=True).reshape(zs // 4, 16, 128)]
    all_gather x1 -> x0, blocking collectives: 15.9 us -> none  [per_device(): chip = lax.all_gather(block, 'core', axis=0, tiled=False)]
    concatenate x2, other arithmetic: 1.45 us -> 0.06 us  [the longest x1 0.05 us: per_device(): last = jnp.concatenate([same, second.reshape(rows * 2, 16, 128)], axis=0)]
    ppermute x2 -> x3, starting transfers between devices: 7.35 us -> 8.64 us  [the longest x1 5.42 us: per_device(): last_mate = lax.ppermute(last, 'core', swap)]
    unnamed x5 -> x10, local copies, waits for them, and re-layouts: 2.54 us -> 1.58 us
  transfers between devices with their start and end apart: 4 -> 6, of which waited for: 2 -> 4; matrix products, arithmetic and copies ran while one was open for 1% -> 0% of each run, Pallas kernels for 7% -> 7%
where the time goes in v2:
time: 109 us; the launch traced here: 108 us
  starting transfers between devices  34.5 us (32%)
  waiting for transfers between devices  30.1 us (28%)
  blocking collectives  24 us (22%)
  Pallas kernels  15.3 us (14%)
  local copies, waits for them, and re-layouts  3.3 us (3%)
    all_to_all x1, blocking collectives, per_device(): own = lax.all_to_all(own, row_axes, 0, 0, tiled=True)  24 us
    all_to_all x1, waiting for transfers between devices, per_device(): lax.all_to_all(cluster, 'z', 0, 0, tiled=True).reshape(zs // 4, 16, 128)  22 us
    all_to_all x1, starting transfers between devices, per_device(): lax.all_to_all(cluster, 'z', 0, 0, tiled=True).reshape(zs // 4, 16, 128)  18.9 us
    pallas_call x1, Pallas kernels, per_device(): pl.pallas_call(functools.partial(near_kernel, cols), out_shape=jax.ShapeD...  7.6 us
    all_to_all x1, waiting for transfers between devices, per_device(): lax.all_to_all(line, ('x', 'y'), 0, 0, tiled=True).reshape(groups, 16, 128)  5.84 us
    pallas_call x1, Pallas kernels, per_device(): pl.pallas_call(functools.partial(far_kernel, groups, cols), out_shape=jax...  5.81 us
    ppermute x1, starting transfers between devices, per_device(): last_mate = lax.ppermute(last, 'core', swap)  5.42 us
    all_to_all x1, starting transfers between devices, per_device(): lax.all_to_all(line, ('x', 'y'), 0, 0, tiled=True).reshape(groups, 16, 128)  4.9 us
  transfers between devices with their start and end apart: 6, of which 4 were waited for; matrix products, arithmetic and copies ran while one was open for 0% of the time, Pallas kernels for 7%

profile of v2, /device:TPU:1, one launch (start us, length us, event | category | flops | bytes accessed | tf_op | source)
XLA Modules:
  0.0 108.0 jit_solution(5474630479681883173)
XLA Ops:
  0.0 1.9 %pack.1 = (bf16[10,16,128]{2,1,0:T(8,128)(2,1)}, bf16[32,4,128]{2,1,0:T(4,128)(2,1)}) custom-call(bf16[8,1024]{1,0:T(8,128)(2,1)} %rhs_ref.1, f32[3,1024]{1,0:T(4,128)} %points_ref.3, bf16[4,64,256]{2,1,0:T(8,128)(2,1)} %bitcast.5, bf16[4,64,64]{2,1,0:T(8,128)(2,1)} %transfer_ref.3), custom_call_target="tpu_custom_call" | custom-call | tf_op jit(solution)/shard_map/pack/pallas_call | solution.py:212
  1.9 0.8 broadcast_in_dim.4
  2.7 24.0 %all_to_all.15.own_ref = bf16[8,10,16,128]{3,2,1,0:T(8,128)(2,1)S(1)} all-to-all(bf16[8,10,16,128]{3,2,1,0:T(8,128)(2,1)S(1)} %broadcast_in_dim.4), channel_id=1, replica_groups=mesh['x'=4,'core'=2,'y'=4,'z'=32] {'x','core'}, dimensions={0} | all-to-all | bytes 655360 | tf_op jit(solution)/shard_map/all_to_all | solution.py:233
  26.8 0.0 copy-start
  26.8 1.3 %collective-permute-start = (bf16[8,10,16,128]{3,2,1,0:T(8,128)(2,1)S(1)}, bf16[8,10,16,128]{3,2,1,0:T(8,128)(2,1)S(1)}, u32[]{:S(2)}, u32[]{:S(2)}) collective-permute-start(bf16[8,10,16,128]{3,2,1,0:T(8,128)(2,1)S(1)} %all_to_all.15.own_ref), channel_id=1, source_target_pairs={{1,0},{2,1},{3,2},{4,3},{5,4},{6,5},{7,6},{8,7},{9,8},{10,9},{11,1... | collective-permute-start | bytes 983048 | tf_op jit(solution)/shard_map/ppermute | solution.py:234
  28.1 18.9 %all-to-all-start.1 = ((bf16[32,4,128]{2,1,0:T(4,128)(2,1)}), bf16[32,4,128]{2,1,0:T(4,128)(2,1)S(1)}, u32[]{:S(2)}, u32[]{:S(2)}) async-start(bf16[32,4,128]{2,1,0:T(4,128)(2,1)} %get-tuple-element.15), calls=%async_computation.1 | async-start | bytes 65536 | tf_op jit(solution)/shard_map/all_to_all | solution.py:236
  47.0 22.0 %all-to-all-done.1 = bf16[32,4,128]{2,1,0:T(4,128)(2,1)S(1)} async-done(((bf16[32,4,128]{2,1,0:T(4,128)(2,1)}), bf16[32,4,128]{2,1,0:T(4,128)(2,1)S(1)}, u32[]{:S(2)}, u32[]{:S(2)}) %all-to-all-start.1) | async-done | bytes 32800 | tf_op jit(solution)/shard_map/all_to_all | solution.py:236
  68.9 0.0 collective-permute-done.first_ref
  68.9 0.0 copy-start.2
  69.0 0.9 broadcast_in_dim.5
  69.9 0.0 copy-done
  69.9 4.9 %all-to-all-start.2 = ((bf16[16,8,16,128]{3,2,1,0:T(8,128)(2,1)}), bf16[16,8,16,128]{3,2,1,0:T(8,128)(2,1)S(1)}, u32[]{:S(2)}, u32[]{:S(2)}) async-start(bf16[16,8,16,128]{3,2,1,0:T(8,128)(2,1)} %broadcast_in_dim.5), calls=%async_computation.2 | async-start | bytes 1048576 | tf_op jit(solution)/shard_map/all_to_all | solution.py:243
  74.8 2.1 %collective-permute-start.2 = (bf16[8,2,16,128]{3,2,1,0:T(8,128)(2,1)S(1)}, bf16[8,2,16,128]{3,2,1,0:T(8,128)(2,1)S(1)}, u32[]{:S(2)}, u32[]{:S(2)}) collective-permute-start(bf16[8,2,16,128]{3,2,1,0:T(8,128)(2,1)S(1)} %pad_maximum_fusion.1), channel_id=1, source_target_pairs={{2,0},{3,1},{4,2},{5,3},{6,4},{7,5},{8,6},{9,7},{10,8},{11,9},{12,... | collective-permute-start | bytes 196616 | tf_op jit(solution)/shard_map/ppermute | solution.py:239
  76.9 1.3 %collective-permute-done.2 = bf16[8,2,16,128]{3,2,1,0:T(8,128)(2,1)S(1)} collective-permute-done((bf16[8,2,16,128]{3,2,1,0:T(8,128)(2,1)S(1)}, bf16[8,2,16,128]{3,2,1,0:T(8,128)(2,1)S(1)}, u32[]{:S(2)}, u32[]{:S(2)}) %collective-permute-start.2) | collective-permute-done | bytes 65568 | tf_op jit(solution)/shard_map/ppermute | solution.py:239
  78.2 5.8 %all-to-all-done.2 = bf16[16,8,16,128]{3,2,1,0:T(8,128)(2,1)S(1)} async-done(((bf16[16,8,16,128]{3,2,1,0:T(8,128)(2,1)}), bf16[16,8,16,128]{3,2,1,0:T(8,128)(2,1)S(1)}, u32[]{:S(2)}, u32[]{:S(2)}) %all-to-all-start.2) | async-done | bytes 524320 | tf_op jit(solution)/shard_map/all_to_all | solution.py:243
  84.0 0.1 pad_maximum_fusion.last_ref
  84.1 0.0 copy-start.1
  84.1 5.4 %collective-permute-start.3 = (bf16[144,16,128]{2,1,0:T(8,128)(2,1)S(1)}, bf16[144,16,128]{2,1,0:T(8,128)(2,1)S(1)}, u32[]{:S(2)}, u32[]{:S(2)}) collective-permute-start(bf16[144,16,128]{2,1,0:T(8,128)(2,1)S(1)} %pad_maximum_fusion.last_ref), channel_id=1, source_target_pairs={{0,128},{128,0},{1,129},{129,1},{2,130},{130,2},{3,131},{131,3},{4... | collective-permute-start | bytes 1769480 | tf_op jit(solution)/shard_map/ppermute | solution.py:245
  89.5 0.0 copy-done.2
  89.5 1.9 %collective-permute-start.1 = (bf16[8,10,16,128]{3,2,1,0:T(8,128)(2,1)S(1)}, bf16[8,10,16,128]{3,2,1,0:T(8,128)(2,1)S(1)}, u32[]{:S(2)}, u32[]{:S(2)}) collective-permute-start(bf16[8,10,16,128]{3,2,1,0:T(8,128)(2,1)S(1)} %collective-permute-done.first_ref), channel_id=1, source_target_pairs={{0,128},{128,0},{1,129},{129,1},{2,130},{130,2},{3,131},{131,3},{4... | collective-permute-start | bytes 983048 | tf_op jit(solution)/shard_map/ppermute | solution.py:240
  92.1 0.9 collective-permute-done.1.first_mate_ref
  93.0 0.0 copy-start.3
  93.0 0.8 copy-done.3
  93.8 7.6 %near.1.near_ref = f32[8,1024]{1,0:T(8,128)} custom-call(s32[4,8]{1,0:T(4,128)} %list_ref.1, s32[4]{0:T(128)} %count_ref.1, f32[3,1024]{1,0:T(4,128)} %points_ref.3, bf16[8,10,16,128]{3,2,1,0:T(8,128)(2,1)} %copy-done, bf16[8,10,16,128]{3,2,1,0:T(8,128)(2,1)} %copy-done.2, bf16[8,10,16,128]{3,2,1,0:T(8,128)(2,1)} %copy-done.3), custom_call_target="tpu_custom_call" | custom-call | flops 20000000 | bytes 1200000 | tf_op jit(solution)/shard_map/near/pallas_call | solution.py:247
  101.4 0.0 collective-permute-done.3.last_mate_ref
  101.4 0.0 copy-done.1
  101.4 0.0 copy-start.4
  101.4 0.8 copy-done.4
  102.2 5.8 %far.1 = bf16[8,1024]{1,0:T(8,128)(2,1)} custom-call(s32[4,16]{1,0:T(4,128)} %coupling_list_ref.1, s32[4]{0:T(128)} %coupling_count_ref.1, s32[1,16]{1,0:T(1,128)} %coarse_list_ref.1, s32[1]{0:T(128)S(6)} %copy.14.coarse_count_ref, s32[1024]{0:T(1024)} %owner_ref.1, bf16[8,10,16,128]{3,2,1,0:T(8,128)(2,1)} %copy-done, bf16[8,10,16,128]{3,2,1,0:T(8,128)(2,1)} %copy-done.2, ...), custom_call_target="tpu_custom_call" | custom-call | tf_op jit(solution)/shard_map/far/pallas_call | solution.py:257
  (3 shorter events, 0.0 us)
Async XLA Ops:
  26.8 43.1 %copy-start = (bf16[8,10,16,128]{3,2,1,0:T(8,128)(2,1)}, bf16[8,10,16,128]{3,2,1,0:T(8,128)(2,1)S(1)}, u32[]{:S(2)}) copy-start(bf16[8,10,16,128]{3,2,1,0:T(8,128)(2,1)S(1)} %all_to_all.15.own_ref) | copy-start | bytes 983044
  26.8 42.2 %collective-permute-start = (bf16[8,10,16,128]{3,2,1,0:T(8,128)(2,1)S(1)}, bf16[8,10,16,128]{3,2,1,0:T(8,128)(2,1)S(1)}, u32[]{:S(2)}, u32[]{:S(2)}) collective-permute-start(bf16[8,10,16,128]{3,2,1,0:T(8,128)(2,1)S(1)} %all_to_all.15.own_ref), channel_id=1, source_target_pairs={{1,0},{2,1},{3,2},{4,3},{5,4},{6,5},{7,6},{8,7},{9,8},{10,9},{11,1... | collective-permute-start | bytes 983048 | tf_op jit(solution)/shard_map/ppermute | solution.py:234
  28.1 40.9 %all-to-all-start.1 = ((bf16[32,4,128]{2,1,0:T(4,128)(2,1)}), bf16[32,4,128]{2,1,0:T(4,128)(2,1)S(1)}, u32[]{:S(2)}, u32[]{:S(2)}) async-start(bf16[32,4,128]{2,1,0:T(4,128)(2,1)} %get-tuple-element.15), calls=%async_computation.1 | async-start | bytes 65536 | tf_op jit(solution)/shard_map/all_to_all | solution.py:236
  68.9 20.6 %copy-start.2 = (bf16[8,10,16,128]{3,2,1,0:T(8,128)(2,1)}, bf16[8,10,16,128]{3,2,1,0:T(8,128)(2,1)S(1)}, u32[]{:S(2)}) copy-start(bf16[8,10,16,128]{3,2,1,0:T(8,128)(2,1)S(1)} %collective-permute-done.first_ref) | copy-start | bytes 983044
  69.9 14.1 %all-to-all-start.2 = ((bf16[16,8,16,128]{3,2,1,0:T(8,128)(2,1)}), bf16[16,8,16,128]{3,2,1,0:T(8,128)(2,1)S(1)}, u32[]{:S(2)}, u32[]{:S(2)}) async-start(bf16[16,8,16,128]{3,2,1,0:T(8,128)(2,1)} %broadcast_in_dim.5), calls=%async_computation.2 | async-start | bytes 1048576 | tf_op jit(solution)/shard_map/all_to_all | solution.py:243
  74.8 3.4 %collective-permute-start.2 = (bf16[8,2,16,128]{3,2,1,0:T(8,128)(2,1)S(1)}, bf16[8,2,16,128]{3,2,1,0:T(8,128)(2,1)S(1)}, u32[]{:S(2)}, u32[]{:S(2)}) collective-permute-start(bf16[8,2,16,128]{3,2,1,0:T(8,128)(2,1)S(1)} %pad_maximum_fusion.1), channel_id=1, source_target_pairs={{2,0},{3,1},{4,2},{5,3},{6,4},{7,5},{8,6},{9,7},{10,8},{11,9},{12,... | collective-permute-start | bytes 196616 | tf_op jit(solution)/shard_map/ppermute | solution.py:239
  84.1 17.3 %copy-start.1 = (bf16[144,16,128]{2,1,0:T(8,128)(2,1)}, bf16[144,16,128]{2,1,0:T(8,128)(2,1)S(1)}, u32[]{:S(2)}) copy-start(bf16[144,16,128]{2,1,0:T(8,128)(2,1)S(1)} %pad_maximum_fusion.last_ref) | copy-start | bytes 1769476
  84.1 17.3 %collective-permute-start.3 = (bf16[144,16,128]{2,1,0:T(8,128)(2,1)S(1)}, bf16[144,16,128]{2,1,0:T(8,128)(2,1)S(1)}, u32[]{:S(2)}, u32[]{:S(2)}) collective-permute-start(bf16[144,16,128]{2,1,0:T(8,128)(2,1)S(1)} %pad_maximum_fusion.last_ref), channel_id=1, source_target_pairs={{0,128},{128,0},{1,129},{129,1},{2,130},{130,2},{3,131},{131,3},{4... | collective-permute-start | bytes 1769480 | tf_op jit(solution)/shard_map/ppermute | solution.py:245
  89.5 3.5 %collective-permute-start.1 = (bf16[8,10,16,128]{3,2,1,0:T(8,128)(2,1)S(1)}, bf16[8,10,16,128]{3,2,1,0:T(8,128)(2,1)S(1)}, u32[]{:S(2)}, u32[]{:S(2)}) collective-permute-start(bf16[8,10,16,128]{3,2,1,0:T(8,128)(2,1)S(1)} %collective-permute-done.first_ref), channel_id=1, source_target_pairs={{0,128},{128,0},{1,129},{129,1},{2,130},{130,2},{3,131},{131,3},{4... | collective-permute-start | bytes 983048 | tf_op jit(solution)/shard_map/ppermute | solution.py:240
  93.0 0.8 copy-start.3
  101.4 0.8 copy-start.4

commit v3 on v2

--- a/solution.py
+++ b/solution.py
@@ -121,6 +121,7 @@
 def far_kernel(
     groups,
     cols,
+    zs,
     coupling_list_ref,
     coupling_count_ref,
     coarse_list_ref,
@@ -144,6 +145,7 @@
         device = owner_ref[coarse_list_ref[0, slot]]
         row = device // cols
         col = device - row * cols
+        col = col - lax.rem(col, zs) + lax.rem(col + zs // 2, zs)
         tile_id = (row // 2) * (cols // 4) + col // 4
         mine = lax.rem(row, 2) == my_core
         tile = jnp.where(mine, last_ref[tile_id], last_mate_ref[tile_id]).astype(F32)
@@ -207,6 +209,7 @@
     row_axes = ("x", "core")
     swap = [(0, 1), (1, 0)]
     groups = xs * cols // 4
+    turned = [(place + zs // 2) % zs for place in range(zs)]
     basis = jnp.swapaxes(basis, 1, 2)
 
     block, cluster = pl.pallas_call(
@@ -233,16 +236,15 @@
     own = lax.all_to_all(own, row_axes, 0, 0, tiled=True)
     first = lax.ppermute(own, ("core", "y", "z"), beside(1))
     own, cluster = lax.optimization_barrier((own, cluster))
-    line = lax.all_to_all(cluster, "z", 0, 0, tiled=True).reshape(zs // 4, 16, 128)
+    line = lax.all_to_all(
+        cluster, "z", 0, 0, tiled=True, axis_index_groups=[turned]
+    ).reshape(zs // 4, 16, 128)
     first, line = lax.optimization_barrier((first, line))
+    first_mate = lax.ppermute(first, "core", swap)
     coeffs = jnp.concatenate([own[:, 9:], first[:, 9:]], axis=1)
     second = lax.ppermute(coeffs, ("core", "y", "z"), beside(2))
-    first_mate = lax.ppermute(first, "core", swap)
     line = jnp.broadcast_to(line[None], (xs * ys,) + line.shape)
-    line, coeffs = lax.optimization_barrier((line, coeffs))
     same = lax.all_to_all(line, ("x", "y"), 0, 0, tiled=True).reshape(groups, 16, 128)
-    last = jnp.concatenate([same, second.reshape(rows * 2, 16, 128)], axis=0)
-    last_mate = lax.ppermute(last, "core", swap)
 
     near = pl.pallas_call(
         functools.partial(near_kernel, cols),
@@ -251,11 +253,17 @@
         out_specs=vmem,
         scratch_shapes=[pltpu.VMEM((3, 256, 128), F32)],
         name="near",
-        cost_estimate=pl.CostEstimate(flops=20_000_000, bytes_accessed=1_200_000, transcendentals=0),
+        cost_estimate=pl.CostEstimate(
+            flops=4_000_000_000, bytes_accessed=1_200_000, transcendentals=0
+        ),
     )(near_list, near_count, points, own, first, first_mate)
 
+    same, second, near = lax.optimization_barrier((same, second, near))
+    last = jnp.concatenate([same, second.reshape(rows * 2, 16, 128)], axis=0)
+    last_mate = lax.ppermute(last, "core", swap)
+
     return pl.pallas_call(
-        functools.partial(far_kernel, groups, cols),
+        functools.partial(far_kernel, groups, cols, zs),
         out_shape=jax.ShapeDtypeStruct((8, 1024), BF16),
         in_specs=[smem] * 5 + [vmem] * 10,
         out_specs=vmem,

time: 109 us -> 94 us (0.86)
  waiting for transfers between devices: 30.1 us -> 1.33 us
  blocking collectives: 24 us -> 52.1 us
  starting transfers between devices: 34.5 us -> 18.3 us
  Pallas kernels: 15.3 us -> 16.9 us
    all_to_all x0 -> x1, blocking collectives: none -> 28.1 us  [per_device(): lax.all_to_all(cluster, 'z', 0, 0, tiled=True, axis_index_groups=[turned])]
    all_to_all x1 -> x0, waiting for transfers between devices: 22 us -> none  [per_device(): lax.all_to_all(cluster, 'z', 0, 0, tiled=True).reshape(zs // 4, 16, 128)]
    all_to_all x1 -> x0, starting transfers between devices: 18.9 us -> none  [per_device(): lax.all_to_all(cluster, 'z', 0, 0, tiled=True).reshape(zs // 4, 16, 128)]
    all_to_all x1, waiting for transfers between devices: 5.84 us -> 0.01 us  [per_device(): lax.all_to_all(line, ('x', 'y'), 0, 0, tiled=True).reshape(groups, 16, 128)]
    ppermute x1, starting transfers between devices: 5.42 us -> 1.92 us  [per_device(): last_mate = lax.ppermute(last, 'core', swap)]
    ppermute x1, starting transfers between devices: 1.92 us -> 4.5 us  [per_device(): first_mate = lax.ppermute(first, 'core', swap)]
    ppermute x1, starting transfers between devices: 2.08 us -> 4.03 us  [per_device(): second = lax.ppermute(coeffs, ('core', 'y', 'z'), beside(2))]
    all_to_all x1, starting transfers between devices: 4.9 us -> 6.54 us  [per_device(): lax.all_to_all(line, ('x', 'y'), 0, 0, tiled=True).reshape(groups, 16, 128)]
  transfers between devices with their start and end apart: 6 -> 5, of which waited for: 4 -> 1; matrix products, arithmetic and copies ran while one was open for 0% -> 1% of each run, Pallas kernels for 7% -> 10%
where the time goes in v3:
time: 94 us; the launch traced here: 92.8 us
  blocking collectives  52.1 us (55%)
  starting transfers between devices  18.3 us (19%)
  Pallas kernels  16.9 us (18%)
  local copies, waits for them, and re-layouts  3.33 us (4%)
  waiting for transfers between devices  1.33 us (1%)
    all_to_all x1, blocking collectives, per_device(): lax.all_to_all(cluster, 'z', 0, 0, tiled=True, axis_index_groups=[turned])  28.1 us
    all_to_all x1, blocking collectives, per_device(): own = lax.all_to_all(own, row_axes, 0, 0, tiled=True)  24 us
    pallas_call x1, Pallas kernels, per_device(): pl.pallas_call(functools.partial(near_kernel, cols), out_shape=jax.ShapeD...  9.09 us
    all_to_all x1, starting transfers between devices, per_device(): lax.all_to_all(line, ('x', 'y'), 0, 0, tiled=True).reshape(groups, 16, 128)  6.54 us
    pallas_call x1, Pallas kernels, per_device(): pl.pallas_call(functools.partial(far_kernel, groups, cols, zs), out_shape...  5.88 us
    ppermute x1, starting transfers between devices, per_device(): first_mate = lax.ppermute(first, 'core', swap)  4.5 us
    ppermute x1, starting transfers between devices, per_device(): second = lax.ppermute(coeffs, ('core', 'y', 'z'), beside(2))  4.03 us
    ppermute x1, starting transfers between devices, per_device(): last_mate = lax.ppermute(last, 'core', swap)  1.92 us
  transfers between devices with their start and end apart: 5, of which 1 were waited for; matrix products, arithmetic and copies ran while one was open for 1% of the time, Pallas kernels for 10%

profile of v3, /device:TPU:1, one launch (start us, length us, event | category | flops | bytes accessed | tf_op | source)
XLA Modules:
  0.0 92.8 jit_solution(10509923035016840310)
XLA Ops:
  0.0 1.9 %pack.1 = (bf16[10,16,128]{2,1,0:T(8,128)(2,1)}, bf16[32,4,128]{2,1,0:T(4,128)(2,1)}) custom-call(bf16[8,1024]{1,0:T(8,128)(2,1)} %rhs_ref.1, f32[3,1024]{1,0:T(4,128)} %points_ref.3, bf16[4,64,256]{2,1,0:T(8,128)(2,1)} %bitcast.5, bf16[4,64,64]{2,1,0:T(8,128)(2,1)} %transfer_ref.3), custom_call_target="tpu_custom_call" | custom-call | tf_op jit(solution)/shard_map/pack/pallas_call | solution.py:215
  1.9 0.8 broadcast_in_dim.4
  2.7 0.0 copy-start.5
  2.7 24.0 %all_to_all.15.own_ref = bf16[8,10,16,128]{3,2,1,0:T(8,128)(2,1)S(1)} all-to-all(bf16[8,10,16,128]{3,2,1,0:T(8,128)(2,1)S(1)} %broadcast_in_dim.4), channel_id=1, replica_groups=mesh['x'=4,'core'=2,'y'=4,'z'=32] {'x','core'}, dimensions={0} | all-to-all | bytes 655360 | tf_op jit(solution)/shard_map/all_to_all | solution.py:236
  26.8 0.0 copy-start.1
  26.8 1.3 %collective-permute-start = (bf16[8,10,16,128]{3,2,1,0:T(8,128)(2,1)S(1)}, bf16[8,10,16,128]{3,2,1,0:T(8,128)(2,1)S(1)}, u32[]{:S(2)}, u32[]{:S(2)}) collective-permute-start(bf16[8,10,16,128]{3,2,1,0:T(8,128)(2,1)S(1)} %all_to_all.15.own_ref), channel_id=1, source_target_pairs={{1,0},{2,1},{3,2},{4,3},{5,4},{6,5},{7,6},{8,7},{9,8},{10,9},{11,1... | collective-permute-start | bytes 983048 | tf_op jit(solution)/shard_map/ppermute | solution.py:237
  28.1 0.0 copy-done.5
  28.1 28.1 %all_to_all.16 = bf16[32,4,128]{2,1,0:T(4,128)(2,1)S(1)} all-to-all(bf16[32,4,128]{2,1,0:T(4,128)(2,1)S(1)} %copy-done.5), channel_id=1, replica_groups={{16,17,18,19,20,21,22,23,24,25,26,27,28,29,30,31,0,1,2,3,4,5,6,7,8,9,10..., dimensions={0} | all-to-all | bytes 65536 | tf_op jit(solution)/shard_map/all_to_all | solution.py:239
  56.1 0.0 collective-permute-done.first_ref
  56.1 0.0 copy-start.3
  56.1 4.5 %collective-permute-start.1 = (bf16[8,10,16,128]{3,2,1,0:T(8,128)(2,1)S(1)}, bf16[8,10,16,128]{3,2,1,0:T(8,128)(2,1)S(1)}, u32[]{:S(2)}, u32[]{:S(2)}) collective-permute-start(bf16[8,10,16,128]{3,2,1,0:T(8,128)(2,1)S(1)} %collective-permute-done.first_ref), channel_id=1, source_target_pairs={{0,128},{128,0},{1,129},{129,1},{2,130},{130,2},{3,131},{131,3},{4... | collective-permute-start | bytes 983048 | tf_op jit(solution)/shard_map/ppermute | solution.py:243
  60.7 0.9 broadcast_in_dim.5
  61.6 6.5 %all-to-all-start.2 = ((bf16[16,8,16,128]{3,2,1,0:T(8,128)(2,1)}), bf16[16,8,16,128]{3,2,1,0:T(8,128)(2,1)S(1)}, u32[]{:S(2)}, u32[]{:S(2)}) async-start(bf16[16,8,16,128]{3,2,1,0:T(8,128)(2,1)} %broadcast_in_dim.5), calls=%async_computation.2 | async-start | bytes 1048576 | tf_op jit(solution)/shard_map/all_to_all | solution.py:247
  68.1 0.0 copy-done.1
  68.1 0.0 copy-done.3
  68.2 4.0 %collective-permute-start.2 = (bf16[8,2,16,128]{3,2,1,0:T(8,128)(2,1)S(1)}, bf16[8,2,16,128]{3,2,1,0:T(8,128)(2,1)S(1)}, u32[]{:S(2)}, u32[]{:S(2)}) collective-permute-start(bf16[8,2,16,128]{3,2,1,0:T(8,128)(2,1)S(1)} %pad_maximum_fusion.1), channel_id=1, source_target_pairs={{2,0},{3,1},{4,2},{5,3},{6,4},{7,5},{8,6},{9,7},{10,8},{11,9},{12,... | collective-permute-start | bytes 196616 | tf_op jit(solution)/shard_map/ppermute | solution.py:245
  72.2 0.0 collective-permute-done.1.first_mate_ref
  72.2 0.0 copy-start.4
  72.2 0.8 copy-done.4
  73.0 9.1 %near.1.near_ref = f32[8,1024]{1,0:T(8,128)} custom-call(s32[4,8]{1,0:T(4,128)} %list_ref.1, s32[4]{0:T(128)} %count_ref.1, f32[3,1024]{1,0:T(4,128)} %points_ref.3, bf16[8,10,16,128]{3,2,1,0:T(8,128)(2,1)} %copy-done.1, bf16[8,10,16,128]{3,2,1,0:T(8,128)(2,1)} %copy-done.3, bf16[8,10,16,128]{3,2,1,0:T(8,128)(2,1)} %copy-done.4), custom_call_target="tpu_custom_call" | custom-call | flops 4000000000 | bytes 1200000 | tf_op jit(solution)/shard_map/near/pallas_call | solution.py:249
  82.1 0.0 collective-permute-done.2
  82.1 0.0 all-to-all-done.2
  82.1 0.1 pad_maximum_fusion.last_ref
  82.2 0.0 copy-start
  82.2 1.9 %collective-permute-start.3 = (bf16[144,16,128]{2,1,0:T(8,128)(2,1)S(1)}, bf16[144,16,128]{2,1,0:T(8,128)(2,1)S(1)}, u32[]{:S(2)}, u32[]{:S(2)}) collective-permute-start(bf16[144,16,128]{2,1,0:T(8,128)(2,1)S(1)} %pad_maximum_fusion.last_ref), channel_id=1, source_target_pairs={{0,128},{128,0},{1,129},{129,1},{2,130},{130,2},{3,131},{131,3},{4... | collective-permute-start | bytes 1769480 | tf_op jit(solution)/shard_map/ppermute | solution.py:263
  84.8 1.3 %collective-permute-done.3.last_mate_ref = bf16[144,16,128]{2,1,0:T(8,128)(2,1)S(1)} collective-permute-done((bf16[144,16,128]{2,1,0:T(8,128)(2,1)S(1)}, bf16[144,16,128]{2,1,0:T(8,128)(2,1)S(1)}, u32[]{:S(2)}, u32[]{:S(2)}) %collective-permute-start.3) | collective-permute-done | bytes 589856 | tf_op jit(solution)/shard_map/ppermute | solution.py:263
  86.1 0.0 copy-done
  86.1 0.0 copy-start.2
  86.1 0.8 copy-done.2
  86.9 5.9 %far.1 = bf16[8,1024]{1,0:T(8,128)(2,1)} custom-call(s32[4,16]{1,0:T(4,128)} %coupling_list_ref.1, s32[4]{0:T(128)} %coupling_count_ref.1, s32[1,16]{1,0:T(1,128)} %coarse_list_ref.1, s32[1]{0:T(128)S(6)} %copy.14.coarse_count_ref, s32[1024]{0:T(1024)} %owner_ref.1, bf16[8,10,16,128]{3,2,1,0:T(8,128)(2,1)} %copy-done.1, bf16[8,10,16,128]{3,2,1,0:T(8,128)(2,1)} %copy-done.3, ...), custom_call_target="tpu_custom_call" | custom-call | tf_op jit(solution)/shard_map/far/pallas_call | solution.py:265
  (3 shorter events, 0.0 us)
Async XLA Ops:
  2.7 25.3 %copy-start.5 = (bf16[32,4,128]{2,1,0:T(4,128)(2,1)S(1)}, bf16[32,4,128]{2,1,0:T(4,128)(2,1)}, u32[]{:S(2)}) copy-start(bf16[32,4,128]{2,1,0:T(4,128)(2,1)} %get-tuple-element.17) | copy-start | bytes 98308
  26.8 41.4 %copy-start.1 = (bf16[8,10,16,128]{3,2,1,0:T(8,128)(2,1)}, bf16[8,10,16,128]{3,2,1,0:T(8,128)(2,1)S(1)}, u32[]{:S(2)}) copy-start(bf16[8,10,16,128]{3,2,1,0:T(8,128)(2,1)S(1)} %all_to_all.15.own_ref) | copy-start | bytes 983044
  26.8 29.4 %collective-permute-start = (bf16[8,10,16,128]{3,2,1,0:T(8,128)(2,1)S(1)}, bf16[8,10,16,128]{3,2,1,0:T(8,128)(2,1)S(1)}, u32[]{:S(2)}, u32[]{:S(2)}) collective-permute-start(bf16[8,10,16,128]{3,2,1,0:T(8,128)(2,1)S(1)} %all_to_all.15.own_ref), channel_id=1, source_target_pairs={{1,0},{2,1},{3,2},{4,3},{5,4},{6,5},{7,6},{8,7},{9,8},{10,9},{11,1... | collective-permute-start | bytes 983048 | tf_op jit(solution)/shard_map/ppermute | solution.py:237
  56.1 12.0 %copy-start.3 = (bf16[8,10,16,128]{3,2,1,0:T(8,128)(2,1)}, bf16[8,10,16,128]{3,2,1,0:T(8,128)(2,1)S(1)}, u32[]{:S(2)}) copy-start(bf16[8,10,16,128]{3,2,1,0:T(8,128)(2,1)S(1)} %collective-permute-done.first_ref) | copy-start | bytes 983044
  56.1 16.1 %collective-permute-start.1 = (bf16[8,10,16,128]{3,2,1,0:T(8,128)(2,1)S(1)}, bf16[8,10,16,128]{3,2,1,0:T(8,128)(2,1)S(1)}, u32[]{:S(2)}, u32[]{:S(2)}) collective-permute-start(bf16[8,10,16,128]{3,2,1,0:T(8,128)(2,1)S(1)} %collective-permute-done.first_ref), channel_id=1, source_target_pairs={{0,128},{128,0},{1,129},{129,1},{2,130},{130,2},{3,131},{131,3},{4... | collective-permute-start | bytes 983048 | tf_op jit(solution)/shard_map/ppermute | solution.py:243
  61.6 20.5 %all-to-all-start.2 = ((bf16[16,8,16,128]{3,2,1,0:T(8,128)(2,1)}), bf16[16,8,16,128]{3,2,1,0:T(8,128)(2,1)S(1)}, u32[]{:S(2)}, u32[]{:S(2)}) async-start(bf16[16,8,16,128]{3,2,1,0:T(8,128)(2,1)} %broadcast_in_dim.5), calls=%async_computation.2 | async-start | bytes 1048576 | tf_op jit(solution)/shard_map/all_to_all | solution.py:247
  68.2 13.9 %collective-permute-start.2 = (bf16[8,2,16,128]{3,2,1,0:T(8,128)(2,1)S(1)}, bf16[8,2,16,128]{3,2,1,0:T(8,128)(2,1)S(1)}, u32[]{:S(2)}, u32[]{:S(2)}) collective-permute-start(bf16[8,2,16,128]{3,2,1,0:T(8,128)(2,1)S(1)} %pad_maximum_fusion.1), channel_id=1, source_target_pairs={{2,0},{3,1},{4,2},{5,3},{6,4},{7,5},{8,6},{9,7},{10,8},{11,9},{12,... | collective-permute-start | bytes 196616 | tf_op jit(solution)/shard_map/ppermute | solution.py:245
  72.2 0.8 copy-start.4
  82.2 3.9 %copy-start = (bf16[144,16,128]{2,1,0:T(8,128)(2,1)}, bf16[144,16,128]{2,1,0:T(8,128)(2,1)S(1)}, u32[]{:S(2)}) copy-start(bf16[144,16,128]{2,1,0:T(8,128)(2,1)S(1)} %pad_maximum_fusion.last_ref) | copy-start | bytes 1769476
  82.2 3.9 %collective-permute-start.3 = (bf16[144,16,128]{2,1,0:T(8,128)(2,1)S(1)}, bf16[144,16,128]{2,1,0:T(8,128)(2,1)S(1)}, u32[]{:S(2)}, u32[]{:S(2)}) collective-permute-start(bf16[144,16,128]{2,1,0:T(8,128)(2,1)S(1)} %pad_maximum_fusion.last_ref), channel_id=1, source_target_pairs={{0,128},{128,0},{1,129},{129,1},{2,130},{130,2},{3,131},{131,3},{4... | collective-permute-start | bytes 1769480 | tf_op jit(solution)/shard_map/ppermute | solution.py:263
  86.1 0.8 copy-start.2

commit v4 on v3

--- a/solution.py
+++ b/solution.py
@@ -17,7 +17,8 @@
 BLOCK = 10
 
 
-def pack_kernel(rhs_ref, points_ref, basis_ref, transfer_ref, block_ref, cluster_ref):
+def pack_kernel(rhs_ref, points_ref, basis_ref, transfer_ref, copies_ref, cluster_ref):
+    block_ref = copies_ref.at[0]
     points = points_ref[...]
     part_hi = points.astype(BF16).astype(F32)
     rest = points - part_hi
@@ -43,16 +44,19 @@
     block_ref[9] = jnp.concatenate(
         [jnp.concatenate(coeffs[:2], axis=1), jnp.concatenate(coeffs[2:], axis=1)], axis=0
     ).astype(BF16)
+    block = block_ref[...]
+    for copy in range(1, copies_ref.shape[0]):
+        copies_ref[copy] = block
     packed = jnp.concatenate([cluster[:4], cluster[4:]], axis=1).astype(BF16)
     cluster_ref[...] = jnp.broadcast_to(packed[None], cluster_ref.shape)
 
 
 def locate(leaf_id, cols):
     device = lax.shift_right_logical(leaf_id, 2)
-    row = device // cols
-    gap = device - row * cols - lax.axis_index(("y", "z"))
+    row = lax.shift_right_logical(device, cols.bit_length() - 1)
+    gap = (device & (cols - 1)) - lax.axis_index(("y", "z"))
     fetched_here = (gap > 0) == (lax.axis_index("core") == 0)
-    return row, gap, fetched_here, lax.rem(leaf_id, 4)
+    return row, gap, fetched_here, leaf_id & 3
 
 
 def near_kernel(
@@ -69,39 +73,62 @@
     scale = F32(FOUR_PI * FOUR_PI)
     floor = F32(FOUR_PI * FOUR_PI * SOFTEN)
     row_ids = lax.broadcasted_iota(jnp.int32, (8, 128), 0)
+
+    def source_of(leaf, slot):
+        row, gap, here, source = locate(list_ref[leaf, slot], cols)
+
+        def fetch(place):
+            beside = jnp.where(here, first_ref[row, place], first_mate_ref[row, place])
+            return jnp.where(gap == 0, own_ref[row, place], beside).astype(F32)
+
+        sides = fetch(source)
+        sides = jnp.concatenate([sides[:8], sides[8:]], axis=1)
+        sides = jnp.where(slot < count_ref[leaf], sides, 0.0).astype(BF16)
+        parts = fetch(4 + source)
+        last = fetch(8)[:8]
+        halves = []
+        for half in range(2):
+            part = parts[half * 8 : half * 8 + 8]
+            tail = jnp.sum(
+                jnp.where(row_ids == source * 2 + half, last, 0.0), axis=0, keepdims=True
+            )
+            place = (
+                part[0:1] + part[3:4] + part[6:7],
+                part[1:2] + part[4:5] + part[7:8],
+                part[2:3] + part[5:6] + tail,
+            )
+            halves.append([jnp.broadcast_to(line, (8, 128)) for line in place])
+        return sides, halves
+
     for leaf in range(4):
         own = points_ref[:, leaf * 256 : leaf * 256 + 256]
         own = jnp.concatenate([own, jnp.zeros((5, 256), F32)], axis=0).T
         for axis in range(3):
-            wide_ref[axis] = jnp.broadcast_to(own[:, axis : axis + 1], (256, 128))
-
-        def slot_step(slot, total):
-            row, gap, here, source = locate(list_ref[leaf, slot], cols)
-
-            def fetch(place):
-                beside = jnp.where(here, first_ref[row, place], first_mate_ref[row, place])
-                return jnp.where(gap == 0, own_ref[row, place], beside).astype(F32)
-
-            sides = fetch(source)
-            parts = fetch(4 + source)
-            last = fetch(8)[:8]
-            tiles = []
-            for half in range(2):
-                part = parts[half * 8 : half * 8 + 8]
-                tail = jnp.sum(
-                    jnp.where(row_ids == source * 2 + half, last, 0.0), axis=0, keepdims=True
-                )
-                first = wide_ref[0] - (part[0:1] + part[3:4] + part[6:7])
-                second = wide_ref[1] - (part[1:2] + part[4:5] + part[7:8])
-                third = wide_ref[2] - (part[2:3] + part[5:6] + tail)
-                dist_sq = first * first + second * second + third * third
-                tiles.append(lax.rsqrt(dist_sq * scale + floor).astype(BF16))
-            tile = jnp.concatenate(tiles, axis=1)
-            sides = jnp.concatenate([sides[:8], sides[8:]], axis=1).astype(BF16)
-            return total + lax.dot_general(tile, sides, NT, preferred_element_type=F32)
-
-        total = lax.fori_loop(0, count_ref[leaf], slot_step, jnp.zeros((256, 8), F32))
-        near_ref[:, leaf * 256 : leaf * 256 + 256] = total.T
+            wide = jnp.broadcast_to(own[:, axis : axis + 1], (256, 128))
+            wide_ref[leaf, axis] = wide.reshape(32, 8, 128)
+
+    def leaf_step(leaf, carry):
+        total = jnp.zeros((8, 256), F32)
+        for slot in range(8):
+            sides, halves = source_of(leaf, slot)
+            bands = []
+            for band in range(0, 32, 8):
+                tiles = []
+                target = [wide_ref[leaf, axis, band : band + 8] for axis in range(3)]
+                for place in halves:
+                    first = target[0] - place[0]
+                    second = target[1] - place[1]
+                    third = target[2] - place[2]
+                    dist_sq = first * first + second * second + third * third
+                    inverse = lax.rsqrt(dist_sq * scale + floor)
+                    tiles.append(inverse.reshape(64, 128).astype(BF16))
+                bands.append(jnp.concatenate(tiles, axis=1))
+            tile = jnp.concatenate(bands, axis=0)
+            total += lax.dot_general(sides, tile, NT, preferred_element_type=F32)
+        near_ref[leaf] = total
+        return carry
+
+    lax.fori_loop(0, 4, leaf_step, 0, unroll=4)
 
 
 def couple(matrices, sources):
@@ -143,13 +170,12 @@
     my_core = lax.axis_index("core")
     for slot in range(16):
         device = owner_ref[coarse_list_ref[0, slot]]
-        row = device // cols
-        col = device - row * cols
-        col = col - lax.rem(col, zs) + lax.rem(col + zs // 2, zs)
-        tile_id = (row // 2) * (cols // 4) + col // 4
-        mine = lax.rem(row, 2) == my_core
+        row = lax.shift_right_logical(device, cols.bit_length() - 1)
+        col = (device & (cols - 1)) ^ (zs // 2)
+        tile_id = (row >> 1) * (cols // 4) + (col >> 2)
+        mine = (row & 1) == my_core
         tile = jnp.where(mine, last_ref[tile_id], last_mate_ref[tile_id]).astype(F32)
-        place = lax.rem(col, 4)
+        place = col & 3
         picked = tile[0:4]
         for step in range(1, 4):
             picked = jnp.where(place == step, tile[step * 4 : step * 4 + 4], picked)
@@ -168,7 +194,7 @@
             tile = jnp.where(far == 0, own_ref[row, 9], jnp.where(far == 1, one, more))
             tile = tile.astype(F32)
             half = jnp.where(source >= 2, tile[8:], tile[:8])
-            half = jnp.where(lax.rem(source, 2) == 1, half[:, 64:], half[:, :64])
+            half = jnp.where(source & 1 == 1, half[:, 64:], half[:, :64])
             live = slot < coupling_count_ref[leaf]
             source_ref[slot * 8 : slot * 8 + 8, :] = jnp.where(live, half, 0.0)
         local = couple(leaf_coupling_ref[leaf], source_ref[...])
@@ -181,7 +207,39 @@
         local = local.T[:8].astype(BF16)
         far_part = lax.dot_general(local, basis_ref[leaf], NN, preferred_element_type=F32)
         span = slice(leaf * 256, leaf * 256 + 256)
-        out_ref[:, span] = (near_ref[:, span] + far_part).astype(BF16)
+        out_ref[:, span] = (near_ref[leaf] + far_part).astype(BF16)
+
+
+VMEM = pl.BlockSpec(memory_space=pltpu.VMEM)
+SMEM = pl.BlockSpec(memory_space=pltpu.SMEM)
+PARAMS = pltpu.CompilerParams(vmem_limit_bytes=16 * 2**20)
+
+
+def near_call(cols, *operands):
+    return pl.pallas_call(
+        functools.partial(near_kernel, cols),
+        out_shape=jax.ShapeDtypeStruct((4, 8, 256), F32),
+        in_specs=[SMEM] * 2 + [VMEM] * 4,
+        out_specs=VMEM,
+        scratch_shapes=[pltpu.VMEM((4, 3, 32, 8, 128), F32)],
+        compiler_params=PARAMS,
+        name="near",
+        cost_estimate=pl.CostEstimate(
+            flops=4_000_000_000, bytes_accessed=1_200_000, transcendentals=0
+        ),
+    )(*operands)
+
+
+def far_call(groups, cols, zs, *operands):
+    return pl.pallas_call(
+        functools.partial(far_kernel, groups, cols, zs),
+        out_shape=jax.ShapeDtypeStruct((8, 1024), BF16),
+        in_specs=[SMEM] * 5 + [VMEM] * 10,
+        out_specs=VMEM,
+        scratch_shapes=[pltpu.VMEM((128, 64), F32)],
+        compiler_params=PARAMS,
+        name="far",
+    )(*operands)
 
 
 def per_device(
@@ -204,22 +262,21 @@
 ):
     rows = 2 * xs
     cols = ys * zs
-    vmem = pl.BlockSpec(memory_space=pltpu.VMEM)
-    smem = pl.BlockSpec(memory_space=pltpu.SMEM)
     row_axes = ("x", "core")
     swap = [(0, 1), (1, 0)]
     groups = xs * cols // 4
     turned = [(place + zs // 2) % zs for place in range(zs)]
     basis = jnp.swapaxes(basis, 1, 2)
 
-    block, cluster = pl.pallas_call(
+    own, cluster = pl.pallas_call(
         pack_kernel,
         out_shape=(
-            jax.ShapeDtypeStruct((BLOCK, 16, 128), BF16),
+            jax.ShapeDtypeStruct((rows, BLOCK, 16, 128), BF16),
             jax.ShapeDtypeStruct((zs, 4, 128), BF16),
         ),
-        in_specs=[vmem] * 4,
-        out_specs=(vmem, vmem),
+        in_specs=[VMEM] * 4,
+        out_specs=(VMEM, VMEM),
+        compiler_params=PARAMS,
         name="pack",
     )(rhs, points, basis, transfer)
 
@@ -232,7 +289,6 @@
                     pairs.append((core * cols + source, core * cols + col))
         return pairs
 
-    own = jnp.broadcast_to(block[None], (rows,) + block.shape)
     own = lax.all_to_all(own, row_axes, 0, 0, tiled=True)
     first = lax.ppermute(own, ("core", "y", "z"), beside(1))
     own, cluster = lax.optimization_barrier((own, cluster))
@@ -246,30 +302,15 @@
     line = jnp.broadcast_to(line[None], (xs * ys,) + line.shape)
     same = lax.all_to_all(line, ("x", "y"), 0, 0, tiled=True).reshape(groups, 16, 128)
 
-    near = pl.pallas_call(
-        functools.partial(near_kernel, cols),
-        out_shape=jax.ShapeDtypeStruct((8, 1024), F32),
-        in_specs=[smem] * 2 + [vmem] * 4,
-        out_specs=vmem,
-        scratch_shapes=[pltpu.VMEM((3, 256, 128), F32)],
-        name="near",
-        cost_estimate=pl.CostEstimate(
-            flops=4_000_000_000, bytes_accessed=1_200_000, transcendentals=0
-        ),
-    )(near_list, near_count, points, own, first, first_mate)
-
+    near = near_call(cols, near_list, near_count, points, own, first, first_mate)
     same, second, near = lax.optimization_barrier((same, second, near))
     last = jnp.concatenate([same, second.reshape(rows * 2, 16, 128)], axis=0)
     last_mate = lax.ppermute(last, "core", swap)
 
-    return pl.pallas_call(
-        functools.partial(far_kernel, groups, cols, zs),
-        out_shape=jax.ShapeDtypeStruct((8, 1024), BF16),
-        in_specs=[smem] * 5 + [vmem] * 10,
-        out_specs=vmem,
-        scratch_shapes=[pltpu.VMEM((128, 64), F32)],
-        name="far",
-    )(
+    return far_call(
+        groups,
+        cols,
+        zs,
         coupling_list,
         coupling_count,
         coarse_list,

time: 94 us -> 90.4 us (0.962)
  Pallas kernels: 16.9 us -> 8.73 us
  starting transfers between devices: 18.3 us -> 21.2 us
  waiting for transfers between devices: 1.33 us -> 2.74 us
    pallas_call x3, Pallas kernels: 16.9 us -> 8.73 us  [the longest x1 4.28 us: near_call(): pl.pallas_call(functools.partial(near_kernel, cols), out_shape=jax.ShapeD...]
    ppermute x1, starting transfers between devices: 1.92 us -> 4.78 us  [per_device(): last_mate = lax.ppermute(last, 'core', swap)]
    all_to_all x1, waiting for transfers between devices: 0.01 us -> 1.77 us  [per_device(): lax.all_to_all(line, ('x', 'y'), 0, 0, tiled=True).reshape(groups, 16, 128)]
    unnamed x12 -> x30, local copies, waits for them, and re-layouts: 1.59 us -> 3.24 us
  transfers between devices with their start and end apart: 5 -> 5, of which waited for: 1 -> 2; matrix products, arithmetic and copies ran while one was open for 1% -> 1% of each run, Pallas kernels for 10% -> 5%
where the time goes in v4:
time: 90.4 us; the launch traced here: 89.8 us
  blocking collectives  52.1 us (58%)
  starting transfers between devices  21.2 us (23%)
  Pallas kernels  8.73 us (10%)
  local copies, waits for them, and re-layouts  4.15 us (5%)
  waiting for transfers between devices  2.74 us (3%)
    all_to_all x1, blocking collectives, per_device(): lax.all_to_all(cluster, 'z', 0, 0, tiled=True, axis_index_groups=[turned])  28.1 us
    all_to_all x1, blocking collectives, per_device(): own = lax.all_to_all(own, row_axes, 0, 0, tiled=True)  24 us
    all_to_all x1, starting transfers between devices, per_device(): lax.all_to_all(line, ('x', 'y'), 0, 0, tiled=True).reshape(groups, 16, 128)  6.54 us
    ppermute x1, starting transfers between devices, per_device(): last_mate = lax.ppermute(last, 'core', swap)  4.78 us
    ppermute x1, starting transfers between devices, per_device(): first_mate = lax.ppermute(first, 'core', swap)  4.5 us
    pallas_call x1, Pallas kernels, near_call(): pl.pallas_call(functools.partial(near_kernel, cols), out_shape=jax.ShapeD...  4.28 us
    pallas_call x1, Pallas kernels, far_call(): pl.pallas_call(functools.partial(far_kernel, groups, cols, zs), out_shape...  4.1 us
    ppermute x1, starting transfers between devices, per_device(): second = lax.ppermute(coeffs, ('core', 'y', 'z'), beside(2))  4.03 us
  transfers between devices with their start and end apart: 5, of which 2 were waited for; matrix products, arithmetic and copies ran while one was open for 1% of the time, Pallas kernels for 5%

profile of v4, /device:TPU:1, one launch (start us, length us, event | category | flops | bytes accessed | tf_op | source)
XLA Modules:
  0.0 89.8 jit_solution(3610507974076089525)
XLA Ops:
  0.0 0.0 copy-start.1
  0.0 0.9 %copy-done.1 = bf16[4,256,64]{1,2,0:T(8,128)(2,1)S(1)} copy-done((bf16[4,256,64]{1,2,0:T(8,128)(2,1)S(1)}, bf16[4,256,64]{1,2,0:T(8,128)(2,1)}, u32[]{:S(2)}) %copy-start.1) | copy-done | bytes 131096
  0.9 0.0 copy-start.3
  0.9 0.8 copy-done.3
  1.7 0.0 copy-start.6
  1.7 0.7 copy-done.6
  2.5 0.0 copy-start.7
  2.5 0.7 copy-done.7
  3.2 0.4 pack.1
  3.5 24.0 %all_to_all.15.own_ref = bf16[8,10,16,128]{3,2,1,0:T(8,128)(2,1)S(1)} all-to-all(bf16[8,10,16,128]{3,2,1,0:T(8,128)(2,1)S(1)} %get-tuple-element.14), channel_id=1, replica_groups=mesh['x'=4,'core'=2,'y'=4,'z'=32] {'x','core'}, dimensions={0} | all-to-all | bytes 655360 | tf_op jit(solution)/shard_map/all_to_all | solution.py:292
  27.6 1.3 %collective-permute-start = (bf16[8,10,16,128]{3,2,1,0:T(8,128)(2,1)S(1)}, bf16[8,10,16,128]{3,2,1,0:T(8,128)(2,1)S(1)}, u32[]{:S(2)}, u32[]{:S(2)}) collective-permute-start(bf16[8,10,16,128]{3,2,1,0:T(8,128)(2,1)S(1)} %all_to_all.15.own_ref), channel_id=1, source_target_pairs={{1,0},{2,1},{3,2},{4,3},{5,4},{6,5},{7,6},{8,7},{9,8},{10,9},{11,1... | collective-permute-start | bytes 983048 | tf_op jit(solution)/shard_map/ppermute | solution.py:293
  28.9 28.1 %all_to_all.16 = bf16[32,4,128]{2,1,0:T(4,128)(2,1)S(1)} all-to-all(bf16[32,4,128]{2,1,0:T(4,128)(2,1)S(1)} %get-tuple-element.17), channel_id=1, replica_groups={{16,17,18,19,20,21,22,23,24,25,26,27,28,29,30,31,0,1,2,3,4,5,6,7,8,9,10..., dimensions={0} | all-to-all | bytes 65536 | tf_op jit(solution)/shard_map/all_to_all | solution.py:295
  56.9 0.0 collective-permute-done.first_ref
  57.0 4.5 %collective-permute-start.1 = (bf16[8,10,16,128]{3,2,1,0:T(8,128)(2,1)S(1)}, bf16[8,10,16,128]{3,2,1,0:T(8,128)(2,1)S(1)}, u32[]{:S(2)}, u32[]{:S(2)}) collective-permute-start(bf16[8,10,16,128]{3,2,1,0:T(8,128)(2,1)S(1)} %collective-permute-done.first_ref), channel_id=1, source_target_pairs={{0,128},{128,0},{1,129},{129,1},{2,130},{130,2},{3,131},{131,3},{4... | collective-permute-start | bytes 983048 | tf_op jit(solution)/shard_map/ppermute | solution.py:299
  61.5 0.9 %broadcast_in_dim.2 = bf16[16,8,16,128]{3,2,1,0:T(8,128)(2,1)} broadcast(bf16[8,16,128]{2,1,0:T(8,128)(2,1)S(1)} %bitcast.7), dimensions={1,2,3} | broadcast | bytes 557056 | tf_op jit(solution)/shard_map/broadcast_in_dim | solution.py:302
  62.4 6.5 %all-to-all-start.2 = ((bf16[16,8,16,128]{3,2,1,0:T(8,128)(2,1)}), bf16[16,8,16,128]{3,2,1,0:T(8,128)(2,1)S(1)}, u32[]{:S(2)}, u32[]{:S(2)}) async-start(bf16[16,8,16,128]{3,2,1,0:T(8,128)(2,1)} %broadcast_in_dim.2), calls=%async_computation.2 | async-start | bytes 1048576 | tf_op jit(solution)/shard_map/all_to_all | solution.py:303
  68.9 0.0 copy-start.8
  69.0 0.0 copy-start.13
  69.0 0.0 copy-start.14
  69.0 4.0 %collective-permute-start.2 = (bf16[8,2,16,128]{3,2,1,0:T(8,128)(2,1)S(1)}, bf16[8,2,16,128]{3,2,1,0:T(8,128)(2,1)S(1)}, u32[]{:S(2)}, u32[]{:S(2)}) collective-permute-start(bf16[8,2,16,128]{3,2,1,0:T(8,128)(2,1)S(1)} %pad_maximum_fusion.1), channel_id=1, source_target_pairs={{2,0},{3,1},{4,2},{5,3},{6,4},{7,5},{8,6},{9,7},{10,8},{11,9},{12,... | collective-permute-start | bytes 196616 | tf_op jit(solution)/shard_map/ppermute | solution.py:301
  73.0 0.0 collective-permute-done.1.first_mate_ref
  73.0 0.0 copy-done.8
  73.1 0.0 copy-done.13
  73.1 0.0 copy-done.14
  73.1 0.0 copy-start.4
  73.1 0.0 copy-start.5
  73.1 0.0 copy-start.10
  73.1 4.3 %near.1.near_ref = f32[4,8,256]{2,1,0:T(8,128)S(1)} custom-call(s32[4,8]{1,0:T(4,128)S(1)} %copy-done.13, s32[4]{0:T(128)S(1)} %copy-done.14, f32[3,1024]{1,0:T(4,128)S(1)} %copy-done.8, bf16[8,10,16,128]{3,2,1,0:T(8,128)(2,1)S(1)} %all_to_all.15.own_ref, bf16[8,10,16,128]{3,2,1,0:T(8,128)(2,1)S(1)} %collective-permute-done.first_ref, ...), custom_call_target="tpu_custom_call" | custom-call | flops 4000000000 | bytes 1200000 | tf_op jit(solution)/shard_map/near/pallas_call | solution.py:219
  77.4 0.0 copy-start
  77.4 0.0 collective-permute-done.2
  77.4 1.8 %all-to-all-done.2 = bf16[16,8,16,128]{3,2,1,0:T(8,128)(2,1)S(1)} async-done(((bf16[16,8,16,128]{3,2,1,0:T(8,128)(2,1)}), bf16[16,8,16,128]{3,2,1,0:T(8,128)(2,1)S(1)}, u32[]{:S(2)}, u32[]{:S(2)}) %all-to-all-start.2) | async-done | bytes 524320 | tf_op jit(solution)/shard_map/all_to_all | solution.py:303
  79.2 0.0 copy-start.2
  79.2 0.0 copy-start.9
  79.2 0.1 pad_maximum_fusion.last_ref
  79.2 0.0 copy-start.11
  79.2 0.0 copy-start.12
  79.3 4.8 %collective-permute-start.3 = (bf16[144,16,128]{2,1,0:T(8,128)(2,1)S(1)}, bf16[144,16,128]{2,1,0:T(8,128)(2,1)S(1)}, u32[]{:S(2)}, u32[]{:S(2)}) collective-permute-start(bf16[144,16,128]{2,1,0:T(8,128)(2,1)S(1)} %pad_maximum_fusion.last_ref), channel_id=1, source_target_pairs={{0,128},{128,0},{1,129},{129,1},{2,130},{130,2},{3,131},{131,3},{4... | collective-permute-start | bytes 1769480 | tf_op jit(solution)/shard_map/ppermute | solution.py:308
  84.7 1.0 %collective-permute-done.3.last_mate_ref = bf16[144,16,128]{2,1,0:T(8,128)(2,1)S(1)} collective-permute-done((bf16[144,16,128]{2,1,0:T(8,128)(2,1)S(1)}, bf16[144,16,128]{2,1,0:T(8,128)(2,1)S(1)}, u32[]{:S(2)}, u32[]{:S(2)}) %collective-permute-start.3) | collective-permute-done | bytes 589856 | tf_op jit(solution)/shard_map/ppermute | solution.py:308
  85.7 0.0 copy-done.4
  85.7 0.0 copy-done.5
  85.7 0.0 copy-done.10
  85.7 0.0 copy-done
  85.7 0.0 copy-done.2
  85.7 0.0 copy-done.9
  85.7 0.0 copy-done.11
  85.7 0.0 copy-done.12
  85.7 4.1 %far.1 = bf16[8,1024]{1,0:T(8,128)(2,1)} custom-call(s32[4,16]{1,0:T(4,128)S(1)} %copy-done.10, s32[4]{0:T(128)S(1)} %copy-done.11, s32[1,16]{1,0:T(1,128)S(1)} %copy-done.12, s32[1]{0:T(128)S(6)} %copy.14.coarse_count_ref, s32[1024]{0:T(1024)S(1)} %copy-done.9, bf16[8,10,16,128]{3,2,1,0:T(8,128)(2,1)S(1)} %all_to_all.15.own_ref, ...), custom_call_target="tpu_custom_call" | custom-call | tf_op jit(solution)/shard_map/far/pallas_call | solution.py:234
  (3 shorter events, 0.0 us)
Async XLA Ops:
  0.0 0.9 %copy-start.1 = (bf16[4,256,64]{1,2,0:T(8,128)(2,1)S(1)}, bf16[4,256,64]{1,2,0:T(8,128)(2,1)}, u32[]{:S(2)}) copy-start(bf16[4,256,64]{1,2,0:T(8,128)(2,1)} %param.15) | copy-start | bytes 393220
  0.9 0.8 copy-start.3
  1.7 0.7 copy-start.6
  2.5 0.7 copy-start.7
  27.6 29.4 %collective-permute-start = (bf16[8,10,16,128]{3,2,1,0:T(8,128)(2,1)S(1)}, bf16[8,10,16,128]{3,2,1,0:T(8,128)(2,1)S(1)}, u32[]{:S(2)}, u32[]{:S(2)}) collective-permute-start(bf16[8,10,16,128]{3,2,1,0:T(8,128)(2,1)S(1)} %all_to_all.15.own_ref), channel_id=1, source_target_pairs={{1,0},{2,1},{3,2},{4,3},{5,4},{6,5},{7,6},{8,7},{9,8},{10,9},{11,1... | collective-permute-start | bytes 983048 | tf_op jit(solution)/shard_map/ppermute | solution.py:293
  57.0 16.1 %collective-permute-start.1 = (bf16[8,10,16,128]{3,2,1,0:T(8,128)(2,1)S(1)}, bf16[8,10,16,128]{3,2,1,0:T(8,128)(2,1)S(1)}, u32[]{:S(2)}, u32[]{:S(2)}) collective-permute-start(bf16[8,10,16,128]{3,2,1,0:T(8,128)(2,1)S(1)} %collective-permute-done.first_ref), channel_id=1, source_target_pairs={{0,128},{128,0},{1,129},{129,1},{2,130},{130,2},{3,131},{131,3},{4... | collective-permute-start | bytes 983048 | tf_op jit(solution)/shard_map/ppermute | solution.py:299
  62.4 16.8 %all-to-all-start.2 = ((bf16[16,8,16,128]{3,2,1,0:T(8,128)(2,1)}), bf16[16,8,16,128]{3,2,1,0:T(8,128)(2,1)S(1)}, u32[]{:S(2)}, u32[]{:S(2)}) async-start(bf16[16,8,16,128]{3,2,1,0:T(8,128)(2,1)} %broadcast_in_dim.2), calls=%async_computation.2 | async-start | bytes 1048576 | tf_op jit(solution)/shard_map/all_to_all | solution.py:303
  68.9 4.1 %copy-start.8 = (f32[3,1024]{1,0:T(4,128)S(1)}, f32[3,1024]{1,0:T(4,128)}, u32[]{:S(2)}) copy-start(f32[3,1024]{1,0:T(4,128)} %points_ref.3) | copy-start | bytes 36868
  69.0 4.1 %copy-start.13 = (s32[4,8]{1,0:T(4,128)S(1)}, s32[4,8]{1,0:T(4,128)}, u32[]{:S(2)}) copy-start(s32[4,8]{1,0:T(4,128)} %list_ref.1) | copy-start | bytes 388
  69.0 4.1 %copy-start.14 = (s32[4]{0:T(128)S(1)}, s32[4]{0:T(128)}, u32[]{:S(2)}) copy-start(s32[4]{0:T(128)} %count_ref.1) | copy-start | bytes 52
  69.0 8.4 %collective-permute-start.2 = (bf16[8,2,16,128]{3,2,1,0:T(8,128)(2,1)S(1)}, bf16[8,2,16,128]{3,2,1,0:T(8,128)(2,1)S(1)}, u32[]{:S(2)}, u32[]{:S(2)}) collective-permute-start(bf16[8,2,16,128]{3,2,1,0:T(8,128)(2,1)S(1)} %pad_maximum_fusion.1), channel_id=1, source_target_pairs={{2,0},{3,1},{4,2},{5,3},{6,4},{7,5},{8,6},{9,7},{10,8},{11,9},{12,... | collective-permute-start | bytes 196616 | tf_op jit(solution)/shard_map/ppermute | solution.py:301
  73.1 12.6 %copy-start.4 = (bf16[4,64,64]{2,1,0:T(8,128)(2,1)S(1)}, bf16[4,64,64]{2,1,0:T(8,128)(2,1)}, u32[]{:S(2)}) copy-start(bf16[4,64,64]{2,1,0:T(8,128)(2,1)} %transfer_ref.3) | copy-start | bytes 98308
  73.1 12.6 %copy-start.5 = (bf16[1,16,64,64]{3,2,1,0:T(8,128)(2,1)S(1)}, bf16[1,16,64,64]{3,2,1,0:T(8,128)(2,1)}, u32[]{:S(2)}) copy-start(bf16[1,16,64,64]{3,2,1,0:T(8,128)(2,1)} %coarse_coupling_ref.1) | copy-start | bytes 393220
  73.1 12.6 %copy-start.10 = (s32[4,16]{1,0:T(4,128)S(1)}, s32[4,16]{1,0:T(4,128)}, u32[]{:S(2)}) copy-start(s32[4,16]{1,0:T(4,128)} %coupling_list_ref.1) | copy-start | bytes 772
  77.4 8.3 %copy-start = (bf16[4,16,64,64]{3,2,1,0:T(8,128)(2,1)S(1)}, bf16[4,16,64,64]{3,2,1,0:T(8,128)(2,1)}, u32[]{:S(2)}) copy-start(bf16[4,16,64,64]{3,2,1,0:T(8,128)(2,1)} %leaf_coupling_ref.1) | copy-start | bytes 1572868
  79.2 6.5 %copy-start.2 = (bf16[4,256,64]{1,2,0:T(8,128)(2,1)S(1)}, bf16[4,256,64]{1,2,0:T(8,128)(2,1)}, u32[]{:S(2)}) copy-start(bf16[4,256,64]{1,2,0:T(8,128)(2,1)} %param.15) | copy-start | bytes 393220
  79.2 6.5 %copy-start.9 = (s32[1024]{0:T(1024)S(1)}, s32[1024]{0:T(1024)}, u32[]{:S(2)}) copy-start(s32[1024]{0:T(1024)} %owner_ref.1) | copy-start | bytes 12292
  79.2 6.5 %copy-start.11 = (s32[4]{0:T(128)S(1)}, s32[4]{0:T(128)}, u32[]{:S(2)}) copy-start(s32[4]{0:T(128)} %coupling_count_ref.1) | copy-start | bytes 52
  79.2 6.5 %copy-start.12 = (s32[1,16]{1,0:T(1,128)S(1)}, s32[1,16]{1,0:T(1,128)}, u32[]{:S(2)}) copy-start(s32[1,16]{1,0:T(1,128)} %coarse_list_ref.1) | copy-start | bytes 196
  79.3 6.4 %collective-permute-start.3 = (bf16[144,16,128]{2,1,0:T(8,128)(2,1)S(1)}, bf16[144,16,128]{2,1,0:T(8,128)(2,1)S(1)}, u32[]{:S(2)}, u32[]{:S(2)}) collective-permute-start(bf16[144,16,128]{2,1,0:T(8,128)(2,1)S(1)} %pad_maximum_fusion.last_ref), channel_id=1, source_target_pairs={{0,128},{128,0},{1,129},{129,1},{2,130},{130,2},{3,131},{131,3},{4... | collective-permute-start | bytes 1769480 | tf_op jit(solution)/shard_map/ppermute | solution.py:308

commit v5 on v4

--- a/solution.py
+++ b/solution.py
@@ -17,7 +17,35 @@
 BLOCK = 10
 
 
-def pack_kernel(rhs_ref, points_ref, basis_ref, transfer_ref, copies_ref, cluster_ref):
+def fetch_all(sources, targets, done_ref):
+    copies = [
+        pltpu.make_async_copy(source, target, done_ref.at[place])
+        for place, (source, target) in enumerate(zip(sources, targets))
+    ]
+    for copy in copies:
+        copy.start()
+    for copy in copies:
+        copy.wait()
+
+
+def pack_kernel(
+    rhs_hbm,
+    points_hbm,
+    basis_hbm,
+    transfer_hbm,
+    copies_ref,
+    cluster_ref,
+    rhs_ref,
+    points_ref,
+    basis_ref,
+    transfer_ref,
+    done_ref,
+):
+    fetch_all(
+        (rhs_hbm, points_hbm, basis_hbm, transfer_hbm),
+        (rhs_ref, points_ref, basis_ref, transfer_ref),
+        done_ref,
+    )
     block_ref = copies_ref.at[0]
     points = points_ref[...]
     part_hi = points.astype(BF16).astype(F32)
@@ -137,9 +165,13 @@
         matrices.reshape(slots * 64, 64), sources.astype(BF16), NT, preferred_element_type=F32
     )
     group = lax.broadcasted_iota(jnp.int32, (64, 128), 1) // 8
-    total = jnp.zeros((64, 128), F32)
-    for slot in range(slots):
+    total = products[:64]
+    for slot in range(1, slots):
         total = jnp.where(group == slot, products[slot * 64 : slot * 64 + 64], total)
+    return total
+
+
+def sum_groups(total):
     for shift in (64, 32, 16, 8):
         total = total + pltpu.roll(total, shift, 1)
     return total
@@ -171,19 +203,21 @@
     for slot in range(16):
         device = owner_ref[coarse_list_ref[0, slot]]
         row = lax.shift_right_logical(device, cols.bit_length() - 1)
-        col = (device & (cols - 1)) ^ (zs // 2)
-        tile_id = (row >> 1) * (cols // 4) + (col >> 2)
+        col = device & (cols - 1)
+        z = col & (zs - 1)
+        order = jnp.where(z < zs // 2, z * 2, (zs - z) * 2 + 1)
+        order = jnp.where(z == 0, 1, jnp.where(z == zs // 2, 0, order))
+        tile_id = (row >> 1) * (cols // 4) + ((col - z + order) >> 2)
         mine = (row & 1) == my_core
         tile = jnp.where(mine, last_ref[tile_id], last_mate_ref[tile_id]).astype(F32)
-        place = col & 3
+        place = order & 3
         picked = tile[0:4]
         for step in range(1, 4):
             picked = jnp.where(place == step, tile[step * 4 : step * 4 + 4], picked)
         picked = jnp.where(slot < coarse_count_ref[0], picked, 0.0)
-        source_ref[slot * 8 : slot * 8 + 8, :] = jnp.concatenate(
+        source_ref[4, slot * 8 : slot * 8 + 8, :] = jnp.concatenate(
             [picked[:, :64], picked[:, 64:]], axis=0
         )
-    coarse_field = couple(coarse_coupling_ref[0], source_ref[...])
     for leaf in range(4):
         for slot in range(16):
             row, gap, here, source = locate(coupling_list_ref[leaf, slot], cols)
@@ -196,21 +230,27 @@
             half = jnp.where(source >= 2, tile[8:], tile[:8])
             half = jnp.where(source & 1 == 1, half[:, 64:], half[:, :64])
             live = slot < coupling_count_ref[leaf]
-            source_ref[slot * 8 : slot * 8 + 8, :] = jnp.where(live, half, 0.0)
-        local = couple(leaf_coupling_ref[leaf], source_ref[...])
-        local = local + jnp.dot(
-            transfer_ref[leaf].astype(F32),
-            coarse_field,
-            precision=lax.Precision.HIGHEST,
-            preferred_element_type=F32,
-        )
-        local = local.T[:8].astype(BF16)
-        far_part = lax.dot_general(local, basis_ref[leaf], NN, preferred_element_type=F32)
+            source_ref[leaf, slot * 8 : slot * 8 + 8, :] = jnp.where(live, half, 0.0)
+    totals = [couple(leaf_coupling_ref[leaf], source_ref[leaf]) for leaf in range(4)]
+    coarse_field = sum_groups(couple(coarse_coupling_ref[0], source_ref[4]))
+    field_hi = coarse_field.astype(BF16).astype(F32)
+    rest = coarse_field - field_hi
+    field_mid = rest.astype(BF16).astype(F32)
+    group = lax.broadcasted_iota(jnp.int32, (64, 128), 1) // 8
+    parts = jnp.where(group == 2, rest - field_mid, 0.0)
+    parts = jnp.where(group == 1, field_mid, jnp.where(group == 0, field_hi, parts)).astype(BF16)
+    for leaf in range(4):
+        totals[leaf] += jnp.dot(transfer_ref[leaf], parts, preferred_element_type=F32)
+    local = sum_groups(jnp.concatenate(totals, axis=0)).T[:8]
+    for leaf in range(4):
+        mine = local[:, leaf * 64 : leaf * 64 + 64].astype(BF16)
+        far_part = lax.dot_general(mine, basis_ref[leaf], NN, preferred_element_type=F32)
         span = slice(leaf * 256, leaf * 256 + 256)
         out_ref[:, span] = (near_ref[leaf] + far_part).astype(BF16)
 
 
 VMEM = pl.BlockSpec(memory_space=pltpu.VMEM)
+ANY = pl.BlockSpec(memory_space=pl.ANY)
 SMEM = pl.BlockSpec(memory_space=pltpu.SMEM)
 PARAMS = pltpu.CompilerParams(vmem_limit_bytes=16 * 2**20)
 
@@ -236,7 +276,7 @@
         out_shape=jax.ShapeDtypeStruct((8, 1024), BF16),
         in_specs=[SMEM] * 5 + [VMEM] * 10,
         out_specs=VMEM,
-        scratch_shapes=[pltpu.VMEM((128, 64), F32)],
+        scratch_shapes=[pltpu.VMEM((5, 128, 64), F32)],
         compiler_params=PARAMS,
         name="far",
     )(*operands)
@@ -265,7 +305,8 @@
     row_axes = ("x", "core")
     swap = [(0, 1), (1, 0)]
     groups = xs * cols // 4
-    turned = [(place + zs // 2) % zs for place in range(zs)]
+    half = zs // 2
+    turned = [half, 0] + [z for near in range(1, half) for z in (near, zs - near)]
     basis = jnp.swapaxes(basis, 1, 2)
 
     own, cluster = pl.pallas_call(
@@ -274,9 +315,15 @@
             jax.ShapeDtypeStruct((rows, BLOCK, 16, 128), BF16),
             jax.ShapeDtypeStruct((zs, 4, 128), BF16),
         ),
-        in_specs=[VMEM] * 4,
+        in_specs=[ANY] * 4,
         out_specs=(VMEM, VMEM),
-        compiler_params=PARAMS,
+        scratch_shapes=[
+            pltpu.VMEM(rhs.shape, BF16),
+            pltpu.VMEM(points.shape, F32),
+            pltpu.VMEM(basis.shape, BF16),
+            pltpu.VMEM(transfer.shape, BF16),
+            pltpu.SemaphoreType.DMA((4,)),
+        ],
         name="pack",
     )(rhs, points, basis, transfer)
 

time: 90.4 us -> 88.3 us (0.977)
  local copies, waits for them, and re-layouts: 4.15 us -> 0.98 us
  Pallas kernels: 8.73 us -> 9.64 us
    unnamed x30 -> x24, local copies, waits for them, and re-layouts: 3.24 us -> 0.07 us
    pallas_call x1, Pallas kernels: 0.36 us -> 1.98 us  [per_device(): pl.pallas_call(pack_kernel, out_shape=(jax.ShapeDtypeStruct((rows, BLOCK,...]
    all_to_all x1, blocking collectives: 24 us -> 25 us  [per_device(): own = lax.all_to_all(own, row_axes, 0, 0, tiled=True)]
where the time goes in v5:
time: 88.3 us; the launch traced here: 87.8 us
  blocking collectives  52.3 us (59%)
  starting transfers between devices  21.2 us (24%)
  Pallas kernels  9.64 us (11%)
  waiting for transfers between devices  2.71 us (3%)
  local copies, waits for them, and re-layouts  0.98 us (1%)
    all_to_all x1, blocking collectives, per_device(): lax.all_to_all(cluster, 'z', 0, 0, tiled=True, axis_index_groups=[turned])  27.3 us
    all_to_all x1, blocking collectives, per_device(): own = lax.all_to_all(own, row_axes, 0, 0, tiled=True)  25 us
    all_to_all x1, starting transfers between devices, per_device(): lax.all_to_all(line, ('x', 'y'), 0, 0, tiled=True).reshape(groups, 16, 128)  6.6 us
    ppermute x1, starting transfers between devices, per_device(): last_mate = lax.ppermute(last, 'core', swap)  4.83 us
    ppermute x1, starting transfers between devices, per_device(): first_mate = lax.ppermute(first, 'core', swap)  4.45 us
    pallas_call x1, Pallas kernels, near_call(): pl.pallas_call(functools.partial(near_kernel, cols), out_shape=jax.ShapeD...  4.27 us
    ppermute x1, starting transfers between devices, per_device(): second = lax.ppermute(coeffs, ('core', 'y', 'z'), beside(2))  4.04 us
    pallas_call x1, Pallas kernels, far_call(): pl.pallas_call(functools.partial(far_kernel, groups, cols, zs), out_shape...  3.39 us
  transfers between devices with their start and end apart: 5, of which 2 were waited for; matrix products, arithmetic and copies ran while one was open for 1% of the time, Pallas kernels for 5%

profile of v5, /device:TPU:1, one launch (start us, length us, event | category | flops | bytes accessed | tf_op | source)
XLA Modules:
  0.0 87.8 jit_solution(14614710246367259662)
XLA Ops:
  0.0 2.0 %pack.1 = (bf16[8,10,16,128]{3,2,1,0:T(8,128)(2,1)}, bf16[32,4,128]{2,1,0:T(4,128)(2,1)}) custom-call(bf16[8,1024]{1,0:T(8,128)(2,1)} %rhs_hbm.1, f32[3,1024]{1,0:T(4,128)} %points_ref.1, bf16[4,64,256]{2,1,0:T(8,128)(2,1)} %bitcast.4, bf16[4,64,64]{2,1,0:T(8,128)(2,1)} %transfer_ref.1), custom_call_target="tpu_custom_call" | custom-call | tf_op jit(solution)/shard_map/pack/pallas_call | solution.py:312
  2.0 0.0 copy-start.11
  2.0 25.0 %all_to_all.15.own_ref = bf16[8,10,16,128]{3,2,1,0:T(8,128)(2,1)S(1)} all-to-all(bf16[8,10,16,128]{3,2,1,0:T(8,128)(2,1)} %get-tuple-element.14), channel_id=1, replica_groups=mesh['x'=4,'core'=2,'y'=4,'z'=32] {'x','core'}, dimensions={0} | all-to-all | bytes 655360 | tf_op jit(solution)/shard_map/all_to_all | solution.py:339
  27.0 1.3 %collective-permute-start = (bf16[8,10,16,128]{3,2,1,0:T(8,128)(2,1)S(1)}, bf16[8,10,16,128]{3,2,1,0:T(8,128)(2,1)S(1)}, u32[]{:S(2)}, u32[]{:S(2)}) collective-permute-start(bf16[8,10,16,128]{3,2,1,0:T(8,128)(2,1)S(1)} %all_to_all.15.own_ref), channel_id=1, source_target_pairs={{1,0},{2,1},{3,2},{4,3},{5,4},{6,5},{7,6},{8,7},{9,8},{10,9},{11,1... | collective-permute-start | bytes 983048 | tf_op jit(solution)/shard_map/ppermute | solution.py:340
  28.3 0.0 copy-done.11
  28.3 27.3 %all_to_all.16 = bf16[32,4,128]{2,1,0:T(4,128)(2,1)S(1)} all-to-all(bf16[32,4,128]{2,1,0:T(4,128)(2,1)S(1)} %copy-done.11), channel_id=1, replica_groups={{16,0,1,31,2,30,3,29,4,28,5,27,6,26,7,25,8,24,9,23,10,22,11,21,12,20,13..., dimensions={0} | all-to-all | bytes 65536 | tf_op jit(solution)/shard_map/all_to_all | solution.py:342
  55.6 0.0 collective-permute-done.first_ref
  55.6 4.5 %collective-permute-start.1 = (bf16[8,10,16,128]{3,2,1,0:T(8,128)(2,1)S(1)}, bf16[8,10,16,128]{3,2,1,0:T(8,128)(2,1)S(1)}, u32[]{:S(2)}, u32[]{:S(2)}) collective-permute-start(bf16[8,10,16,128]{3,2,1,0:T(8,128)(2,1)S(1)} %collective-permute-done.first_ref), channel_id=1, source_target_pairs={{0,128},{128,0},{1,129},{129,1},{2,130},{130,2},{3,131},{131,3},{4... | collective-permute-start | bytes 983048 | tf_op jit(solution)/shard_map/ppermute | solution.py:346
  60.1 0.9 %broadcast_in_dim.2 = bf16[16,8,16,128]{3,2,1,0:T(8,128)(2,1)} broadcast(bf16[8,16,128]{2,1,0:T(8,128)(2,1)S(1)} %bitcast.7), dimensions={1,2,3} | broadcast | bytes 557056 | tf_op jit(solution)/shard_map/broadcast_in_dim | solution.py:349
  61.0 6.6 %all-to-all-start.2 = ((bf16[16,8,16,128]{3,2,1,0:T(8,128)(2,1)}), bf16[16,8,16,128]{3,2,1,0:T(8,128)(2,1)S(1)}, u32[]{:S(2)}, u32[]{:S(2)}) async-start(bf16[16,8,16,128]{3,2,1,0:T(8,128)(2,1)} %broadcast_in_dim.2), calls=%async_computation.2 | async-start | bytes 1048576 | tf_op jit(solution)/shard_map/all_to_all | solution.py:350
  67.6 0.0 copy-start.4
  67.6 0.0 copy-start.9
  67.6 0.0 copy-start.10
  67.7 4.0 %collective-permute-start.2 = (bf16[8,2,16,128]{3,2,1,0:T(8,128)(2,1)S(1)}, bf16[8,2,16,128]{3,2,1,0:T(8,128)(2,1)S(1)}, u32[]{:S(2)}, u32[]{:S(2)}) collective-permute-start(bf16[8,2,16,128]{3,2,1,0:T(8,128)(2,1)S(1)} %pad_maximum_fusion.1), channel_id=1, source_target_pairs={{2,0},{3,1},{4,2},{5,3},{6,4},{7,5},{8,6},{9,7},{10,8},{11,9},{12,... | collective-permute-start | bytes 196616 | tf_op jit(solution)/shard_map/ppermute | solution.py:348
  71.7 0.0 collective-permute-done.1.first_mate_ref
  71.7 0.0 copy-done.4
  71.7 0.0 copy-done.9
  71.7 0.0 copy-done.10
  71.8 0.0 copy-start.2
  71.8 0.0 copy-start.3
  71.8 0.0 copy-start.6
  71.8 4.3 %near.1.near_ref = f32[4,8,256]{2,1,0:T(8,128)S(1)} custom-call(s32[4,8]{1,0:T(4,128)S(1)} %copy-done.9, s32[4]{0:T(128)S(1)} %copy-done.10, f32[3,1024]{1,0:T(4,128)S(1)} %copy-done.4, bf16[8,10,16,128]{3,2,1,0:T(8,128)(2,1)S(1)} %all_to_all.15.own_ref, bf16[8,10,16,128]{3,2,1,0:T(8,128)(2,1)S(1)} %collective-permute-done.first_ref, ...), custom_call_target="tpu_custom_call" | custom-call | flops 4000000000 | bytes 1200000 | tf_op jit(solution)/shard_map/near/pallas_call | solution.py:259
  76.1 0.0 copy-start
  76.1 0.0 collective-permute-done.2
  76.1 1.7 %all-to-all-done.2 = bf16[16,8,16,128]{3,2,1,0:T(8,128)(2,1)S(1)} async-done(((bf16[16,8,16,128]{3,2,1,0:T(8,128)(2,1)}), bf16[16,8,16,128]{3,2,1,0:T(8,128)(2,1)S(1)}, u32[]{:S(2)}, u32[]{:S(2)}) %all-to-all-start.2) | async-done | bytes 524320 | tf_op jit(solution)/shard_map/all_to_all | solution.py:350
  77.8 0.0 copy-start.1
  77.8 0.0 copy-start.5
  77.8 0.1 pad_maximum_fusion.last_ref
  77.9 0.0 copy-start.7
  77.9 0.0 copy-start.8
  77.9 4.8 %collective-permute-start.3 = (bf16[144,16,128]{2,1,0:T(8,128)(2,1)S(1)}, bf16[144,16,128]{2,1,0:T(8,128)(2,1)S(1)}, u32[]{:S(2)}, u32[]{:S(2)}) collective-permute-start(bf16[144,16,128]{2,1,0:T(8,128)(2,1)S(1)} %pad_maximum_fusion.last_ref), channel_id=1, source_target_pairs={{0,128},{128,0},{1,129},{129,1},{2,130},{130,2},{3,131},{131,3},{4... | collective-permute-start | bytes 1769480 | tf_op jit(solution)/shard_map/ppermute | solution.py:355
  83.4 1.0 %collective-permute-done.3.last_mate_ref = bf16[144,16,128]{2,1,0:T(8,128)(2,1)S(1)} collective-permute-done((bf16[144,16,128]{2,1,0:T(8,128)(2,1)S(1)}, bf16[144,16,128]{2,1,0:T(8,128)(2,1)S(1)}, u32[]{:S(2)}, u32[]{:S(2)}) %collective-permute-start.3) | collective-permute-done | bytes 589856 | tf_op jit(solution)/shard_map/ppermute | solution.py:355
  84.3 0.0 copy-done.2
  84.3 0.0 copy-done.3
  84.3 0.0 copy-done.6
  84.3 0.0 copy-done
  84.4 0.0 copy-done.1
  84.4 0.0 copy-done.5
  84.4 0.0 copy-done.7
  84.4 0.0 copy-done.8
  84.4 3.4 %far.1 = bf16[8,1024]{1,0:T(8,128)(2,1)} custom-call(s32[4,16]{1,0:T(4,128)S(1)} %copy-done.6, s32[4]{0:T(128)S(1)} %copy-done.7, s32[1,16]{1,0:T(1,128)S(1)} %copy-done.8, s32[1]{0:T(128)S(6)} %copy.14.coarse_count_ref, s32[1024]{0:T(1024)S(1)} %copy-done.5, bf16[8,10,16,128]{3,2,1,0:T(8,128)(2,1)S(1)} %all_to_all.15.own_ref, ...), custom_call_target="tpu_custom_call" | custom-call | tf_op jit(solution)/shard_map/far/pallas_call | solution.py:274
  (3 shorter events, 0.0 us)
Async XLA Ops:
  2.0 26.3 %copy-start.11 = (bf16[32,4,128]{2,1,0:T(4,128)(2,1)S(1)}, bf16[32,4,128]{2,1,0:T(4,128)(2,1)}, u32[]{:S(2)}) copy-start(bf16[32,4,128]{2,1,0:T(4,128)(2,1)} %get-tuple-element.17) | copy-start | bytes 98308
  27.0 28.6 %collective-permute-start = (bf16[8,10,16,128]{3,2,1,0:T(8,128)(2,1)S(1)}, bf16[8,10,16,128]{3,2,1,0:T(8,128)(2,1)S(1)}, u32[]{:S(2)}, u32[]{:S(2)}) collective-permute-start(bf16[8,10,16,128]{3,2,1,0:T(8,128)(2,1)S(1)} %all_to_all.15.own_ref), channel_id=1, source_target_pairs={{1,0},{2,1},{3,2},{4,3},{5,4},{6,5},{7,6},{8,7},{9,8},{10,9},{11,1... | collective-permute-start | bytes 983048 | tf_op jit(solution)/shard_map/ppermute | solution.py:340
  55.6 16.1 %collective-permute-start.1 = (bf16[8,10,16,128]{3,2,1,0:T(8,128)(2,1)S(1)}, bf16[8,10,16,128]{3,2,1,0:T(8,128)(2,1)S(1)}, u32[]{:S(2)}, u32[]{:S(2)}) collective-permute-start(bf16[8,10,16,128]{3,2,1,0:T(8,128)(2,1)S(1)} %collective-permute-done.first_ref), channel_id=1, source_target_pairs={{0,128},{128,0},{1,129},{129,1},{2,130},{130,2},{3,131},{131,3},{4... | collective-permute-start | bytes 983048 | tf_op jit(solution)/shard_map/ppermute | solution.py:346
  61.0 16.8 %all-to-all-start.2 = ((bf16[16,8,16,128]{3,2,1,0:T(8,128)(2,1)}), bf16[16,8,16,128]{3,2,1,0:T(8,128)(2,1)S(1)}, u32[]{:S(2)}, u32[]{:S(2)}) async-start(bf16[16,8,16,128]{3,2,1,0:T(8,128)(2,1)} %broadcast_in_dim.2), calls=%async_computation.2 | async-start | bytes 1048576 | tf_op jit(solution)/shard_map/all_to_all | solution.py:350
  67.6 4.1 %copy-start.4 = (f32[3,1024]{1,0:T(4,128)S(1)}, f32[3,1024]{1,0:T(4,128)}, u32[]{:S(2)}) copy-start(f32[3,1024]{1,0:T(4,128)} %points_ref.1) | copy-start | bytes 36868
  67.6 4.1 %copy-start.9 = (s32[4,8]{1,0:T(4,128)S(1)}, s32[4,8]{1,0:T(4,128)}, u32[]{:S(2)}) copy-start(s32[4,8]{1,0:T(4,128)} %list_ref.1) | copy-start | bytes 388
  67.6 4.1 %copy-start.10 = (s32[4]{0:T(128)S(1)}, s32[4]{0:T(128)}, u32[]{:S(2)}) copy-start(s32[4]{0:T(128)} %count_ref.1) | copy-start | bytes 52
  67.7 8.4 %collective-permute-start.2 = (bf16[8,2,16,128]{3,2,1,0:T(8,128)(2,1)S(1)}, bf16[8,2,16,128]{3,2,1,0:T(8,128)(2,1)S(1)}, u32[]{:S(2)}, u32[]{:S(2)}) collective-permute-start(bf16[8,2,16,128]{3,2,1,0:T(8,128)(2,1)S(1)} %pad_maximum_fusion.1), channel_id=1, source_target_pairs={{2,0},{3,1},{4,2},{5,3},{6,4},{7,5},{8,6},{9,7},{10,8},{11,9},{12,... | collective-permute-start | bytes 196616 | tf_op jit(solution)/shard_map/ppermute | solution.py:348
  71.8 12.6 %copy-start.2 = (bf16[4,64,64]{2,1,0:T(8,128)(2,1)S(1)}, bf16[4,64,64]{2,1,0:T(8,128)(2,1)}, u32[]{:S(2)}) copy-start(bf16[4,64,64]{2,1,0:T(8,128)(2,1)} %transfer_ref.1) | copy-start | bytes 98308
  71.8 12.6 %copy-start.3 = (bf16[1,16,64,64]{3,2,1,0:T(8,128)(2,1)S(1)}, bf16[1,16,64,64]{3,2,1,0:T(8,128)(2,1)}, u32[]{:S(2)}) copy-start(bf16[1,16,64,64]{3,2,1,0:T(8,128)(2,1)} %coarse_coupling_ref.1) | copy-start | bytes 393220
  71.8 12.6 %copy-start.6 = (s32[4,16]{1,0:T(4,128)S(1)}, s32[4,16]{1,0:T(4,128)}, u32[]{:S(2)}) copy-start(s32[4,16]{1,0:T(4,128)} %coupling_list_ref.1) | copy-start | bytes 772
  76.1 8.3 %copy-start = (bf16[4,16,64,64]{3,2,1,0:T(8,128)(2,1)S(1)}, bf16[4,16,64,64]{3,2,1,0:T(8,128)(2,1)}, u32[]{:S(2)}) copy-start(bf16[4,16,64,64]{3,2,1,0:T(8,128)(2,1)} %leaf_coupling_ref.1) | copy-start | bytes 1572868
  77.8 6.5 %copy-start.1 = (bf16[4,256,64]{1,2,0:T(8,128)(2,1)S(1)}, bf16[4,256,64]{1,2,0:T(8,128)(2,1)}, u32[]{:S(2)}) copy-start(bf16[4,256,64]{1,2,0:T(8,128)(2,1)} %param.15) | copy-start | bytes 393220
  77.8 6.6 %copy-start.5 = (s32[1024]{0:T(1024)S(1)}, s32[1024]{0:T(1024)}, u32[]{:S(2)}) copy-start(s32[1024]{0:T(1024)} %owner_ref.1) | copy-start | bytes 12292
  77.9 6.5 %copy-start.7 = (s32[4]{0:T(128)S(1)}, s32[4]{0:T(128)}, u32[]{:S(2)}) copy-start(s32[4]{0:T(128)} %coupling_count_ref.1) | copy-start | bytes 52
  77.9 6.5 %copy-start.8 = (s32[1,16]{1,0:T(1,128)S(1)}, s32[1,16]{1,0:T(1,128)}, u32[]{:S(2)}) copy-start(s32[1,16]{1,0:T(1,128)} %coarse_list_ref.1) | copy-start | bytes 196
  77.9 6.4 %collective-permute-start.3 = (bf16[144,16,128]{2,1,0:T(8,128)(2,1)S(1)}, bf16[144,16,128]{2,1,0:T(8,128)(2,1)S(1)}, u32[]{:S(2)}, u32[]{:S(2)}) collective-permute-start(bf16[144,16,128]{2,1,0:T(8,128)(2,1)S(1)} %pad_maximum_fusion.last_ref), channel_id=1, source_target_pairs={{0,128},{128,0},{1,129},{129,1},{2,130},{130,2},{3,131},{131,3},{4... | collective-permute-start | bytes 1769480 | tf_op jit(solution)/shard_map/ppermute | solution.py:355

commit v6 on v5

--- a/solution.py
+++ b/solution.py
@@ -72,9 +72,7 @@
     block_ref[9] = jnp.concatenate(
         [jnp.concatenate(coeffs[:2], axis=1), jnp.concatenate(coeffs[2:], axis=1)], axis=0
     ).astype(BF16)
-    block = block_ref[...]
-    for copy in range(1, copies_ref.shape[0]):
-        copies_ref[copy] = block
+    copies_ref[1] = block_ref[...]
     packed = jnp.concatenate([cluster[:4], cluster[4:]], axis=1).astype(BF16)
     cluster_ref[...] = jnp.broadcast_to(packed[None], cluster_ref.shape)
 
@@ -82,9 +80,9 @@
 def locate(leaf_id, cols):
     device = lax.shift_right_logical(leaf_id, 2)
     row = lax.shift_right_logical(device, cols.bit_length() - 1)
+    chip_gap = (row >> 1) - lax.axis_index("x")
     gap = (device & (cols - 1)) - lax.axis_index(("y", "z"))
-    fetched_here = (gap > 0) == (lax.axis_index("core") == 0)
-    return row, gap, fetched_here, leaf_id & 3
+    return chip_gap, row & 1, gap, leaf_id & 3
 
 
 def near_kernel(
@@ -92,9 +90,8 @@
     list_ref,
     count_ref,
     points_ref,
-    own_ref,
-    first_ref,
-    first_mate_ref,
+    window_ref,
+    beside_ref,
     near_ref,
     wide_ref,
 ):
@@ -103,11 +100,13 @@
     row_ids = lax.broadcasted_iota(jnp.int32, (8, 128), 0)
 
     def source_of(leaf, slot):
-        row, gap, here, source = locate(list_ref[leaf, slot], cols)
+        chip_gap, row, gap, source = locate(list_ref[leaf, slot], cols)
+        holder = jnp.where(gap == 0, row, jnp.where(gap > 0, 0, 1))
+        base = jnp.where(gap == 0, 0, BLOCK + row * BLOCK)
 
         def fetch(place):
-            beside = jnp.where(here, first_ref[row, place], first_mate_ref[row, place])
-            return jnp.where(gap == 0, own_ref[row, place], beside).astype(F32)
+            here = window_ref[holder, base + place]
+            return jnp.where(chip_gap == 0, here, beside_ref[holder, base + place]).astype(F32)
 
         sides = fetch(source)
         sides = jnp.concatenate([sides[:8], sides[8:]], axis=1)
@@ -186,11 +185,10 @@
     coarse_list_ref,
     coarse_count_ref,
     owner_ref,
-    own_ref,
-    first_ref,
-    first_mate_ref,
+    coeffs_ref,
     last_ref,
     last_mate_ref,
+    beyond_ref,
     leaf_coupling_ref,
     coarse_coupling_ref,
     transfer_ref,
@@ -220,13 +218,14 @@
         )
     for leaf in range(4):
         for slot in range(16):
-            row, gap, here, source = locate(coupling_list_ref[leaf, slot], cols)
+            chip_gap, row, gap, source = locate(coupling_list_ref[leaf, slot], cols)
             far = jnp.abs(gap)
-            beyond = groups + row * 2 + jnp.where(far == 3, 1, 0)
-            one = jnp.where(here, first_ref[row, 9], first_mate_ref[row, 9])
-            more = jnp.where(here, last_ref[beyond], last_mate_ref[beyond])
-            tile = jnp.where(far == 0, own_ref[row, 9], jnp.where(far == 1, one, more))
-            tile = tile.astype(F32)
+            place = jnp.where(far == 1, 1 + row, 1 + row * 2 + far) + jnp.where(gap < 0, 7, 0)
+            place = jnp.where(far == 0, row * 7, place)
+            fetched_here = (chip_gap < 0) == (my_core == 0)
+            tile = jnp.where(fetched_here, last_ref[groups + place], last_mate_ref[groups + place])
+            tile = jnp.where(jnp.abs(chip_gap) == 2, beyond_ref[place], tile)
+            tile = jnp.where(chip_gap == 0, coeffs_ref[place], tile).astype(F32)
             half = jnp.where(source >= 2, tile[8:], tile[:8])
             half = jnp.where(source & 1 == 1, half[:, 64:], half[:, :64])
             live = slot < coupling_count_ref[leaf]
@@ -259,7 +258,7 @@
     return pl.pallas_call(
         functools.partial(near_kernel, cols),
         out_shape=jax.ShapeDtypeStruct((4, 8, 256), F32),
-        in_specs=[SMEM] * 2 + [VMEM] * 4,
+        in_specs=[SMEM] * 2 + [VMEM] * 3,
         out_specs=VMEM,
         scratch_shapes=[pltpu.VMEM((4, 3, 32, 8, 128), F32)],
         compiler_params=PARAMS,
@@ -274,7 +273,7 @@
     return pl.pallas_call(
         functools.partial(far_kernel, groups, cols, zs),
         out_shape=jax.ShapeDtypeStruct((8, 1024), BF16),
-        in_specs=[SMEM] * 5 + [VMEM] * 10,
+        in_specs=[SMEM] * 5 + [VMEM] * 9,
         out_specs=VMEM,
         scratch_shapes=[pltpu.VMEM((5, 128, 64), F32)],
         compiler_params=PARAMS,
@@ -300,19 +299,16 @@
     near_list,
     near_count,
 ):
-    rows = 2 * xs
     cols = ys * zs
-    row_axes = ("x", "core")
-    swap = [(0, 1), (1, 0)]
     groups = xs * cols // 4
     half = zs // 2
     turned = [half, 0] + [z for near in range(1, half) for z in (near, zs - near)]
     basis = jnp.swapaxes(basis, 1, 2)
 
-    own, cluster = pl.pallas_call(
+    blocks, cluster = pl.pallas_call(
         pack_kernel,
         out_shape=(
-            jax.ShapeDtypeStruct((rows, BLOCK, 16, 128), BF16),
+            jax.ShapeDtypeStruct((2, BLOCK, 16, 128), BF16),
             jax.ShapeDtypeStruct((zs, 4, 128), BF16),
         ),
         in_specs=[ANY] * 4,
@@ -327,7 +323,7 @@
         name="pack",
     )(rhs, points, basis, transfer)
 
-    def beside(step):
+    def along_col(step):
         pairs = []
         for core in range(2):
             for col in range(cols):
@@ -336,23 +332,43 @@
                     pairs.append((core * cols + source, core * cols + col))
         return pairs
 
-    own = lax.all_to_all(own, row_axes, 0, 0, tiled=True)
-    first = lax.ppermute(own, ("core", "y", "z"), beside(1))
-    own, cluster = lax.optimization_barrier((own, cluster))
+    def along_x(step):
+        pairs = []
+        for x in range(xs):
+            for core in range(2):
+                source = x - step if core == 0 else x + step
+                if 0 <= source < xs:
+                    pairs.append((source * 2 + core, x * 2 + core))
+        return pairs
+
+    def coeffs_of(window):
+        parts = [window[:, place : place + 1] for place in (9, 19, 29)]
+        return jnp.concatenate(parts + [window[:, 30:]], axis=1).reshape(14, 16, 128)
+
+    chip = lax.all_gather(blocks, "core", axis=0, tiled=False)
+    first = lax.ppermute(chip, ("core", "y", "z"), along_col(1))[:, 0]
+    chip, cluster = lax.optimization_barrier((chip, cluster))
     line = lax.all_to_all(
         cluster, "z", 0, 0, tiled=True, axis_index_groups=[turned]
     ).reshape(zs // 4, 16, 128)
     first, line = lax.optimization_barrier((first, line))
-    first_mate = lax.ppermute(first, "core", swap)
-    coeffs = jnp.concatenate([own[:, 9:], first[:, 9:]], axis=1)
-    second = lax.ppermute(coeffs, ("core", "y", "z"), beside(2))
+    second = jnp.concatenate([chip[:, 0, 9:], first[:, 9:]], axis=1)
+    second = lax.ppermute(second, ("core", "y", "z"), along_col(2))
     line = jnp.broadcast_to(line[None], (xs * ys,) + line.shape)
     same = lax.all_to_all(line, ("x", "y"), 0, 0, tiled=True).reshape(groups, 16, 128)
 
-    near = near_call(cols, near_list, near_count, points, own, first, first_mate)
-    same, second, near = lax.optimization_barrier((same, second, near))
-    last = jnp.concatenate([same, second.reshape(rows * 2, 16, 128)], axis=0)
-    last_mate = lax.ppermute(last, "core", swap)
+    window = jnp.concatenate(
+        [blocks[0], first.reshape(2 * BLOCK, 16, 128), second.reshape(4, 16, 128)], axis=0
+    )
+    window = lax.all_gather(window, "core", axis=0, tiled=False)
+    beside = lax.ppermute(window, ("x", "core"), along_x(1))
+    coeffs = coeffs_of(window)
+    beyond = lax.ppermute(coeffs, ("x", "core"), along_x(2))
+    near = near_call(cols, near_list, near_count, points, window, beside)
+
+    same, beside, beyond, near = lax.optimization_barrier((same, beside, beyond, near))
+    last = jnp.concatenate([same, coeffs_of(beside)], axis=0)
+    last_mate = lax.ppermute(last, "core", [(0, 1), (1, 0)])
 
     return far_call(
         groups,
@@ -363,11 +379,10 @@
         coarse_list,
         coarse_count,
         owner,
-        own,
-        first,
-        first_mate,
+        coeffs,
         last,
         last_mate,
+        beyond,
         leaf_coupling,
         coarse_coupling,
         transfer,

time: 88.3 us -> 85.8 us (0.972)
  blocking collectives: 52.3 us -> 23.1 us
  starting transfers between devices: 21.2 us -> 41.4 us
  waiting for transfers between devices: 2.71 us -> 8.98 us
    all_to_all x2 -> x0, blocking collectives: 52.3 us -> none  [the longest x1 27.3 us: per_device(): lax.all_to_all(cluster, 'z', 0, 0, tiled=True, axis_index_groups=[turned])]
    all_to_all x0 -> x1, starting transfers between devices: none -> 23.6 us  [per_device(): lax.all_to_all(cluster, 'z', 0, 0, tiled=True, axis_index_groups=[turned])]
    all_gather x0 -> x2, blocking collectives: none -> 23.1 us  [the longest x1 15.9 us: per_device(): chip = lax.all_gather(blocks, 'core', axis=0, tiled=False)]
    ppermute x4 -> x5, waiting for transfers between devices: 0.97 us -> 6.06 us  [the longest x1 5.1 us: per_device(): beside = lax.ppermute(window, ('x', 'core'), along_x(1))]
    ppermute x4 -> x5, starting transfers between devices: 14.6 us -> 11 us  [the longest x1 4.02 us: per_device(): second = lax.ppermute(second, ('core', 'y', 'z'), along_col(2))]
    all_to_all x0 -> x1, waiting for transfers between devices: none -> 2.92 us  [per_device(): lax.all_to_all(cluster, 'z', 0, 0, tiled=True, axis_index_groups=[turned])]
    all_to_all x1, waiting for transfers between devices: 1.74 us -> 0.01 us  [per_device(): lax.all_to_all(line, ('x', 'y'), 0, 0, tiled=True).reshape(groups, 16, 128)]
  transfers between devices with their start and end apart: 5 -> 7, of which waited for: 2 -> 3; matrix products, arithmetic and copies ran while one was open for 1% -> 1% of each run, Pallas kernels for 5% -> 5%
where the time goes in v6:
time: 85.8 us; the launch traced here: 85.3 us
  starting transfers between devices  41.4 us (48%)
  blocking collectives  23.1 us (27%)
  Pallas kernels  9.78 us (11%)
  waiting for transfers between devices  8.98 us (10%)
  local copies, waits for them, and re-layouts  1.01 us (1%)
  between operations  0.97 us (1%)
    all_to_all x1, starting transfers between devices, per_device(): lax.all_to_all(cluster, 'z', 0, 0, tiled=True, axis_index_groups=[turned])  23.6 us
    all_gather x1, blocking collectives, per_device(): chip = lax.all_gather(blocks, 'core', axis=0, tiled=False)  15.9 us
    all_gather x1, blocking collectives, per_device(): window = lax.all_gather(window, 'core', axis=0, tiled=False)  7.19 us
    all_to_all x1, starting transfers between devices, per_device(): lax.all_to_all(line, ('x', 'y'), 0, 0, tiled=True).reshape(groups, 16, 128)  6.76 us
    ppermute x1, waiting for transfers between devices, per_device(): beside = lax.ppermute(window, ('x', 'core'), along_x(1))  5.1 us
    pallas_call x1, Pallas kernels, near_call(): pl.pallas_call(functools.partial(near_kernel, cols), out_shape=jax.ShapeD...  4.25 us
    ppermute x1, starting transfers between devices, per_device(): second = lax.ppermute(second, ('core', 'y', 'z'), along_col(2))  4.02 us
    pallas_call x1, Pallas kernels, far_call(): pl.pallas_call(functools.partial(far_kernel, groups, cols, zs), out_shape...  3.59 us
  transfers between devices with their start and end apart: 7, of which 3 were waited for; matrix products, arithmetic and copies ran while one was open for 1% of the time, Pallas kernels for 5%

profile of v6, /device:TPU:1, one launch (start us, length us, event | category | flops | bytes accessed | tf_op | source)
XLA Modules:
  0.0 85.3 jit_solution(13570053832191717787)
XLA Ops:
  0.0 1.9 %pack.1 = (bf16[2,10,16,128]{3,2,1,0:T(8,128)(2,1)}, bf16[32,4,128]{2,1,0:T(4,128)(2,1)}) custom-call(bf16[8,1024]{1,0:T(8,128)(2,1)} %rhs_hbm.1, f32[3,1024]{1,0:T(4,128)} %points_ref.1, bf16[4,64,256]{2,1,0:T(8,128)(2,1)} %bitcast.15, bf16[4,64,64]{2,1,0:T(8,128)(2,1)} %transfer_ref.1), custom_call_target="tpu_custom_call" | custom-call | tf_op jit(solution)/shard_map/pack/pallas_call | solution.py:308
  1.9 15.9 %all-gather = bf16[4,10,16,128]{3,2,1,0:T(8,128)(2,1)S(1)} all-gather(bf16[2,10,16,128]{3,2,1,0:T(8,128)(2,1)} %get-tuple-element.15), channel_id=2, replica_groups=mesh['x'=4,'core'=2,'y'=4,'z'=32] {'core'}, dimensions={0}, use_global_device_ids=true | all-gather | bytes 245760 | tf_op jit(solution)/shard_map/all_gather | solution.py:348
  17.9 1.3 %collective-permute-start = (bf16[2,2,10,16,128]{4,3,2,1,0:T(8,128)(2,1)S(1)}, bf16[2,2,10,16,128]{4,3,2,1,0:T(8,128)(2,1)S(1)}, u32[]{:S(2)}, u32[]{:S(2)}) collective-permute-start(bf16[2,2,10,16,128]{4,3,2,1,0:T(8,128)(2,1)S(1)} %bitcast.26), channel_id=1, source_target_pairs={{1,0},{2,1},{3,2},{4,3},{5,4},{6,5},{7,6},{8,7},{9,8},{10,9},{11,1... | collective-permute-start | bytes 491528 | tf_op jit(solution)/shard_map/ppermute | solution.py:349
  19.2 23.6 %all-to-all-start = ((bf16[32,4,128]{2,1,0:T(4,128)(2,1)}), bf16[32,4,128]{2,1,0:T(4,128)(2,1)S(1)}, u32[]{:S(2)}, u32[]{:S(2)}) async-start(bf16[32,4,128]{2,1,0:T(4,128)(2,1)} %get-tuple-element.17), calls=%async_computation | async-start | bytes 65536 | tf_op jit(solution)/shard_map/all_to_all | solution.py:351
  42.8 0.0 copy-start.11
  42.8 0.0 collective-permute-done
  42.8 2.9 %all-to-all-done = bf16[32,4,128]{2,1,0:T(4,128)(2,1)S(1)} async-done(((bf16[32,4,128]{2,1,0:T(4,128)(2,1)}), bf16[32,4,128]{2,1,0:T(4,128)(2,1)S(1)}, u32[]{:S(2)}, u32[]{:S(2)}) %all-to-all-start) | async-done | bytes 32800 | tf_op jit(solution)/shard_map/all_to_all | solution.py:351
  45.7 4.0 %collective-permute-start.1 = (bf16[2,2,16,128]{3,2,1,0:T(8,128)(2,1)S(1)}, bf16[2,2,16,128]{3,2,1,0:T(8,128)(2,1)S(1)}, u32[]{:S(2)}, u32[]{:S(2)}) collective-permute-start(bf16[2,2,16,128]{3,2,1,0:T(8,128)(2,1)S(1)} %pad_maximum_fusion.4), channel_id=1, source_target_pairs={{2,0},{3,1},{4,2},{5,3},{6,4},{7,5},{8,6},{9,7},{10,8},{11,9},{12,... | collective-permute-start | bytes 49160 | tf_op jit(solution)/shard_map/ppermute | solution.py:356
  49.8 0.0 copy-done.11
  49.8 0.9 %broadcast_in_dim.2 = bf16[16,8,16,128]{3,2,1,0:T(8,128)(2,1)} broadcast(bf16[8,16,128]{2,1,0:T(8,128)(2,1)S(1)} %bitcast.28), dimensions={1,2,3} | broadcast | bytes 557056 | tf_op jit(solution)/shard_map/broadcast_in_dim | solution.py:357
  50.7 6.8 %all-to-all-start.1 = ((bf16[16,8,16,128]{3,2,1,0:T(8,128)(2,1)}), bf16[16,8,16,128]{3,2,1,0:T(8,128)(2,1)S(1)}, u32[]{:S(2)}, u32[]{:S(2)}) async-start(bf16[16,8,16,128]{3,2,1,0:T(8,128)(2,1)} %broadcast_in_dim.2), calls=%async_computation.1 | async-start | bytes 1048576 | tf_op jit(solution)/shard_map/all_to_all | solution.py:358
  57.5 0.0 collective-permute-done.1
  57.5 7.2 %all-gather.1 = bf16[68,16,128]{2,1,0:T(8,128)(2,1)S(1)} all-gather(bf16[34,16,128]{2,1,0:T(8,128)(2,1)S(1)} %pad_maximum_fusion.1), channel_id=3, replica_groups=mesh['x'=4,'core'=2,'y'=4,'z'=32] {'core'}, dimensions={0}, use_global_device_ids=true | all-gather | bytes 417792 | tf_op jit(solution)/shard_map/all_gather | solution.py:363
  64.7 1.3 %collective-permute-start.2 = (bf16[2,34,16,128]{3,2,1,0:T(8,128)(2,1)S(1)}, bf16[2,34,16,128]{3,2,1,0:T(8,128)(2,1)S(1)}, u32[]{:S(2)}, u32[]{:S(2)}) collective-permute-start(bf16[2,34,16,128]{3,2,1,0:T(8,128)(2,1)S(1)} %bitcast.17), channel_id=1, source_target_pairs={{384,128},{0,256},{640,384},{256,512},{896,640},{512,768},{385,129... | collective-permute-start | bytes 835592 | tf_op jit(solution)/shard_map/ppermute | solution.py:364
  66.0 0.0 copy-start.4
  66.0 0.0 copy-start.9
  66.0 0.0 copy-start.10
  66.0 1.3 %collective-permute-start.3 = (bf16[14,16,128]{2,1,0:T(8,128)(2,1)S(1)}, bf16[14,16,128]{2,1,0:T(8,128)(2,1)S(1)}, u32[]{:S(2)}, u32[]{:S(2)}) collective-permute-start(bf16[14,16,128]{2,1,0:T(8,128)(2,1)S(1)} %bitcast.21), channel_id=1, source_target_pairs={{640,128},{896,384},{0,512},{256,768},{641,129},{897,385},{1,513},... | collective-permute-start | bytes 172040 | tf_op jit(solution)/shard_map/ppermute | solution.py:366
  67.3 5.1 %collective-permute-done.2.beside_ref = bf16[2,34,16,128]{3,2,1,0:T(8,128)(2,1)S(1)} collective-permute-done((bf16[2,34,16,128]{3,2,1,0:T(8,128)(2,1)S(1)}, bf16[2,34,16,128]{3,2,1,0:T(8,128)(2,1)S(1)}, u32[]{:S(2)}, u32[]{:S(2)}) %collective-permute-start.2) | collective-permute-done | bytes 278560 | tf_op jit(solution)/shard_map/ppermute | solution.py:364
  72.5 0.0 copy-done.4
  72.5 0.0 copy-done.9
  72.5 0.0 copy-done.10
  72.5 0.0 copy-start.2
  72.5 4.2 %near.1.near_ref = f32[4,8,256]{2,1,0:T(8,128)S(1)} custom-call(s32[4,8]{1,0:T(4,128)S(1)} %copy-done.9, s32[4]{0:T(128)S(1)} %copy-done.10, f32[3,1024]{1,0:T(4,128)S(1)} %copy-done.4, bf16[2,34,16,128]{3,2,1,0:T(8,128)(2,1)S(1)} %bitcast.20, bf16[2,34,16,128]{3,2,1,0:T(8,128)(2,1)S(1)} %collective-permute-done.2.beside_ref), custom_call_target="tpu_custom_call" | custom-call | flops 4000000000 | bytes 1200000 | tf_op jit(solution)/shard_map/near/pallas_call | solution.py:258
  76.7 0.0 copy-start
  76.7 0.0 collective-permute-done.3.beyond_ref
  76.7 0.0 all-to-all-done.1
  76.8 0.0 copy-start.1
  76.8 0.0 copy-start.3
  76.8 0.0 copy-start.5
  76.8 0.0 copy-start.6
  76.8 0.1 pad_maximum_fusion.last_ref
  76.9 0.0 copy-start.7
  76.9 0.0 copy-start.8
  76.9 3.2 %collective-permute-start.4 = (bf16[142,16,128]{2,1,0:T(8,128)(2,1)S(1)}, bf16[142,16,128]{2,1,0:T(8,128)(2,1)S(1)}, u32[]{:S(2)}, u32[]{:S(2)}) collective-permute-start(bf16[142,16,128]{2,1,0:T(8,128)(2,1)S(1)} %pad_maximum_fusion.last_ref), channel_id=1, source_target_pairs={{0,128},{128,0},{1,129},{129,1},{2,130},{130,2},{3,131},{131,3},{4... | collective-permute-start | bytes 1744904 | tf_op jit(solution)/shard_map/ppermute | solution.py:371
  80.7 0.9 %collective-permute-done.4.last_mate_ref = bf16[142,16,128]{2,1,0:T(8,128)(2,1)S(1)} collective-permute-done((bf16[142,16,128]{2,1,0:T(8,128)(2,1)S(1)}, bf16[142,16,128]{2,1,0:T(8,128)(2,1)S(1)}, u32[]{:S(2)}, u32[]{:S(2)}) %collective-permute-start.4) | collective-permute-done | bytes 581664 | tf_op jit(solution)/shard_map/ppermute | solution.py:371
  81.7 0.0 copy-done.2
  81.7 0.0 copy-done
  81.7 0.0 copy-done.1
  81.7 0.0 copy-done.3
  81.7 0.0 copy-done.5
  81.7 0.0 copy-done.6
  81.7 0.0 copy-done.7
  81.7 0.0 copy-done.8
  81.7 3.6 %far.1 = bf16[8,1024]{1,0:T(8,128)(2,1)} custom-call(s32[4,16]{1,0:T(4,128)S(1)} %copy-done.6, s32[4]{0:T(128)S(1)} %copy-done.7, s32[1,16]{1,0:T(1,128)S(1)} %copy-done.8, s32[1]{0:T(128)S(6)} %copy.18.coarse_count_ref, s32[1024]{0:T(1024)S(1)} %copy-done.5, bf16[14,16,128]{2,1,0:T(8,128)(2,1)S(1)} %bitcast.22, ...), custom_call_target="tpu_custom_call" | custom-call | tf_op jit(solution)/shard_map/far/pallas_call | solution.py:273
  (12 shorter events, 0.1 us)
Async XLA Ops:
  17.9 24.9 %collective-permute-start = (bf16[2,2,10,16,128]{4,3,2,1,0:T(8,128)(2,1)S(1)}, bf16[2,2,10,16,128]{4,3,2,1,0:T(8,128)(2,1)S(1)}, u32[]{:S(2)}, u32[]{:S(2)}) collective-permute-start(bf16[2,2,10,16,128]{4,3,2,1,0:T(8,128)(2,1)S(1)} %bitcast.26), channel_id=1, source_target_pairs={{1,0},{2,1},{3,2},{4,3},{5,4},{6,5},{7,6},{8,7},{9,8},{10,9},{11,1... | collective-permute-start | bytes 491528 | tf_op jit(solution)/shard_map/ppermute | solution.py:349
  19.2 26.5 %all-to-all-start = ((bf16[32,4,128]{2,1,0:T(4,128)(2,1)}), bf16[32,4,128]{2,1,0:T(4,128)(2,1)S(1)}, u32[]{:S(2)}, u32[]{:S(2)}) async-start(bf16[32,4,128]{2,1,0:T(4,128)(2,1)} %get-tuple-element.17), calls=%async_computation | async-start | bytes 65536 | tf_op jit(solution)/shard_map/all_to_all | solution.py:351
  42.8 7.0 %copy-start.11 = (bf16[2,10,16,128]{3,2,1,0:T(8,128)(2,1)S(1)}, bf16[2,10,16,128]{3,2,1,0:T(8,128)(2,1)}, u32[]{:S(2)}) copy-start(bf16[2,10,16,128]{3,2,1,0:T(8,128)(2,1)} %get-tuple-element.15) | copy-start | bytes 245764
  45.7 11.7 %collective-permute-start.1 = (bf16[2,2,16,128]{3,2,1,0:T(8,128)(2,1)S(1)}, bf16[2,2,16,128]{3,2,1,0:T(8,128)(2,1)S(1)}, u32[]{:S(2)}, u32[]{:S(2)}) collective-permute-start(bf16[2,2,16,128]{3,2,1,0:T(8,128)(2,1)S(1)} %pad_maximum_fusion.4), channel_id=1, source_target_pairs={{2,0},{3,1},{4,2},{5,3},{6,4},{7,5},{8,6},{9,7},{10,8},{11,9},{12,... | collective-permute-start | bytes 49160 | tf_op jit(solution)/shard_map/ppermute | solution.py:356
  50.7 26.0 %all-to-all-start.1 = ((bf16[16,8,16,128]{3,2,1,0:T(8,128)(2,1)}), bf16[16,8,16,128]{3,2,1,0:T(8,128)(2,1)S(1)}, u32[]{:S(2)}, u32[]{:S(2)}) async-start(bf16[16,8,16,128]{3,2,1,0:T(8,128)(2,1)} %broadcast_in_dim.2), calls=%async_computation.1 | async-start | bytes 1048576 | tf_op jit(solution)/shard_map/all_to_all | solution.py:358
  64.7 7.8 %collective-permute-start.2 = (bf16[2,34,16,128]{3,2,1,0:T(8,128)(2,1)S(1)}, bf16[2,34,16,128]{3,2,1,0:T(8,128)(2,1)S(1)}, u32[]{:S(2)}, u32[]{:S(2)}) collective-permute-start(bf16[2,34,16,128]{3,2,1,0:T(8,128)(2,1)S(1)} %bitcast.17), channel_id=1, source_target_pairs={{384,128},{0,256},{640,384},{256,512},{896,640},{512,768},{385,129... | collective-permute-start | bytes 835592 | tf_op jit(solution)/shard_map/ppermute | solution.py:364
  66.0 6.5 %copy-start.4 = (f32[3,1024]{1,0:T(4,128)S(1)}, f32[3,1024]{1,0:T(4,128)}, u32[]{:S(2)}) copy-start(f32[3,1024]{1,0:T(4,128)} %points_ref.1) | copy-start | bytes 36868
  66.0 6.4 %copy-start.9 = (s32[4,8]{1,0:T(4,128)S(1)}, s32[4,8]{1,0:T(4,128)}, u32[]{:S(2)}) copy-start(s32[4,8]{1,0:T(4,128)} %list_ref.1) | copy-start | bytes 388
  66.0 6.4 %copy-start.10 = (s32[4]{0:T(128)S(1)}, s32[4]{0:T(128)}, u32[]{:S(2)}) copy-start(s32[4]{0:T(128)} %count_ref.1) | copy-start | bytes 52
  66.0 10.7 %collective-permute-start.3 = (bf16[14,16,128]{2,1,0:T(8,128)(2,1)S(1)}, bf16[14,16,128]{2,1,0:T(8,128)(2,1)S(1)}, u32[]{:S(2)}, u32[]{:S(2)}) collective-permute-start(bf16[14,16,128]{2,1,0:T(8,128)(2,1)S(1)} %bitcast.21), channel_id=1, source_target_pairs={{640,128},{896,384},{0,512},{256,768},{641,129},{897,385},{1,513},... | collective-permute-start | bytes 172040 | tf_op jit(solution)/shard_map/ppermute | solution.py:366
  72.5 9.2 %copy-start.2 = (bf16[1,16,64,64]{3,2,1,0:T(8,128)(2,1)S(1)}, bf16[1,16,64,64]{3,2,1,0:T(8,128)(2,1)}, u32[]{:S(2)}) copy-start(bf16[1,16,64,64]{3,2,1,0:T(8,128)(2,1)} %coarse_coupling_ref.1) | copy-start | bytes 393220
  76.7 5.0 %copy-start = (bf16[4,16,64,64]{3,2,1,0:T(8,128)(2,1)S(1)}, bf16[4,16,64,64]{3,2,1,0:T(8,128)(2,1)}, u32[]{:S(2)}) copy-start(bf16[4,16,64,64]{3,2,1,0:T(8,128)(2,1)} %leaf_coupling_ref.1) | copy-start | bytes 1572868
  76.8 4.9 %copy-start.1 = (bf16[4,256,64]{1,2,0:T(8,128)(2,1)S(1)}, bf16[4,256,64]{1,2,0:T(8,128)(2,1)}, u32[]{:S(2)}) copy-start(bf16[4,256,64]{1,2,0:T(8,128)(2,1)} %param.15) | copy-start | bytes 393220
  76.8 4.9 %copy-start.3 = (bf16[4,64,64]{2,1,0:T(8,128)(2,1)S(1)}, bf16[4,64,64]{2,1,0:T(8,128)(2,1)}, u32[]{:S(2)}) copy-start(bf16[4,64,64]{2,1,0:T(8,128)(2,1)} %transfer_ref.1) | copy-start | bytes 98308
  76.8 4.9 %copy-start.5 = (s32[1024]{0:T(1024)S(1)}, s32[1024]{0:T(1024)}, u32[]{:S(2)}) copy-start(s32[1024]{0:T(1024)} %owner_ref.1) | copy-start | bytes 12292
  76.8 4.9 %copy-start.6 = (s32[4,16]{1,0:T(4,128)S(1)}, s32[4,16]{1,0:T(4,128)}, u32[]{:S(2)}) copy-start(s32[4,16]{1,0:T(4,128)} %coupling_list_ref.1) | copy-start | bytes 772
  76.9 4.8 %copy-start.7 = (s32[4]{0:T(128)S(1)}, s32[4]{0:T(128)}, u32[]{:S(2)}) copy-start(s32[4]{0:T(128)} %coupling_count_ref.1) | copy-start | bytes 52
  76.9 4.8 %copy-start.8 = (s32[1,16]{1,0:T(1,128)S(1)}, s32[1,16]{1,0:T(1,128)}, u32[]{:S(2)}) copy-start(s32[1,16]{1,0:T(1,128)} %coarse_list_ref.1) | copy-start | bytes 196
  76.9 4.8 %collective-permute-start.4 = (bf16[142,16,128]{2,1,0:T(8,128)(2,1)S(1)}, bf16[142,16,128]{2,1,0:T(8,128)(2,1)S(1)}, u32[]{:S(2)}, u32[]{:S(2)}) collective-permute-start(bf16[142,16,128]{2,1,0:T(8,128)(2,1)S(1)} %pad_maximum_fusion.last_ref), channel_id=1, source_target_pairs={{0,128},{128,0},{1,129},{129,1},{2,130},{130,2},{3,131},{131,3},{4... | collective-permute-start | bytes 1744904 | tf_op jit(solution)/shard_map/ppermute | solution.py:371

commit v7 on v6

--- a/solution.py
+++ b/solution.py
@@ -351,7 +351,6 @@
     line = lax.all_to_all(
         cluster, "z", 0, 0, tiled=True, axis_index_groups=[turned]
     ).reshape(zs // 4, 16, 128)
-    first, line = lax.optimization_barrier((first, line))
     second = jnp.concatenate([chip[:, 0, 9:], first[:, 9:]], axis=1)
     second = lax.ppermute(second, ("core", "y", "z"), along_col(2))
     line = jnp.broadcast_to(line[None], (xs * ys,) + line.shape)
@@ -364,10 +363,10 @@
     beside = lax.ppermute(window, ("x", "core"), along_x(1))
     coeffs = coeffs_of(window)
     beyond = lax.ppermute(coeffs, ("x", "core"), along_x(2))
+    same, beside = lax.optimization_barrier((same, beside))
+    last = jnp.concatenate([same, coeffs_of(beside)], axis=0)
+    last, beside = lax.optimization_barrier((last, beside))
     near = near_call(cols, near_list, near_count, points, window, beside)
-
-    same, beside, beyond, near = lax.optimization_barrier((same, beside, beyond, near))
-    last = jnp.concatenate([same, coeffs_of(beside)], axis=0)
     last_mate = lax.ppermute(last, "core", [(0, 1), (1, 0)])
 
     return far_call(

time: 85.8 us -> 82.9 us (0.966)
  the two profiles are of different devices: /device:TPU:1 before, /device:TPU:8 now
where the time goes in v7:
time: 82.9 us; the launch traced here: 82.4 us
  starting transfers between devices  61.2 us (74%)
  Pallas kernels  9.8 us (12%)
  waiting for transfers between devices  5.12 us (6%)
  blocking collectives  4.14 us (5%)
  local copies, waits for them, and re-layouts  1.03 us (1%)
  between operations  1 us (1%)
    all_to_all x1, starting transfers between devices, per_device(): lax.all_to_all(cluster, 'z', 0, 0, tiled=True, axis_index_groups=[turned])  21.8 us
    ppermute x1, starting transfers between devices, per_device(): first = lax.ppermute(chip, ('core', 'y', 'z'), along_col(1))[:, 0]  18.6 us
    all_to_all x1, starting transfers between devices, per_device(): lax.all_to_all(line, ('x', 'y'), 0, 0, tiled=True).reshape(groups, 16, 128)  7.64 us
    ppermute x1, starting transfers between devices, per_device(): beyond = lax.ppermute(coeffs, ('x', 'core'), along_x(2))  6.02 us
    pallas_call x1, Pallas kernels, near_call(): pl.pallas_call(functools.partial(near_kernel, cols), out_shape=jax.ShapeD...  4.25 us
    pallas_call x1, Pallas kernels, far_call(): pl.pallas_call(functools.partial(far_kernel, groups, cols, zs), out_shape...  3.6 us
    ppermute x1, waiting for transfers between devices, per_device(): beside = lax.ppermute(window, ('x', 'core'), along_x(1))  3.38 us
    ppermute x1, starting transfers between devices, per_device(): beside = lax.ppermute(window, ('x', 'core'), along_x(1))  3.37 us
  transfers between devices with their start and end apart: 7, of which 2 were waited for; matrix products, arithmetic and copies ran while one was open for 1% of the time, Pallas kernels for 5%

profile of v7, /device:TPU:8, one launch (start us, length us, event | category | flops | bytes accessed | tf_op | source)
XLA Modules:
  0.0 82.4 jit_solution(11653306317237577682)
XLA Ops:
  0.0 2.0 %pack.1 = (bf16[2,10,16,128]{3,2,1,0:T(8,128)(2,1)}, bf16[32,4,128]{2,1,0:T(4,128)(2,1)}) custom-call(bf16[8,1024]{1,0:T(8,128)(2,1)} %rhs_hbm.1, f32[3,1024]{1,0:T(4,128)} %points_ref.1, bf16[4,64,256]{2,1,0:T(8,128)(2,1)} %bitcast.15, bf16[4,64,64]{2,1,0:T(8,128)(2,1)} %transfer_ref.1), custom_call_target="tpu_custom_call" | custom-call | tf_op jit(solution)/shard_map/pack/pallas_call | solution.py:308
  2.0 2.1 %all-gather = bf16[4,10,16,128]{3,2,1,0:T(8,128)(2,1)S(1)} all-gather(bf16[2,10,16,128]{3,2,1,0:T(8,128)(2,1)} %get-tuple-element.13), channel_id=2, replica_groups=mesh['x'=4,'core'=2,'y'=4,'z'=32] {'core'}, dimensions={0}, use_global_device_ids=true | all-gather | bytes 245760 | tf_op jit(solution)/shard_map/all_gather | solution.py:348
  4.1 18.6 %collective-permute-start = (bf16[2,2,10,16,128]{4,3,2,1,0:T(8,128)(2,1)S(1)}, bf16[2,2,10,16,128]{4,3,2,1,0:T(8,128)(2,1)S(1)}, u32[]{:S(2)}, u32[]{:S(2)}) collective-permute-start(bf16[2,2,10,16,128]{4,3,2,1,0:T(8,128)(2,1)S(1)} %bitcast.26), channel_id=1, source_target_pairs={{1,0},{2,1},{3,2},{4,3},{5,4},{6,5},{7,6},{8,7},{9,8},{10,9},{11,1... | collective-permute-start | bytes 491528 | tf_op jit(solution)/shard_map/ppermute | solution.py:349
  22.7 21.8 %all-to-all-start = ((bf16[32,4,128]{2,1,0:T(4,128)(2,1)}), bf16[32,4,128]{2,1,0:T(4,128)(2,1)S(1)}, u32[]{:S(2)}, u32[]{:S(2)}) async-start(bf16[32,4,128]{2,1,0:T(4,128)(2,1)} %get-tuple-element.16), calls=%async_computation | async-start | bytes 65536 | tf_op jit(solution)/shard_map/all_to_all | solution.py:351
  44.5 0.0 collective-permute-done
  44.5 1.9 %collective-permute-start.1 = (bf16[2,2,16,128]{3,2,1,0:T(8,128)(2,1)S(1)}, bf16[2,2,16,128]{3,2,1,0:T(8,128)(2,1)S(1)}, u32[]{:S(2)}, u32[]{:S(2)}) collective-permute-start(bf16[2,2,16,128]{3,2,1,0:T(8,128)(2,1)S(1)} %pad_maximum_fusion.4), channel_id=1, source_target_pairs={{2,0},{3,1},{4,2},{5,3},{6,4},{7,5},{8,6},{9,7},{10,8},{11,9},{12,... | collective-permute-start | bytes 49160 | tf_op jit(solution)/shard_map/ppermute | solution.py:355
  46.5 1.7 %all-to-all-done = bf16[32,4,128]{2,1,0:T(4,128)(2,1)S(1)} async-done(((bf16[32,4,128]{2,1,0:T(4,128)(2,1)}), bf16[32,4,128]{2,1,0:T(4,128)(2,1)S(1)}, u32[]{:S(2)}, u32[]{:S(2)}) %all-to-all-start) | async-done | bytes 32800 | tf_op jit(solution)/shard_map/all_to_all | solution.py:351
  48.2 0.9 %broadcast_in_dim.8 = bf16[16,8,16,128]{3,2,1,0:T(8,128)(2,1)} broadcast(bf16[8,16,128]{2,1,0:T(8,128)(2,1)S(1)} %bitcast.28), dimensions={1,2,3} | broadcast | bytes 557056 | tf_op jit(solution)/shard_map/broadcast_in_dim | solution.py:356
  49.1 0.0 copy-start.11
  49.1 7.6 %all-to-all-start.1 = ((bf16[16,8,16,128]{3,2,1,0:T(8,128)(2,1)}), bf16[16,8,16,128]{3,2,1,0:T(8,128)(2,1)S(1)}, u32[]{:S(2)}, u32[]{:S(2)}) async-start(bf16[16,8,16,128]{3,2,1,0:T(8,128)(2,1)} %broadcast_in_dim.8), calls=%async_computation.1 | async-start | bytes 1048576 | tf_op jit(solution)/shard_map/all_to_all | solution.py:357
  56.7 0.0 copy-done.11
  56.8 0.0 collective-permute-done.1
  56.8 2.0 %all-gather.1 = bf16[68,16,128]{2,1,0:T(8,128)(2,1)S(1)} all-gather(bf16[34,16,128]{2,1,0:T(8,128)(2,1)S(1)} %pad_maximum_fusion.1), channel_id=3, replica_groups=mesh['x'=4,'core'=2,'y'=4,'z'=32] {'core'}, dimensions={0}, use_global_device_ids=true | all-gather | bytes 417792 | tf_op jit(solution)/shard_map/all_gather | solution.py:362
  58.8 3.4 %collective-permute-start.2 = (bf16[2,34,16,128]{3,2,1,0:T(8,128)(2,1)S(1)}, bf16[2,34,16,128]{3,2,1,0:T(8,128)(2,1)S(1)}, u32[]{:S(2)}, u32[]{:S(2)}) collective-permute-start(bf16[2,34,16,128]{3,2,1,0:T(8,128)(2,1)S(1)} %bitcast.17), channel_id=1, source_target_pairs={{384,128},{0,256},{640,384},{256,512},{896,640},{512,768},{385,129... | collective-permute-start | bytes 835592 | tf_op jit(solution)/shard_map/ppermute | solution.py:363
  62.8 3.4 %collective-permute-done.2.beside_ref = bf16[2,34,16,128]{3,2,1,0:T(8,128)(2,1)S(1)} collective-permute-done((bf16[2,34,16,128]{3,2,1,0:T(8,128)(2,1)S(1)}, bf16[2,34,16,128]{3,2,1,0:T(8,128)(2,1)S(1)}, u32[]{:S(2)}, u32[]{:S(2)}) %collective-permute-start.2) | collective-permute-done | bytes 278560 | tf_op jit(solution)/shard_map/ppermute | solution.py:363
  66.2 0.0 all-to-all-done.1
  66.2 0.1 pad_maximum_fusion.last_ref
  66.3 1.9 %collective-permute-start.3 = (bf16[142,16,128]{2,1,0:T(8,128)(2,1)S(1)}, bf16[142,16,128]{2,1,0:T(8,128)(2,1)S(1)}, u32[]{:S(2)}, u32[]{:S(2)}) collective-permute-start(bf16[142,16,128]{2,1,0:T(8,128)(2,1)S(1)} %pad_maximum_fusion.last_ref), channel_id=1, source_target_pairs={{0,128},{128,0},{1,129},{129,1},{2,130},{130,2},{3,131},{131,3},{4... | collective-permute-start | bytes 1744904 | tf_op jit(solution)/shard_map/ppermute | solution.py:370
  68.3 0.0 copy-start.4
  68.3 0.0 copy-start.9
  68.3 0.0 copy-start.10
  68.3 0.0 copy-start
  68.3 0.0 copy-start.1
  68.3 0.0 copy-start.2
  68.4 0.0 copy-start.3
  68.4 0.0 copy-start.5
  68.4 0.0 copy-start.6
  68.4 0.0 copy-start.7
  68.4 0.0 copy-start.8
  68.4 6.0 %collective-permute-start.4 = (bf16[14,16,128]{2,1,0:T(8,128)(2,1)S(1)}, bf16[14,16,128]{2,1,0:T(8,128)(2,1)S(1)}, u32[]{:S(2)}, u32[]{:S(2)}) collective-permute-start(bf16[14,16,128]{2,1,0:T(8,128)(2,1)S(1)} %bitcast.21), channel_id=1, source_target_pairs={{640,128},{896,384},{0,512},{256,768},{641,129},{897,385},{1,513},... | collective-permute-start | bytes 172040 | tf_op jit(solution)/shard_map/ppermute | solution.py:365
  74.4 0.0 copy-done.4
  74.5 0.0 copy-done.9
  74.5 0.0 copy-done.10
  74.5 4.2 %near.1.near_ref = f32[4,8,256]{2,1,0:T(8,128)S(1)} custom-call(s32[4,8]{1,0:T(4,128)S(1)} %copy-done.9, s32[4]{0:T(128)S(1)} %copy-done.10, f32[3,1024]{1,0:T(4,128)S(1)} %copy-done.4, bf16[2,34,16,128]{3,2,1,0:T(8,128)(2,1)S(1)} %bitcast.20, bf16[2,34,16,128]{3,2,1,0:T(8,128)(2,1)S(1)} %collective-permute-done.2.beside_ref), custom_call_target="tpu_custom_call" | custom-call | flops 4000000000 | bytes 1200000 | tf_op jit(solution)/shard_map/near/pallas_call | solution.py:258
  78.7 0.0 collective-permute-done.4.beyond_ref
  78.7 0.0 collective-permute-done.3.last_mate_ref
  78.7 0.0 copy-done
  78.7 0.0 copy-done.1
  78.8 0.0 copy-done.2
  78.8 0.0 copy-done.3
  78.8 0.0 copy-done.5
  78.8 0.0 copy-done.6
  78.8 0.0 copy-done.7
  78.8 0.0 copy-done.8
  78.8 3.6 %far.1 = bf16[8,1024]{1,0:T(8,128)(2,1)} custom-call(s32[4,16]{1,0:T(4,128)S(1)} %copy-done.6, s32[4]{0:T(128)S(1)} %copy-done.7, s32[1,16]{1,0:T(1,128)S(1)} %copy-done.8, s32[1]{0:T(128)S(6)} %copy.18.coarse_count_ref, s32[1024]{0:T(1024)S(1)} %copy-done.5, bf16[14,16,128]{2,1,0:T(8,128)(2,1)S(1)} %bitcast.22, ...), custom_call_target="tpu_custom_call" | custom-call | tf_op jit(solution)/shard_map/far/pallas_call | solution.py:273
  (12 shorter events, 0.1 us)
Async XLA Ops:
  4.1 40.4 %collective-permute-start = (bf16[2,2,10,16,128]{4,3,2,1,0:T(8,128)(2,1)S(1)}, bf16[2,2,10,16,128]{4,3,2,1,0:T(8,128)(2,1)S(1)}, u32[]{:S(2)}, u32[]{:S(2)}) collective-permute-start(bf16[2,2,10,16,128]{4,3,2,1,0:T(8,128)(2,1)S(1)} %bitcast.26), channel_id=1, source_target_pairs={{1,0},{2,1},{3,2},{4,3},{5,4},{6,5},{7,6},{8,7},{9,8},{10,9},{11,1... | collective-permute-start | bytes 491528 | tf_op jit(solution)/shard_map/ppermute | solution.py:349
  22.7 25.5 %all-to-all-start = ((bf16[32,4,128]{2,1,0:T(4,128)(2,1)}), bf16[32,4,128]{2,1,0:T(4,128)(2,1)S(1)}, u32[]{:S(2)}, u32[]{:S(2)}) async-start(bf16[32,4,128]{2,1,0:T(4,128)(2,1)} %get-tuple-element.16), calls=%async_computation | async-start | bytes 65536 | tf_op jit(solution)/shard_map/all_to_all | solution.py:351
  44.5 12.2 %collective-permute-start.1 = (bf16[2,2,16,128]{3,2,1,0:T(8,128)(2,1)S(1)}, bf16[2,2,16,128]{3,2,1,0:T(8,128)(2,1)S(1)}, u32[]{:S(2)}, u32[]{:S(2)}) collective-permute-start(bf16[2,2,16,128]{3,2,1,0:T(8,128)(2,1)S(1)} %pad_maximum_fusion.4), channel_id=1, source_target_pairs={{2,0},{3,1},{4,2},{5,3},{6,4},{7,5},{8,6},{9,7},{10,8},{11,9},{12,... | collective-permute-start | bytes 49160 | tf_op jit(solution)/shard_map/ppermute | solution.py:355
  49.1 7.6 %copy-start.11 = (bf16[2,10,16,128]{3,2,1,0:T(8,128)(2,1)S(1)}, bf16[2,10,16,128]{3,2,1,0:T(8,128)(2,1)}, u32[]{:S(2)}) copy-start(bf16[2,10,16,128]{3,2,1,0:T(8,128)(2,1)} %get-tuple-element.13) | copy-start | bytes 245764
  49.1 17.1 %all-to-all-start.1 = ((bf16[16,8,16,128]{3,2,1,0:T(8,128)(2,1)}), bf16[16,8,16,128]{3,2,1,0:T(8,128)(2,1)S(1)}, u32[]{:S(2)}, u32[]{:S(2)}) async-start(bf16[16,8,16,128]{3,2,1,0:T(8,128)(2,1)} %broadcast_in_dim.8), calls=%async_computation.1 | async-start | bytes 1048576 | tf_op jit(solution)/shard_map/all_to_all | solution.py:357
  58.8 7.4 %collective-permute-start.2 = (bf16[2,34,16,128]{3,2,1,0:T(8,128)(2,1)S(1)}, bf16[2,34,16,128]{3,2,1,0:T(8,128)(2,1)S(1)}, u32[]{:S(2)}, u32[]{:S(2)}) collective-permute-start(bf16[2,34,16,128]{3,2,1,0:T(8,128)(2,1)S(1)} %bitcast.17), channel_id=1, source_target_pairs={{384,128},{0,256},{640,384},{256,512},{896,640},{512,768},{385,129... | collective-permute-start | bytes 835592 | tf_op jit(solution)/shard_map/ppermute | solution.py:363
  66.3 12.4 %collective-permute-start.3 = (bf16[142,16,128]{2,1,0:T(8,128)(2,1)S(1)}, bf16[142,16,128]{2,1,0:T(8,128)(2,1)S(1)}, u32[]{:S(2)}, u32[]{:S(2)}) collective-permute-start(bf16[142,16,128]{2,1,0:T(8,128)(2,1)S(1)} %pad_maximum_fusion.last_ref), channel_id=1, source_target_pairs={{0,128},{128,0},{1,129},{129,1},{2,130},{130,2},{3,131},{131,3},{4... | collective-permute-start | bytes 1744904 | tf_op jit(solution)/shard_map/ppermute | solution.py:370
  68.3 6.2 %copy-start.4 = (f32[3,1024]{1,0:T(4,128)S(1)}, f32[3,1024]{1,0:T(4,128)}, u32[]{:S(2)}) copy-start(f32[3,1024]{1,0:T(4,128)} %points_ref.1) | copy-start | bytes 36868
  68.3 6.2 %copy-start.9 = (s32[4,8]{1,0:T(4,128)S(1)}, s32[4,8]{1,0:T(4,128)}, u32[]{:S(2)}) copy-start(s32[4,8]{1,0:T(4,128)} %list_ref.1) | copy-start | bytes 388
  68.3 6.2 %copy-start.10 = (s32[4]{0:T(128)S(1)}, s32[4]{0:T(128)}, u32[]{:S(2)}) copy-start(s32[4]{0:T(128)} %count_ref.1) | copy-start | bytes 52
  68.3 10.4 %copy-start = (bf16[4,16,64,64]{3,2,1,0:T(8,128)(2,1)S(1)}, bf16[4,16,64,64]{3,2,1,0:T(8,128)(2,1)}, u32[]{:S(2)}) copy-start(bf16[4,16,64,64]{3,2,1,0:T(8,128)(2,1)} %leaf_coupling_ref.1) | copy-start | bytes 1572868
  68.3 10.4 %copy-start.1 = (bf16[4,256,64]{1,2,0:T(8,128)(2,1)S(1)}, bf16[4,256,64]{1,2,0:T(8,128)(2,1)}, u32[]{:S(2)}) copy-start(bf16[4,256,64]{1,2,0:T(8,128)(2,1)} %param.15) | copy-start | bytes 393220
  68.3 10.4 %copy-start.2 = (bf16[1,16,64,64]{3,2,1,0:T(8,128)(2,1)S(1)}, bf16[1,16,64,64]{3,2,1,0:T(8,128)(2,1)}, u32[]{:S(2)}) copy-start(bf16[1,16,64,64]{3,2,1,0:T(8,128)(2,1)} %coarse_coupling_ref.1) | copy-start | bytes 393220
  68.4 10.4 %copy-start.3 = (bf16[4,64,64]{2,1,0:T(8,128)(2,1)S(1)}, bf16[4,64,64]{2,1,0:T(8,128)(2,1)}, u32[]{:S(2)}) copy-start(bf16[4,64,64]{2,1,0:T(8,128)(2,1)} %transfer_ref.1) | copy-start | bytes 98308
  68.4 10.4 %copy-start.5 = (s32[1024]{0:T(1024)S(1)}, s32[1024]{0:T(1024)}, u32[]{:S(2)}) copy-start(s32[1024]{0:T(1024)} %owner_ref.1) | copy-start | bytes 12292
  68.4 10.4 %copy-start.6 = (s32[4,16]{1,0:T(4,128)S(1)}, s32[4,16]{1,0:T(4,128)}, u32[]{:S(2)}) copy-start(s32[4,16]{1,0:T(4,128)} %coupling_list_ref.1) | copy-start | bytes 772
  68.4 10.4 %copy-start.7 = (s32[4]{0:T(128)S(1)}, s32[4]{0:T(128)}, u32[]{:S(2)}) copy-start(s32[4]{0:T(128)} %coupling_count_ref.1) | copy-start | bytes 52
  68.4 10.4 %copy-start.8 = (s32[1,16]{1,0:T(1,128)S(1)}, s32[1,16]{1,0:T(1,128)}, u32[]{:S(2)}) copy-start(s32[1,16]{1,0:T(1,128)} %coarse_list_ref.1) | copy-start | bytes 196
  68.4 10.3 %collective-permute-start.4 = (bf16[14,16,128]{2,1,0:T(8,128)(2,1)S(1)}, bf16[14,16,128]{2,1,0:T(8,128)(2,1)S(1)}, u32[]{:S(2)}, u32[]{:S(2)}) collective-permute-start(bf16[14,16,128]{2,1,0:T(8,128)(2,1)S(1)} %bitcast.21), channel_id=1, source_target_pairs={{640,128},{896,384},{0,512},{256,768},{641,129},{897,385},{1,513},... | collective-permute-start | bytes 172040 | tf_op jit(solution)/shard_map/ppermute | solution.py:365

commit v8 on v7

--- a/solution.py
+++ b/solution.py
@@ -86,6 +86,7 @@
 
 
 def near_kernel(
+    base_leaf,
     cols,
     list_ref,
     count_ref,
@@ -127,8 +128,9 @@
             halves.append([jnp.broadcast_to(line, (8, 128)) for line in place])
         return sides, halves
 
-    for leaf in range(4):
-        own = points_ref[:, leaf * 256 : leaf * 256 + 256]
+    for leaf in range(2):
+        span = slice((base_leaf + leaf) * 256, (base_leaf + leaf) * 256 + 256)
+        own = points_ref[:, span]
         own = jnp.concatenate([own, jnp.zeros((5, 256), F32)], axis=0).T
         for axis in range(3):
             wide = jnp.broadcast_to(own[:, axis : axis + 1], (256, 128))
@@ -137,7 +139,7 @@
     def leaf_step(leaf, carry):
         total = jnp.zeros((8, 256), F32)
         for slot in range(8):
-            sides, halves = source_of(leaf, slot)
+            sides, halves = source_of(base_leaf + leaf, slot)
             bands = []
             for band in range(0, 32, 8):
                 tiles = []
@@ -155,7 +157,7 @@
         near_ref[leaf] = total
         return carry
 
-    lax.fori_loop(0, 4, leaf_step, 0, unroll=4)
+    lax.fori_loop(0, 2, leaf_step, 0, unroll=2)
 
 
 def couple(matrices, sources):
@@ -193,7 +195,8 @@
     coarse_coupling_ref,
     transfer_ref,
     basis_ref,
-    near_ref,
+    near_low_ref,
+    near_high_ref,
     out_ref,
     source_ref,
 ):
@@ -245,7 +248,8 @@
         mine = local[:, leaf * 64 : leaf * 64 + 64].astype(BF16)
         far_part = lax.dot_general(mine, basis_ref[leaf], NN, preferred_element_type=F32)
         span = slice(leaf * 256, leaf * 256 + 256)
-        out_ref[:, span] = (near_ref[leaf] + far_part).astype(BF16)
+        near_part = near_low_ref[leaf] if leaf < 2 else near_high_ref[leaf - 2]
+        out_ref[:, span] = (near_part + far_part).astype(BF16)
 
 
 VMEM = pl.BlockSpec(memory_space=pltpu.VMEM)
@@ -254,17 +258,17 @@
 PARAMS = pltpu.CompilerParams(vmem_limit_bytes=16 * 2**20)
 
 
-def near_call(cols, *operands):
+def near_call(base_leaf, cols, *operands):
     return pl.pallas_call(
-        functools.partial(near_kernel, cols),
-        out_shape=jax.ShapeDtypeStruct((4, 8, 256), F32),
+        functools.partial(near_kernel, base_leaf, cols),
+        out_shape=jax.ShapeDtypeStruct((2, 8, 256), F32),
         in_specs=[SMEM] * 2 + [VMEM] * 3,
         out_specs=VMEM,
-        scratch_shapes=[pltpu.VMEM((4, 3, 32, 8, 128), F32)],
+        scratch_shapes=[pltpu.VMEM((2, 3, 32, 8, 128), F32)],
         compiler_params=PARAMS,
-        name="near",
+        name=f"near{base_leaf}",
         cost_estimate=pl.CostEstimate(
-            flops=4_000_000_000, bytes_accessed=1_200_000, transcendentals=0
+            flops=100_000_000, bytes_accessed=1_200_000, transcendentals=0
         ),
     )(*operands)
 
@@ -273,7 +277,7 @@
     return pl.pallas_call(
         functools.partial(far_kernel, groups, cols, zs),
         out_shape=jax.ShapeDtypeStruct((8, 1024), BF16),
-        in_specs=[SMEM] * 5 + [VMEM] * 9,
+        in_specs=[SMEM] * 5 + [VMEM] * 10,
         out_specs=VMEM,
         scratch_shapes=[pltpu.VMEM((5, 128, 64), F32)],
         compiler_params=PARAMS,
@@ -353,6 +357,7 @@
     ).reshape(zs // 4, 16, 128)
     second = jnp.concatenate([chip[:, 0, 9:], first[:, 9:]], axis=1)
     second = lax.ppermute(second, ("core", "y", "z"), along_col(2))
+    first, line = lax.optimization_barrier((first, line))
     line = jnp.broadcast_to(line[None], (xs * ys,) + line.shape)
     same = lax.all_to_all(line, ("x", "y"), 0, 0, tiled=True).reshape(groups, 16, 128)
 
@@ -363,10 +368,11 @@
     beside = lax.ppermute(window, ("x", "core"), along_x(1))
     coeffs = coeffs_of(window)
     beyond = lax.ppermute(coeffs, ("x", "core"), along_x(2))
-    same, beside = lax.optimization_barrier((same, beside))
+    near_low = near_call(0, cols, near_list, near_count, points, window, beside)
+    same, beside, beyond, near_low = lax.optimization_barrier((same, beside, beyond, near_low))
     last = jnp.concatenate([same, coeffs_of(beside)], axis=0)
     last, beside = lax.optimization_barrier((last, beside))
-    near = near_call(cols, near_list, near_count, points, window, beside)
+    near_high = near_call(2, cols, near_list, near_count, points, window, beside)
     last_mate = lax.ppermute(last, "core", [(0, 1), (1, 0)])
 
     return far_call(
@@ -386,7 +392,8 @@
         coarse_coupling,
         transfer,
         basis,
-        near,
+        near_low,
+        near_high,
     )
 
 

time: 82.9 us -> 80.5 us (0.971)
  the two profiles are of different devices: /device:TPU:8 before, /device:TPU:1 now
where the time goes in v8:
time: 80.5 us; the launch traced here: 80 us
  starting transfers between devices  39.5 us (49%)
  blocking collectives  22 us (27%)
  Pallas kernels  10.7 us (13%)
  waiting for transfers between devices  5.8 us (7%)
  local copies, waits for them, and re-layouts  1.01 us (1%)
  between operations  1 us (1%)
    all_to_all x1, starting transfers between devices, per_device(): lax.all_to_all(cluster, 'z', 0, 0, tiled=True, axis_index_groups=[turned])  23.6 us
    all_gather x1, blocking collectives, per_device(): chip = lax.all_gather(blocks, 'core', axis=0, tiled=False)  15.9 us
    all_to_all x1, starting transfers between devices, per_device(): lax.all_to_all(line, ('x', 'y'), 0, 0, tiled=True).reshape(groups, 16, 128)  6.75 us
    all_gather x1, blocking collectives, per_device(): window = lax.all_gather(window, 'core', axis=0, tiled=False)  6.02 us
    pallas_call x2, Pallas kernels, near_call(): pl.pallas_call(functools.partial(near_kernel, base_leaf, cols), out_shape...  5.12 us
    ppermute x1, waiting for transfers between devices, per_device(): beside = lax.ppermute(window, ('x', 'core'), along_x(1))  5.11 us
    pallas_call x1, Pallas kernels, far_call(): pl.pallas_call(functools.partial(far_kernel, groups, cols, zs), out_shape...  3.6 us
    ppermute x1, starting transfers between devices, per_device(): last_mate = lax.ppermute(last, 'core', [(0, 1), (1, 0)])  3.15 us
  transfers between devices with their start and end apart: 7, of which 2 were waited for; matrix products, arithmetic and copies ran while one was open for 1% of the time, Pallas kernels for 6%

profile of v8, /device:TPU:1, one launch (start us, length us, event | category | flops | bytes accessed | tf_op | source)
XLA Modules:
  0.0 80.0 jit_solution(11711162404765548307)
XLA Ops:
  0.0 1.9 %pack.1 = (bf16[2,10,16,128]{3,2,1,0:T(8,128)(2,1)}, bf16[32,4,128]{2,1,0:T(4,128)(2,1)}) custom-call(bf16[8,1024]{1,0:T(8,128)(2,1)} %rhs_hbm.1, f32[3,1024]{1,0:T(4,128)} %points_ref.3, bf16[4,64,256]{2,1,0:T(8,128)(2,1)} %bitcast.20, bf16[4,64,64]{2,1,0:T(8,128)(2,1)} %transfer_ref.1), custom_call_target="tpu_custom_call" | custom-call | tf_op jit(solution)/shard_map/pack/pallas_call | solution.py:312
  1.9 15.9 %all-gather = bf16[4,10,16,128]{3,2,1,0:T(8,128)(2,1)S(1)} all-gather(bf16[2,10,16,128]{3,2,1,0:T(8,128)(2,1)} %get-tuple-element.17), channel_id=2, replica_groups=mesh['x'=4,'core'=2,'y'=4,'z'=32] {'core'}, dimensions={0}, use_global_device_ids=true | all-gather | bytes 245760 | tf_op jit(solution)/shard_map/all_gather | solution.py:352
  17.9 1.3 %collective-permute-start = (bf16[2,2,10,16,128]{4,3,2,1,0:T(8,128)(2,1)S(1)}, bf16[2,2,10,16,128]{4,3,2,1,0:T(8,128)(2,1)S(1)}, u32[]{:S(2)}, u32[]{:S(2)}) collective-permute-start(bf16[2,2,10,16,128]{4,3,2,1,0:T(8,128)(2,1)S(1)} %bitcast.27), channel_id=1, source_target_pairs={{1,0},{2,1},{3,2},{4,3},{5,4},{6,5},{7,6},{8,7},{9,8},{10,9},{11,1... | collective-permute-start | bytes 491528 | tf_op jit(solution)/shard_map/ppermute | solution.py:353
  19.2 23.6 %all-to-all-start = ((bf16[32,4,128]{2,1,0:T(4,128)(2,1)}), bf16[32,4,128]{2,1,0:T(4,128)(2,1)S(1)}, u32[]{:S(2)}, u32[]{:S(2)}) async-start(bf16[32,4,128]{2,1,0:T(4,128)(2,1)} %get-tuple-element.19), calls=%async_computation | async-start | bytes 65536 | tf_op jit(solution)/shard_map/all_to_all | solution.py:355
  42.8 0.0 copy-start.11
  42.8 0.0 collective-permute-done
  42.8 2.2 %collective-permute-start.1 = (bf16[2,2,16,128]{3,2,1,0:T(8,128)(2,1)S(1)}, bf16[2,2,16,128]{3,2,1,0:T(8,128)(2,1)S(1)}, u32[]{:S(2)}, u32[]{:S(2)}) collective-permute-start(bf16[2,2,16,128]{3,2,1,0:T(8,128)(2,1)S(1)} %pad_maximum_fusion.4), channel_id=1, source_target_pairs={{2,0},{3,1},{4,2},{5,3},{6,4},{7,5},{8,6},{9,7},{10,8},{11,9},{12,... | collective-permute-start | bytes 49160 | tf_op jit(solution)/shard_map/ppermute | solution.py:359
  45.0 0.0 copy-done.11
  45.1 0.7 all-to-all-done
  45.7 0.9 %broadcast_in_dim.2 = bf16[16,8,16,128]{3,2,1,0:T(8,128)(2,1)} broadcast(bf16[8,16,128]{2,1,0:T(8,128)(2,1)S(1)} %bitcast.29), dimensions={1,2,3} | broadcast | bytes 557056 | tf_op jit(solution)/shard_map/broadcast_in_dim | solution.py:361
  46.6 6.8 %all-to-all-start.1 = ((bf16[16,8,16,128]{3,2,1,0:T(8,128)(2,1)}), bf16[16,8,16,128]{3,2,1,0:T(8,128)(2,1)S(1)}, u32[]{:S(2)}, u32[]{:S(2)}) async-start(bf16[16,8,16,128]{3,2,1,0:T(8,128)(2,1)} %broadcast_in_dim.2), calls=%async_computation.1 | async-start | bytes 1048576 | tf_op jit(solution)/shard_map/all_to_all | solution.py:362
  53.4 0.0 collective-permute-done.1
  53.4 6.0 %all-gather.1 = bf16[68,16,128]{2,1,0:T(8,128)(2,1)S(1)} all-gather(bf16[34,16,128]{2,1,0:T(8,128)(2,1)S(1)} %pad_maximum_fusion.1), channel_id=3, replica_groups=mesh['x'=4,'core'=2,'y'=4,'z'=32] {'core'}, dimensions={0}, use_global_device_ids=true | all-gather | bytes 417792 | tf_op jit(solution)/shard_map/all_gather | solution.py:367
  59.5 1.3 %collective-permute-start.2 = (bf16[2,34,16,128]{3,2,1,0:T(8,128)(2,1)S(1)}, bf16[2,34,16,128]{3,2,1,0:T(8,128)(2,1)S(1)}, u32[]{:S(2)}, u32[]{:S(2)}) collective-permute-start(bf16[2,34,16,128]{3,2,1,0:T(8,128)(2,1)S(1)} %bitcast.16), channel_id=1, source_target_pairs={{384,128},{0,256},{640,384},{256,512},{896,640},{512,768},{385,129... | collective-permute-start | bytes 835592 | tf_op jit(solution)/shard_map/ppermute | solution.py:368
  60.8 0.0 copy-start.4
  60.8 0.0 copy-start.5
  60.8 0.0 copy-start.8
  60.8 1.3 %collective-permute-start.3 = (bf16[14,16,128]{2,1,0:T(8,128)(2,1)S(1)}, bf16[14,16,128]{2,1,0:T(8,128)(2,1)S(1)}, u32[]{:S(2)}, u32[]{:S(2)}) collective-permute-start(bf16[14,16,128]{2,1,0:T(8,128)(2,1)S(1)} %bitcast.22), channel_id=1, source_target_pairs={{640,128},{896,384},{0,512},{256,768},{641,129},{897,385},{1,513},... | collective-permute-start | bytes 172040 | tf_op jit(solution)/shard_map/ppermute | solution.py:370
  62.1 5.1 %collective-permute-done.2.beside_ref = bf16[2,34,16,128]{3,2,1,0:T(8,128)(2,1)S(1)} collective-permute-done((bf16[2,34,16,128]{3,2,1,0:T(8,128)(2,1)S(1)}, bf16[2,34,16,128]{3,2,1,0:T(8,128)(2,1)S(1)}, u32[]{:S(2)}, u32[]{:S(2)}) %collective-permute-start.2) | collective-permute-done | bytes 278560 | tf_op jit(solution)/shard_map/ppermute | solution.py:368
  67.2 0.0 copy-done.4
  67.2 0.0 copy-done.5
  67.2 0.0 copy-done.8
  67.2 2.6 %near0.1.near_low_ref = f32[2,8,256]{2,1,0:T(8,128)S(1)} custom-call(s32[4,8]{1,0:T(4,128)S(1)} %copy-done.5, s32[4]{0:T(128)S(1)} %copy-done.8, f32[3,1024]{1,0:T(4,128)S(1)} %copy-done.4, bf16[2,34,16,128]{3,2,1,0:T(8,128)(2,1)S(1)} %bitcast.18, bf16[2,34,16,128]{3,2,1,0:T(8,128)(2,1)S(1)} %collective-permute-done.2.beside_ref), custom_call_target="tpu_custom_call" | custom-call | flops 100000000 | bytes 1200000 | tf_op jit(solution)/shard_map/near0/pallas_call | solution.py:262
  69.8 0.0 copy-start
  69.8 0.0 collective-permute-done.3.beyond_ref
  69.8 0.0 all-to-all-done.1
  69.9 0.1 pad_maximum_fusion.last_ref
  69.9 3.2 %collective-permute-start.4 = (bf16[142,16,128]{2,1,0:T(8,128)(2,1)S(1)}, bf16[142,16,128]{2,1,0:T(8,128)(2,1)S(1)}, u32[]{:S(2)}, u32[]{:S(2)}) collective-permute-start(bf16[142,16,128]{2,1,0:T(8,128)(2,1)S(1)} %pad_maximum_fusion.last_ref), channel_id=1, source_target_pairs={{0,128},{128,0},{1,129},{129,1},{2,130},{130,2},{3,131},{131,3},{4... | collective-permute-start | bytes 1744904 | tf_op jit(solution)/shard_map/ppermute | solution.py:376
  73.7 0.0 copy-start.1
  73.7 0.0 copy-start.2
  73.7 0.0 copy-start.3
  73.8 0.0 copy-start.6
  73.8 0.0 copy-start.7
  73.8 0.0 copy-start.9
  73.8 0.0 copy-start.10
  73.8 2.6 %near2.1.near_high_ref = f32[2,8,256]{2,1,0:T(8,128)S(1)} custom-call(s32[4,8]{1,0:T(4,128)S(1)} %copy-done.5, s32[4]{0:T(128)S(1)} %copy-done.8, f32[3,1024]{1,0:T(4,128)S(1)} %copy-done.4, bf16[2,34,16,128]{3,2,1,0:T(8,128)(2,1)S(1)} %bitcast.19, bf16[2,34,16,128]{3,2,1,0:T(8,128)(2,1)S(1)} %collective-permute-done.2.beside_ref), custom_call_target="tpu_custom_call" | custom-call | flops 100000000 | bytes 1200000 | tf_op jit(solution)/shard_map/near2/pallas_call | solution.py:262
  76.4 0.0 collective-permute-done.4.last_mate_ref
  76.4 0.0 copy-done
  76.4 0.0 copy-done.1
  76.4 0.0 copy-done.2
  76.4 0.0 copy-done.3
  76.4 0.0 copy-done.6
  76.4 0.0 copy-done.7
  76.4 0.0 copy-done.9
  76.4 0.0 copy-done.10
  76.4 3.6 %far.1 = bf16[8,1024]{1,0:T(8,128)(2,1)} custom-call(s32[4,16]{1,0:T(4,128)S(1)} %copy-done.7, s32[4]{0:T(128)S(1)} %copy-done.9, s32[1,16]{1,0:T(1,128)S(1)} %copy-done.10, s32[1]{0:T(128)S(6)} %copy.18.coarse_count_ref, s32[1024]{0:T(1024)S(1)} %copy-done.6, bf16[14,16,128]{2,1,0:T(8,128)(2,1)S(1)} %bitcast.23, ...), custom_call_target="tpu_custom_call" | custom-call | tf_op jit(solution)/shard_map/far/pallas_call | solution.py:277
  (12 shorter events, 0.1 us)
Async XLA Ops:
  17.9 24.9 %collective-permute-start = (bf16[2,2,10,16,128]{4,3,2,1,0:T(8,128)(2,1)S(1)}, bf16[2,2,10,16,128]{4,3,2,1,0:T(8,128)(2,1)S(1)}, u32[]{:S(2)}, u32[]{:S(2)}) collective-permute-start(bf16[2,2,10,16,128]{4,3,2,1,0:T(8,128)(2,1)S(1)} %bitcast.27), channel_id=1, source_target_pairs={{1,0},{2,1},{3,2},{4,3},{5,4},{6,5},{7,6},{8,7},{9,8},{10,9},{11,1... | collective-permute-start | bytes 491528 | tf_op jit(solution)/shard_map/ppermute | solution.py:353
  19.2 26.5 %all-to-all-start = ((bf16[32,4,128]{2,1,0:T(4,128)(2,1)}), bf16[32,4,128]{2,1,0:T(4,128)(2,1)S(1)}, u32[]{:S(2)}, u32[]{:S(2)}) async-start(bf16[32,4,128]{2,1,0:T(4,128)(2,1)} %get-tuple-element.19), calls=%async_computation | async-start | bytes 65536 | tf_op jit(solution)/shard_map/all_to_all | solution.py:355
  42.8 2.3 %copy-start.11 = (bf16[2,10,16,128]{3,2,1,0:T(8,128)(2,1)S(1)}, bf16[2,10,16,128]{3,2,1,0:T(8,128)(2,1)}, u32[]{:S(2)}) copy-start(bf16[2,10,16,128]{3,2,1,0:T(8,128)(2,1)} %get-tuple-element.17) | copy-start | bytes 245764
  42.8 10.6 %collective-permute-start.1 = (bf16[2,2,16,128]{3,2,1,0:T(8,128)(2,1)S(1)}, bf16[2,2,16,128]{3,2,1,0:T(8,128)(2,1)S(1)}, u32[]{:S(2)}, u32[]{:S(2)}) collective-permute-start(bf16[2,2,16,128]{3,2,1,0:T(8,128)(2,1)S(1)} %pad_maximum_fusion.4), channel_id=1, source_target_pairs={{2,0},{3,1},{4,2},{5,3},{6,4},{7,5},{8,6},{9,7},{10,8},{11,9},{12,... | collective-permute-start | bytes 49160 | tf_op jit(solution)/shard_map/ppermute | solution.py:359
  46.6 23.2 %all-to-all-start.1 = ((bf16[16,8,16,128]{3,2,1,0:T(8,128)(2,1)}), bf16[16,8,16,128]{3,2,1,0:T(8,128)(2,1)S(1)}, u32[]{:S(2)}, u32[]{:S(2)}) async-start(bf16[16,8,16,128]{3,2,1,0:T(8,128)(2,1)} %broadcast_in_dim.2), calls=%async_computation.1 | async-start | bytes 1048576 | tf_op jit(solution)/shard_map/all_to_all | solution.py:362
  59.5 7.8 %collective-permute-start.2 = (bf16[2,34,16,128]{3,2,1,0:T(8,128)(2,1)S(1)}, bf16[2,34,16,128]{3,2,1,0:T(8,128)(2,1)S(1)}, u32[]{:S(2)}, u32[]{:S(2)}) collective-permute-start(bf16[2,34,16,128]{3,2,1,0:T(8,128)(2,1)S(1)} %bitcast.16), channel_id=1, source_target_pairs={{384,128},{0,256},{640,384},{256,512},{896,640},{512,768},{385,129... | collective-permute-start | bytes 835592 | tf_op jit(solution)/shard_map/ppermute | solution.py:368
  60.8 6.5 %copy-start.4 = (f32[3,1024]{1,0:T(4,128)S(1)}, f32[3,1024]{1,0:T(4,128)}, u32[]{:S(2)}) copy-start(f32[3,1024]{1,0:T(4,128)} %points_ref.3) | copy-start | bytes 36868
  60.8 6.5 %copy-start.5 = (s32[4,8]{1,0:T(4,128)S(1)}, s32[4,8]{1,0:T(4,128)}, u32[]{:S(2)}) copy-start(s32[4,8]{1,0:T(4,128)} %list_ref.3) | copy-start | bytes 388
  60.8 6.4 %copy-start.8 = (s32[4]{0:T(128)S(1)}, s32[4]{0:T(128)}, u32[]{:S(2)}) copy-start(s32[4]{0:T(128)} %count_ref.3) | copy-start | bytes 52
  60.8 9.0 %collective-permute-start.3 = (bf16[14,16,128]{2,1,0:T(8,128)(2,1)S(1)}, bf16[14,16,128]{2,1,0:T(8,128)(2,1)S(1)}, u32[]{:S(2)}, u32[]{:S(2)}) collective-permute-start(bf16[14,16,128]{2,1,0:T(8,128)(2,1)S(1)} %bitcast.22), channel_id=1, source_target_pairs={{640,128},{896,384},{0,512},{256,768},{641,129},{897,385},{1,513},... | collective-permute-start | bytes 172040 | tf_op jit(solution)/shard_map/ppermute | solution.py:370
  69.8 6.6 %copy-start = (bf16[4,16,64,64]{3,2,1,0:T(8,128)(2,1)S(1)}, bf16[4,16,64,64]{3,2,1,0:T(8,128)(2,1)}, u32[]{:S(2)}) copy-start(bf16[4,16,64,64]{3,2,1,0:T(8,128)(2,1)} %leaf_coupling_ref.1) | copy-start | bytes 1572868
  69.9 6.5 %collective-permute-start.4 = (bf16[142,16,128]{2,1,0:T(8,128)(2,1)S(1)}, bf16[142,16,128]{2,1,0:T(8,128)(2,1)S(1)}, u32[]{:S(2)}, u32[]{:S(2)}) collective-permute-start(bf16[142,16,128]{2,1,0:T(8,128)(2,1)S(1)} %pad_maximum_fusion.last_ref), channel_id=1, source_target_pairs={{0,128},{128,0},{1,129},{129,1},{2,130},{130,2},{3,131},{131,3},{4... | collective-permute-start | bytes 1744904 | tf_op jit(solution)/shard_map/ppermute | solution.py:376
  73.7 2.7 %copy-start.1 = (bf16[4,256,64]{1,2,0:T(8,128)(2,1)S(1)}, bf16[4,256,64]{1,2,0:T(8,128)(2,1)}, u32[]{:S(2)}) copy-start(bf16[4,256,64]{1,2,0:T(8,128)(2,1)} %param.15) | copy-start | bytes 393220
  73.7 2.7 %copy-start.2 = (bf16[1,16,64,64]{3,2,1,0:T(8,128)(2,1)S(1)}, bf16[1,16,64,64]{3,2,1,0:T(8,128)(2,1)}, u32[]{:S(2)}) copy-start(bf16[1,16,64,64]{3,2,1,0:T(8,128)(2,1)} %coarse_coupling_ref.1) | copy-start | bytes 393220
  73.7 2.7 %copy-start.3 = (bf16[4,64,64]{2,1,0:T(8,128)(2,1)S(1)}, bf16[4,64,64]{2,1,0:T(8,128)(2,1)}, u32[]{:S(2)}) copy-start(bf16[4,64,64]{2,1,0:T(8,128)(2,1)} %transfer_ref.1) | copy-start | bytes 98308
  73.8 2.7 %copy-start.6 = (s32[1024]{0:T(1024)S(1)}, s32[1024]{0:T(1024)}, u32[]{:S(2)}) copy-start(s32[1024]{0:T(1024)} %owner_ref.1) | copy-start | bytes 12292
  73.8 2.7 %copy-start.7 = (s32[4,16]{1,0:T(4,128)S(1)}, s32[4,16]{1,0:T(4,128)}, u32[]{:S(2)}) copy-start(s32[4,16]{1,0:T(4,128)} %coupling_list_ref.1) | copy-start | bytes 772
  73.8 2.6 %copy-start.9 = (s32[4]{0:T(128)S(1)}, s32[4]{0:T(128)}, u32[]{:S(2)}) copy-start(s32[4]{0:T(128)} %coupling_count_ref.1) | copy-start | bytes 52
  73.8 2.6 %copy-start.10 = (s32[1,16]{1,0:T(1,128)S(1)}, s32[1,16]{1,0:T(1,128)}, u32[]{:S(2)}) copy-start(s32[1,16]{1,0:T(1,128)} %coarse_list_ref.1) | copy-start | bytes 196

commit v9 on v8

--- a/solution.py
+++ b/solution.py
@@ -29,21 +29,20 @@
 
 
 def pack_kernel(
-    rhs_hbm,
+    rhs_ref,
     points_hbm,
     basis_hbm,
     transfer_hbm,
     copies_ref,
     cluster_ref,
-    rhs_ref,
     points_ref,
     basis_ref,
     transfer_ref,
     done_ref,
 ):
     fetch_all(
-        (rhs_hbm, points_hbm, basis_hbm, transfer_hbm),
-        (rhs_ref, points_ref, basis_ref, transfer_ref),
+        (points_hbm, basis_hbm, transfer_hbm),
+        (points_ref, basis_ref, transfer_ref),
         done_ref,
     )
     block_ref = copies_ref.at[0]
@@ -315,14 +314,13 @@
             jax.ShapeDtypeStruct((2, BLOCK, 16, 128), BF16),
             jax.ShapeDtypeStruct((zs, 4, 128), BF16),
         ),
-        in_specs=[ANY] * 4,
+        in_specs=[VMEM] + [ANY] * 3,
         out_specs=(VMEM, VMEM),
         scratch_shapes=[
-            pltpu.VMEM(rhs.shape, BF16),
             pltpu.VMEM(points.shape, F32),
             pltpu.VMEM(basis.shape, BF16),
             pltpu.VMEM(transfer.shape, BF16),
-            pltpu.SemaphoreType.DMA((4,)),
+            pltpu.SemaphoreType.DMA((3,)),
         ],
         name="pack",
     )(rhs, points, basis, transfer)

time: 80.5 us -> 81.3 us (level)
  no operation moved by 1% of the time
where the time goes in v9:
time: 81.3 us; the launch traced here: 80.7 us
  starting transfers between devices  39.5 us (49%)
  blocking collectives  22 us (27%)
  Pallas kernels  11.3 us (14%)
  waiting for transfers between devices  5.8 us (7%)
  local copies, waits for them, and re-layouts  1.01 us (1%)
  between operations  1 us (1%)
    all_to_all x1, starting transfers between devices, per_device(): lax.all_to_all(cluster, 'z', 0, 0, tiled=True, axis_index_groups=[turned])  23.6 us
    all_gather x1, blocking collectives, per_device(): chip = lax.all_gather(blocks, 'core', axis=0, tiled=False)  15.9 us
    all_to_all x1, starting transfers between devices, per_device(): lax.all_to_all(line, ('x', 'y'), 0, 0, tiled=True).reshape(groups, 16, 128)  6.75 us
    all_gather x1, blocking collectives, per_device(): window = lax.all_gather(window, 'core', axis=0, tiled=False)  6.02 us
    pallas_call x2, Pallas kernels, near_call(): pl.pallas_call(functools.partial(near_kernel, base_leaf, cols), out_shape...  5.12 us
    ppermute x1, waiting for transfers between devices, per_device(): beside = lax.ppermute(window, ('x', 'core'), along_x(1))  5.11 us
    pallas_call x1, Pallas kernels, far_call(): pl.pallas_call(functools.partial(far_kernel, groups, cols, zs), out_shape...  3.6 us
    ppermute x1, starting transfers between devices, per_device(): last_mate = lax.ppermute(last, 'core', [(0, 1), (1, 0)])  3.15 us
  transfers between devices with their start and end apart: 7, of which 2 were waited for; matrix products, arithmetic and copies ran while one was open for 1% of the time, Pallas kernels for 6%

profile of v9, /device:TPU:1, one launch (start us, length us, event | category | flops | bytes accessed | tf_op | source)
XLA Modules:
  0.0 80.7 jit_solution(5953819063522085641)
XLA Ops:
  0.0 2.6 %pack.1 = (bf16[2,10,16,128]{3,2,1,0:T(8,128)(2,1)}, bf16[32,4,128]{2,1,0:T(4,128)(2,1)}) custom-call(bf16[8,1024]{1,0:T(8,128)(2,1)} %rhs_ref.1, f32[3,1024]{1,0:T(4,128)} %points_ref.3, bf16[4,64,256]{2,1,0:T(8,128)(2,1)} %bitcast.20, bf16[4,64,64]{2,1,0:T(8,128)(2,1)} %transfer_ref.1), custom_call_target="tpu_custom_call" | custom-call | tf_op jit(solution)/shard_map/pack/pallas_call | solution.py:311
  2.6 15.9 %all-gather = bf16[4,10,16,128]{3,2,1,0:T(8,128)(2,1)S(1)} all-gather(bf16[2,10,16,128]{3,2,1,0:T(8,128)(2,1)} %get-tuple-element.17), channel_id=2, replica_groups=mesh['x'=4,'core'=2,'y'=4,'z'=32] {'core'}, dimensions={0}, use_global_device_ids=true | all-gather | bytes 245760 | tf_op jit(solution)/shard_map/all_gather | solution.py:350
  18.6 1.3 %collective-permute-start = (bf16[2,2,10,16,128]{4,3,2,1,0:T(8,128)(2,1)S(1)}, bf16[2,2,10,16,128]{4,3,2,1,0:T(8,128)(2,1)S(1)}, u32[]{:S(2)}, u32[]{:S(2)}) collective-permute-start(bf16[2,2,10,16,128]{4,3,2,1,0:T(8,128)(2,1)S(1)} %bitcast.27), channel_id=1, source_target_pairs={{1,0},{2,1},{3,2},{4,3},{5,4},{6,5},{7,6},{8,7},{9,8},{10,9},{11,1... | collective-permute-start | bytes 491528 | tf_op jit(solution)/shard_map/ppermute | solution.py:351
  19.9 23.6 %all-to-all-start = ((bf16[32,4,128]{2,1,0:T(4,128)(2,1)}), bf16[32,4,128]{2,1,0:T(4,128)(2,1)S(1)}, u32[]{:S(2)}, u32[]{:S(2)}) async-start(bf16[32,4,128]{2,1,0:T(4,128)(2,1)} %get-tuple-element.19), calls=%async_computation | async-start | bytes 65536 | tf_op jit(solution)/shard_map/all_to_all | solution.py:353
  43.5 0.0 copy-start.11
  43.5 0.0 collective-permute-done
  43.5 2.2 %collective-permute-start.1 = (bf16[2,2,16,128]{3,2,1,0:T(8,128)(2,1)S(1)}, bf16[2,2,16,128]{3,2,1,0:T(8,128)(2,1)S(1)}, u32[]{:S(2)}, u32[]{:S(2)}) collective-permute-start(bf16[2,2,16,128]{3,2,1,0:T(8,128)(2,1)S(1)} %pad_maximum_fusion.4), channel_id=1, source_target_pairs={{2,0},{3,1},{4,2},{5,3},{6,4},{7,5},{8,6},{9,7},{10,8},{11,9},{12,... | collective-permute-start | bytes 49160 | tf_op jit(solution)/shard_map/ppermute | solution.py:357
  45.7 0.0 copy-done.11
  45.7 0.7 all-to-all-done
  46.4 0.9 %broadcast_in_dim.2 = bf16[16,8,16,128]{3,2,1,0:T(8,128)(2,1)} broadcast(bf16[8,16,128]{2,1,0:T(8,128)(2,1)S(1)} %bitcast.29), dimensions={1,2,3} | broadcast | bytes 557056 | tf_op jit(solution)/shard_map/broadcast_in_dim | solution.py:359
  47.3 6.8 %all-to-all-start.1 = ((bf16[16,8,16,128]{3,2,1,0:T(8,128)(2,1)}), bf16[16,8,16,128]{3,2,1,0:T(8,128)(2,1)S(1)}, u32[]{:S(2)}, u32[]{:S(2)}) async-start(bf16[16,8,16,128]{3,2,1,0:T(8,128)(2,1)} %broadcast_in_dim.2), calls=%async_computation.1 | async-start | bytes 1048576 | tf_op jit(solution)/shard_map/all_to_all | solution.py:360
  54.1 0.0 collective-permute-done.1
  54.1 6.0 %all-gather.1 = bf16[68,16,128]{2,1,0:T(8,128)(2,1)S(1)} all-gather(bf16[34,16,128]{2,1,0:T(8,128)(2,1)S(1)} %pad_maximum_fusion.1), channel_id=3, replica_groups=mesh['x'=4,'core'=2,'y'=4,'z'=32] {'core'}, dimensions={0}, use_global_device_ids=true | all-gather | bytes 417792 | tf_op jit(solution)/shard_map/all_gather | solution.py:365
  60.1 1.3 %collective-permute-start.2 = (bf16[2,34,16,128]{3,2,1,0:T(8,128)(2,1)S(1)}, bf16[2,34,16,128]{3,2,1,0:T(8,128)(2,1)S(1)}, u32[]{:S(2)}, u32[]{:S(2)}) collective-permute-start(bf16[2,34,16,128]{3,2,1,0:T(8,128)(2,1)S(1)} %bitcast.16), channel_id=1, source_target_pairs={{384,128},{0,256},{640,384},{256,512},{896,640},{512,768},{385,129... | collective-permute-start | bytes 835592 | tf_op jit(solution)/shard_map/ppermute | solution.py:366
  61.4 0.0 copy-start.4
  61.5 0.0 copy-start.5
  61.5 0.0 copy-start.8
  61.5 1.3 %collective-permute-start.3 = (bf16[14,16,128]{2,1,0:T(8,128)(2,1)S(1)}, bf16[14,16,128]{2,1,0:T(8,128)(2,1)S(1)}, u32[]{:S(2)}, u32[]{:S(2)}) collective-permute-start(bf16[14,16,128]{2,1,0:T(8,128)(2,1)S(1)} %bitcast.22), channel_id=1, source_target_pairs={{640,128},{896,384},{0,512},{256,768},{641,129},{897,385},{1,513},... | collective-permute-start | bytes 172040 | tf_op jit(solution)/shard_map/ppermute | solution.py:368
  62.8 5.1 %collective-permute-done.2.beside_ref = bf16[2,34,16,128]{3,2,1,0:T(8,128)(2,1)S(1)} collective-permute-done((bf16[2,34,16,128]{3,2,1,0:T(8,128)(2,1)S(1)}, bf16[2,34,16,128]{3,2,1,0:T(8,128)(2,1)S(1)}, u32[]{:S(2)}, u32[]{:S(2)}) %collective-permute-start.2) | collective-permute-done | bytes 278560 | tf_op jit(solution)/shard_map/ppermute | solution.py:366
  67.9 0.0 copy-done.4
  67.9 0.0 copy-done.5
  67.9 0.0 copy-done.8
  67.9 2.6 %near0.1.near_low_ref = f32[2,8,256]{2,1,0:T(8,128)S(1)} custom-call(s32[4,8]{1,0:T(4,128)S(1)} %copy-done.5, s32[4]{0:T(128)S(1)} %copy-done.8, f32[3,1024]{1,0:T(4,128)S(1)} %copy-done.4, bf16[2,34,16,128]{3,2,1,0:T(8,128)(2,1)S(1)} %bitcast.18, bf16[2,34,16,128]{3,2,1,0:T(8,128)(2,1)S(1)} %collective-permute-done.2.beside_ref), custom_call_target="tpu_custom_call" | custom-call | flops 100000000 | bytes 1200000 | tf_op jit(solution)/shard_map/near0/pallas_call | solution.py:261
  70.5 0.0 copy-start
  70.5 0.0 collective-permute-done.3.beyond_ref
  70.5 0.0 all-to-all-done.1
  70.5 0.1 pad_maximum_fusion.last_ref
  70.6 3.2 %collective-permute-start.4 = (bf16[142,16,128]{2,1,0:T(8,128)(2,1)S(1)}, bf16[142,16,128]{2,1,0:T(8,128)(2,1)S(1)}, u32[]{:S(2)}, u32[]{:S(2)}) collective-permute-start(bf16[142,16,128]{2,1,0:T(8,128)(2,1)S(1)} %pad_maximum_fusion.last_ref), channel_id=1, source_target_pairs={{0,128},{128,0},{1,129},{129,1},{2,130},{130,2},{3,131},{131,3},{4... | collective-permute-start | bytes 1744904 | tf_op jit(solution)/shard_map/ppermute | solution.py:374
  74.4 0.0 copy-start.1
  74.4 0.0 copy-start.2
  74.4 0.0 copy-start.3
  74.4 0.0 copy-start.6
  74.5 0.0 copy-start.7
  74.5 0.0 copy-start.9
  74.5 0.0 copy-start.10
  74.5 2.6 %near2.1.near_high_ref = f32[2,8,256]{2,1,0:T(8,128)S(1)} custom-call(s32[4,8]{1,0:T(4,128)S(1)} %copy-done.5, s32[4]{0:T(128)S(1)} %copy-done.8, f32[3,1024]{1,0:T(4,128)S(1)} %copy-done.4, bf16[2,34,16,128]{3,2,1,0:T(8,128)(2,1)S(1)} %bitcast.19, bf16[2,34,16,128]{3,2,1,0:T(8,128)(2,1)S(1)} %collective-permute-done.2.beside_ref), custom_call_target="tpu_custom_call" | custom-call | flops 100000000 | bytes 1200000 | tf_op jit(solution)/shard_map/near2/pallas_call | solution.py:261
  77.1 0.0 collective-permute-done.4.last_mate_ref
  77.1 0.0 copy-done
  77.1 0.0 copy-done.1
  77.1 0.0 copy-done.2
  77.1 0.0 copy-done.3
  77.1 0.0 copy-done.6
  77.1 0.0 copy-done.7
  77.1 0.0 copy-done.9
  77.1 0.0 copy-done.10
  77.1 3.6 %far.1 = bf16[8,1024]{1,0:T(8,128)(2,1)} custom-call(s32[4,16]{1,0:T(4,128)S(1)} %copy-done.7, s32[4]{0:T(128)S(1)} %copy-done.9, s32[1,16]{1,0:T(1,128)S(1)} %copy-done.10, s32[1]{0:T(128)S(6)} %copy.18.coarse_count_ref, s32[1024]{0:T(1024)S(1)} %copy-done.6, bf16[14,16,128]{2,1,0:T(8,128)(2,1)S(1)} %bitcast.23, ...), custom_call_target="tpu_custom_call" | custom-call | tf_op jit(solution)/shard_map/far/pallas_call | solution.py:276
  (12 shorter events, 0.1 us)
Async XLA Ops:
  18.6 24.9 %collective-permute-start = (bf16[2,2,10,16,128]{4,3,2,1,0:T(8,128)(2,1)S(1)}, bf16[2,2,10,16,128]{4,3,2,1,0:T(8,128)(2,1)S(1)}, u32[]{:S(2)}, u32[]{:S(2)}) collective-permute-start(bf16[2,2,10,16,128]{4,3,2,1,0:T(8,128)(2,1)S(1)} %bitcast.27), channel_id=1, source_target_pairs={{1,0},{2,1},{3,2},{4,3},{5,4},{6,5},{7,6},{8,7},{9,8},{10,9},{11,1... | collective-permute-start | bytes 491528 | tf_op jit(solution)/shard_map/ppermute | solution.py:351
  19.9 26.5 %all-to-all-start = ((bf16[32,4,128]{2,1,0:T(4,128)(2,1)}), bf16[32,4,128]{2,1,0:T(4,128)(2,1)S(1)}, u32[]{:S(2)}, u32[]{:S(2)}) async-start(bf16[32,4,128]{2,1,0:T(4,128)(2,1)} %get-tuple-element.19), calls=%async_computation | async-start | bytes 65536 | tf_op jit(solution)/shard_map/all_to_all | solution.py:353
  43.5 2.3 %copy-start.11 = (bf16[2,10,16,128]{3,2,1,0:T(8,128)(2,1)S(1)}, bf16[2,10,16,128]{3,2,1,0:T(8,128)(2,1)}, u32[]{:S(2)}) copy-start(bf16[2,10,16,128]{3,2,1,0:T(8,128)(2,1)} %get-tuple-element.17) | copy-start | bytes 245764
  43.5 10.6 %collective-permute-start.1 = (bf16[2,2,16,128]{3,2,1,0:T(8,128)(2,1)S(1)}, bf16[2,2,16,128]{3,2,1,0:T(8,128)(2,1)S(1)}, u32[]{:S(2)}, u32[]{:S(2)}) collective-permute-start(bf16[2,2,16,128]{3,2,1,0:T(8,128)(2,1)S(1)} %pad_maximum_fusion.4), channel_id=1, source_target_pairs={{2,0},{3,1},{4,2},{5,3},{6,4},{7,5},{8,6},{9,7},{10,8},{11,9},{12,... | collective-permute-start | bytes 49160 | tf_op jit(solution)/shard_map/ppermute | solution.py:357
  47.3 23.2 %all-to-all-start.1 = ((bf16[16,8,16,128]{3,2,1,0:T(8,128)(2,1)}), bf16[16,8,16,128]{3,2,1,0:T(8,128)(2,1)S(1)}, u32[]{:S(2)}, u32[]{:S(2)}) async-start(bf16[16,8,16,128]{3,2,1,0:T(8,128)(2,1)} %broadcast_in_dim.2), calls=%async_computation.1 | async-start | bytes 1048576 | tf_op jit(solution)/shard_map/all_to_all | solution.py:360
  60.1 7.8 %collective-permute-start.2 = (bf16[2,34,16,128]{3,2,1,0:T(8,128)(2,1)S(1)}, bf16[2,34,16,128]{3,2,1,0:T(8,128)(2,1)S(1)}, u32[]{:S(2)}, u32[]{:S(2)}) collective-permute-start(bf16[2,34,16,128]{3,2,1,0:T(8,128)(2,1)S(1)} %bitcast.16), channel_id=1, source_target_pairs={{384,128},{0,256},{640,384},{256,512},{896,640},{512,768},{385,129... | collective-permute-start | bytes 835592 | tf_op jit(solution)/shard_map/ppermute | solution.py:366
  61.4 6.5 %copy-start.4 = (f32[3,1024]{1,0:T(4,128)S(1)}, f32[3,1024]{1,0:T(4,128)}, u32[]{:S(2)}) copy-start(f32[3,1024]{1,0:T(4,128)} %points_ref.3) | copy-start | bytes 36868
  61.5 6.5 %copy-start.5 = (s32[4,8]{1,0:T(4,128)S(1)}, s32[4,8]{1,0:T(4,128)}, u32[]{:S(2)}) copy-start(s32[4,8]{1,0:T(4,128)} %list_ref.3) | copy-start | bytes 388
  61.5 6.4 %copy-start.8 = (s32[4]{0:T(128)S(1)}, s32[4]{0:T(128)}, u32[]{:S(2)}) copy-start(s32[4]{0:T(128)} %count_ref.3) | copy-start | bytes 52
  61.5 9.0 %collective-permute-start.3 = (bf16[14,16,128]{2,1,0:T(8,128)(2,1)S(1)}, bf16[14,16,128]{2,1,0:T(8,128)(2,1)S(1)}, u32[]{:S(2)}, u32[]{:S(2)}) collective-permute-start(bf16[14,16,128]{2,1,0:T(8,128)(2,1)S(1)} %bitcast.22), channel_id=1, source_target_pairs={{640,128},{896,384},{0,512},{256,768},{641,129},{897,385},{1,513},... | collective-permute-start | bytes 172040 | tf_op jit(solution)/shard_map/ppermute | solution.py:368
  70.5 6.6 %copy-start = (bf16[4,16,64,64]{3,2,1,0:T(8,128)(2,1)S(1)}, bf16[4,16,64,64]{3,2,1,0:T(8,128)(2,1)}, u32[]{:S(2)}) copy-start(bf16[4,16,64,64]{3,2,1,0:T(8,128)(2,1)} %leaf_coupling_ref.1) | copy-start | bytes 1572868
  70.6 6.5 %collective-permute-start.4 = (bf16[142,16,128]{2,1,0:T(8,128)(2,1)S(1)}, bf16[142,16,128]{2,1,0:T(8,128)(2,1)S(1)}, u32[]{:S(2)}, u32[]{:S(2)}) collective-permute-start(bf16[142,16,128]{2,1,0:T(8,128)(2,1)S(1)} %pad_maximum_fusion.last_ref), channel_id=1, source_target_pairs={{0,128},{128,0},{1,129},{129,1},{2,130},{130,2},{3,131},{131,3},{4... | collective-permute-start | bytes 1744904 | tf_op jit(solution)/shard_map/ppermute | solution.py:374
  74.4 2.7 %copy-start.1 = (bf16[4,256,64]{1,2,0:T(8,128)(2,1)S(1)}, bf16[4,256,64]{1,2,0:T(8,128)(2,1)}, u32[]{:S(2)}) copy-start(bf16[4,256,64]{1,2,0:T(8,128)(2,1)} %param.15) | copy-start | bytes 393220
  74.4 2.7 %copy-start.2 = (bf16[1,16,64,64]{3,2,1,0:T(8,128)(2,1)S(1)}, bf16[1,16,64,64]{3,2,1,0:T(8,128)(2,1)}, u32[]{:S(2)}) copy-start(bf16[1,16,64,64]{3,2,1,0:T(8,128)(2,1)} %coarse_coupling_ref.1) | copy-start | bytes 393220
  74.4 2.7 %copy-start.3 = (bf16[4,64,64]{2,1,0:T(8,128)(2,1)S(1)}, bf16[4,64,64]{2,1,0:T(8,128)(2,1)}, u32[]{:S(2)}) copy-start(bf16[4,64,64]{2,1,0:T(8,128)(2,1)} %transfer_ref.1) | copy-start | bytes 98308
  74.4 2.7 %copy-start.6 = (s32[1024]{0:T(1024)S(1)}, s32[1024]{0:T(1024)}, u32[]{:S(2)}) copy-start(s32[1024]{0:T(1024)} %owner_ref.1) | copy-start | bytes 12292
  74.5 2.6 %copy-start.7 = (s32[4,16]{1,0:T(4,128)S(1)}, s32[4,16]{1,0:T(4,128)}, u32[]{:S(2)}) copy-start(s32[4,16]{1,0:T(4,128)} %coupling_list_ref.1) | copy-start | bytes 772
  74.5 2.6 %copy-start.9 = (s32[4]{0:T(128)S(1)}, s32[4]{0:T(128)}, u32[]{:S(2)}) copy-start(s32[4]{0:T(128)} %coupling_count_ref.1) | copy-start | bytes 52
  74.5 2.6 %copy-start.10 = (s32[1,16]{1,0:T(1,128)S(1)}, s32[1,16]{1,0:T(1,128)}, u32[]{:S(2)}) copy-start(s32[1,16]{1,0:T(1,128)} %coarse_list_ref.1) | copy-start | bytes 196

commit v10 on v9

--- a/solution.py
+++ b/solution.py
@@ -15,17 +15,6 @@
 NT = (((1,), (1,)), ((), ()))
 
 BLOCK = 10
-
-
-def fetch_all(sources, targets, done_ref):
-    copies = [
-        pltpu.make_async_copy(source, target, done_ref.at[place])
-        for place, (source, target) in enumerate(zip(sources, targets))
-    ]
-    for copy in copies:
-        copy.start()
-    for copy in copies:
-        copy.wait()
 
 
 def pack_kernel(
@@ -40,38 +29,45 @@
     transfer_ref,
     done_ref,
 ):
-    fetch_all(
-        (points_hbm, basis_hbm, transfer_hbm),
-        (points_ref, basis_ref, transfer_ref),
-        done_ref,
-    )
+    pairs = ((points_hbm, points_ref), (basis_hbm, basis_ref), (transfer_hbm, transfer_ref))
+    copies = [
+        pltpu.make_async_copy(source, target, done_ref.at[place])
+        for place, (source, target) in enumerate(pairs)
+    ]
+    for copy in copies:
+        copy.start()
     block_ref = copies_ref.at[0]
+    copies[0].wait()
     points = points_ref[...]
     part_hi = points.astype(BF16).astype(F32)
     rest = points - part_hi
     part_mid = rest.astype(BF16).astype(F32)
     part_lo = rest - part_mid
     parts = jnp.concatenate([part_hi, part_mid, part_lo[:2]], axis=0)
-    cluster = jnp.zeros((8, 64), F32)
-    coeffs = []
     last_rows = []
     for leaf in range(4):
         low = slice(leaf * 256, leaf * 256 + 128)
         high = slice(leaf * 256 + 128, leaf * 256 + 256)
-        sides = rhs_ref[:, leaf * 256 : leaf * 256 + 256]
-        coeff = lax.dot_general(sides, basis_ref[leaf], NT, preferred_element_type=F32)
-        coeff = coeff.astype(BF16)
-        cluster = cluster + jnp.dot(coeff, transfer_ref[leaf], preferred_element_type=F32)
-        coeffs.append(coeff.astype(F32))
-        wide = sides.astype(F32)
+        wide = rhs_ref[:, leaf * 256 : leaf * 256 + 256].astype(F32)
         block_ref[leaf] = jnp.concatenate([wide[:, :128], wide[:, 128:]], axis=0).astype(BF16)
         block_ref[4 + leaf] = jnp.concatenate([parts[:, low], parts[:, high]], axis=0).astype(BF16)
         last_rows += [part_lo[2:3, low], part_lo[2:3, high]]
     block_ref[8] = jnp.concatenate(last_rows + [jnp.zeros((8, 128), F32)], axis=0).astype(BF16)
+    copies[1].wait()
+    coeffs = []
+    for leaf in range(4):
+        sides = rhs_ref[:, leaf * 256 : leaf * 256 + 256]
+        coeff = lax.dot_general(sides, basis_ref[leaf], NT, preferred_element_type=F32)
+        coeffs.append(coeff.astype(BF16).astype(F32))
     block_ref[9] = jnp.concatenate(
         [jnp.concatenate(coeffs[:2], axis=1), jnp.concatenate(coeffs[2:], axis=1)], axis=0
     ).astype(BF16)
     copies_ref[1] = block_ref[...]
+    copies[2].wait()
+    cluster = jnp.zeros((8, 64), F32)
+    for leaf in range(4):
+        coeff = coeffs[leaf].astype(BF16)
+        cluster = cluster + jnp.dot(coeff, transfer_ref[leaf], preferred_element_type=F32)
     packed = jnp.concatenate([cluster[:4], cluster[4:]], axis=1).astype(BF16)
     cluster_ref[...] = jnp.broadcast_to(packed[None], cluster_ref.shape)
 

time: 81.3 us -> 81.4 us (level)
  no operation moved by 1% of the time
where the time goes in v10:
time: 81.4 us; the launch traced here: 80.8 us
  starting transfers between devices  39.5 us (49%)
  blocking collectives  22 us (27%)
  Pallas kernels  11.5 us (14%)
  waiting for transfers between devices  5.8 us (7%)
  local copies, waits for them, and re-layouts  1.01 us (1%)
  between operations  1 us (1%)
    all_to_all x1, starting transfers between devices, per_device(): lax.all_to_all(cluster, 'z', 0, 0, tiled=True, axis_index_groups=[turned])  23.6 us
    all_gather x1, blocking collectives, per_device(): chip = lax.all_gather(blocks, 'core', axis=0, tiled=False)  15.9 us
    all_to_all x1, starting transfers between devices, per_device(): lax.all_to_all(line, ('x', 'y'), 0, 0, tiled=True).reshape(groups, 16, 128)  6.75 us
    all_gather x1, blocking collectives, per_device(): window = lax.all_gather(window, 'core', axis=0, tiled=False)  6.02 us
    pallas_call x2, Pallas kernels, near_call(): pl.pallas_call(functools.partial(near_kernel, base_leaf, cols), out_shape...  5.12 us
    ppermute x1, waiting for transfers between devices, per_device(): beside = lax.ppermute(window, ('x', 'core'), along_x(1))  5.11 us
    pallas_call x1, Pallas kernels, far_call(): pl.pallas_call(functools.partial(far_kernel, groups, cols, zs), out_shape...  3.6 us
    ppermute x1, starting transfers between devices, per_device(): last_mate = lax.ppermute(last, 'core', [(0, 1), (1, 0)])  3.15 us
  transfers between devices with their start and end apart: 7, of which 2 were waited for; matrix products, arithmetic and copies ran while one was open for 1% of the time, Pallas kernels for 6%

profile of v10, /device:TPU:1, one launch (start us, length us, event | category | flops | bytes accessed | tf_op | source)
XLA Modules:
  0.0 80.8 jit_solution(16439305257567481265)
XLA Ops:
  0.0 2.7 %pack.1 = (bf16[2,10,16,128]{3,2,1,0:T(8,128)(2,1)}, bf16[32,4,128]{2,1,0:T(4,128)(2,1)}) custom-call(bf16[8,1024]{1,0:T(8,128)(2,1)} %rhs_ref.1, f32[3,1024]{1,0:T(4,128)} %points_ref.3, bf16[4,64,256]{2,1,0:T(8,128)(2,1)} %bitcast.20, bf16[4,64,64]{2,1,0:T(8,128)(2,1)} %transfer_ref.1), custom_call_target="tpu_custom_call" | custom-call | tf_op jit(solution)/shard_map/pack/pallas_call | solution.py:307
  2.7 15.9 %all-gather = bf16[4,10,16,128]{3,2,1,0:T(8,128)(2,1)S(1)} all-gather(bf16[2,10,16,128]{3,2,1,0:T(8,128)(2,1)} %get-tuple-element.17), channel_id=2, replica_groups=mesh['x'=4,'core'=2,'y'=4,'z'=32] {'core'}, dimensions={0}, use_global_device_ids=true | all-gather | bytes 245760 | tf_op jit(solution)/shard_map/all_gather | solution.py:346
  18.7 1.3 %collective-permute-start = (bf16[2,2,10,16,128]{4,3,2,1,0:T(8,128)(2,1)S(1)}, bf16[2,2,10,16,128]{4,3,2,1,0:T(8,128)(2,1)S(1)}, u32[]{:S(2)}, u32[]{:S(2)}) collective-permute-start(bf16[2,2,10,16,128]{4,3,2,1,0:T(8,128)(2,1)S(1)} %bitcast.27), channel_id=1, source_target_pairs={{1,0},{2,1},{3,2},{4,3},{5,4},{6,5},{7,6},{8,7},{9,8},{10,9},{11,1... | collective-permute-start | bytes 491528 | tf_op jit(solution)/shard_map/ppermute | solution.py:347
  20.0 23.6 %all-to-all-start = ((bf16[32,4,128]{2,1,0:T(4,128)(2,1)}), bf16[32,4,128]{2,1,0:T(4,128)(2,1)S(1)}, u32[]{:S(2)}, u32[]{:S(2)}) async-start(bf16[32,4,128]{2,1,0:T(4,128)(2,1)} %get-tuple-element.19), calls=%async_computation | async-start | bytes 65536 | tf_op jit(solution)/shard_map/all_to_all | solution.py:349
  43.6 0.0 copy-start.11
  43.6 0.0 collective-permute-done
  43.6 2.2 %collective-permute-start.1 = (bf16[2,2,16,128]{3,2,1,0:T(8,128)(2,1)S(1)}, bf16[2,2,16,128]{3,2,1,0:T(8,128)(2,1)S(1)}, u32[]{:S(2)}, u32[]{:S(2)}) collective-permute-start(bf16[2,2,16,128]{3,2,1,0:T(8,128)(2,1)S(1)} %pad_maximum_fusion.4), channel_id=1, source_target_pairs={{2,0},{3,1},{4,2},{5,3},{6,4},{7,5},{8,6},{9,7},{10,8},{11,9},{12,... | collective-permute-start | bytes 49160 | tf_op jit(solution)/shard_map/ppermute | solution.py:353
  45.8 0.0 copy-done.11
  45.9 0.7 all-to-all-done
  46.5 0.9 %broadcast_in_dim.2 = bf16[16,8,16,128]{3,2,1,0:T(8,128)(2,1)} broadcast(bf16[8,16,128]{2,1,0:T(8,128)(2,1)S(1)} %bitcast.29), dimensions={1,2,3} | broadcast | bytes 557056 | tf_op jit(solution)/shard_map/broadcast_in_dim | solution.py:355
  47.4 6.8 %all-to-all-start.1 = ((bf16[16,8,16,128]{3,2,1,0:T(8,128)(2,1)}), bf16[16,8,16,128]{3,2,1,0:T(8,128)(2,1)S(1)}, u32[]{:S(2)}, u32[]{:S(2)}) async-start(bf16[16,8,16,128]{3,2,1,0:T(8,128)(2,1)} %broadcast_in_dim.2), calls=%async_computation.1 | async-start | bytes 1048576 | tf_op jit(solution)/shard_map/all_to_all | solution.py:356
  54.2 0.0 collective-permute-done.1
  54.2 6.0 %all-gather.1 = bf16[68,16,128]{2,1,0:T(8,128)(2,1)S(1)} all-gather(bf16[34,16,128]{2,1,0:T(8,128)(2,1)S(1)} %pad_maximum_fusion.1), channel_id=3, replica_groups=mesh['x'=4,'core'=2,'y'=4,'z'=32] {'core'}, dimensions={0}, use_global_device_ids=true | all-gather | bytes 417792 | tf_op jit(solution)/shard_map/all_gather | solution.py:361
  60.3 1.3 %collective-permute-start.2 = (bf16[2,34,16,128]{3,2,1,0:T(8,128)(2,1)S(1)}, bf16[2,34,16,128]{3,2,1,0:T(8,128)(2,1)S(1)}, u32[]{:S(2)}, u32[]{:S(2)}) collective-permute-start(bf16[2,34,16,128]{3,2,1,0:T(8,128)(2,1)S(1)} %bitcast.16), channel_id=1, source_target_pairs={{384,128},{0,256},{640,384},{256,512},{896,640},{512,768},{385,129... | collective-permute-start | bytes 835592 | tf_op jit(solution)/shard_map/ppermute | solution.py:362
  61.6 0.0 copy-start.4
  61.6 0.0 copy-start.5
  61.6 0.0 copy-start.8
  61.6 1.3 %collective-permute-start.3 = (bf16[14,16,128]{2,1,0:T(8,128)(2,1)S(1)}, bf16[14,16,128]{2,1,0:T(8,128)(2,1)S(1)}, u32[]{:S(2)}, u32[]{:S(2)}) collective-permute-start(bf16[14,16,128]{2,1,0:T(8,128)(2,1)S(1)} %bitcast.22), channel_id=1, source_target_pairs={{640,128},{896,384},{0,512},{256,768},{641,129},{897,385},{1,513},... | collective-permute-start | bytes 172040 | tf_op jit(solution)/shard_map/ppermute | solution.py:364
  62.9 5.1 %collective-permute-done.2.beside_ref = bf16[2,34,16,128]{3,2,1,0:T(8,128)(2,1)S(1)} collective-permute-done((bf16[2,34,16,128]{3,2,1,0:T(8,128)(2,1)S(1)}, bf16[2,34,16,128]{3,2,1,0:T(8,128)(2,1)S(1)}, u32[]{:S(2)}, u32[]{:S(2)}) %collective-permute-start.2) | collective-permute-done | bytes 278560 | tf_op jit(solution)/shard_map/ppermute | solution.py:362
  68.0 0.0 copy-done.4
  68.0 0.0 copy-done.5
  68.0 0.0 copy-done.8
  68.0 2.6 %near0.1.near_low_ref = f32[2,8,256]{2,1,0:T(8,128)S(1)} custom-call(s32[4,8]{1,0:T(4,128)S(1)} %copy-done.5, s32[4]{0:T(128)S(1)} %copy-done.8, f32[3,1024]{1,0:T(4,128)S(1)} %copy-done.4, bf16[2,34,16,128]{3,2,1,0:T(8,128)(2,1)S(1)} %bitcast.18, bf16[2,34,16,128]{3,2,1,0:T(8,128)(2,1)S(1)} %collective-permute-done.2.beside_ref), custom_call_target="tpu_custom_call" | custom-call | flops 100000000 | bytes 1200000 | tf_op jit(solution)/shard_map/near0/pallas_call | solution.py:257
  70.6 0.0 copy-start
  70.6 0.0 collective-permute-done.3.beyond_ref
  70.6 0.0 all-to-all-done.1
  70.7 0.1 pad_maximum_fusion.last_ref
  70.7 3.1 %collective-permute-start.4 = (bf16[142,16,128]{2,1,0:T(8,128)(2,1)S(1)}, bf16[142,16,128]{2,1,0:T(8,128)(2,1)S(1)}, u32[]{:S(2)}, u32[]{:S(2)}) collective-permute-start(bf16[142,16,128]{2,1,0:T(8,128)(2,1)S(1)} %pad_maximum_fusion.last_ref), channel_id=1, source_target_pairs={{0,128},{128,0},{1,129},{129,1},{2,130},{130,2},{3,131},{131,3},{4... | collective-permute-start | bytes 1744904 | tf_op jit(solution)/shard_map/ppermute | solution.py:370
  74.5 0.0 copy-start.1
  74.5 0.0 copy-start.2
  74.5 0.0 copy-start.3
  74.6 0.0 copy-start.6
  74.6 0.0 copy-start.7
  74.6 0.0 copy-start.9
  74.6 0.0 copy-start.10
  74.6 2.6 %near2.1.near_high_ref = f32[2,8,256]{2,1,0:T(8,128)S(1)} custom-call(s32[4,8]{1,0:T(4,128)S(1)} %copy-done.5, s32[4]{0:T(128)S(1)} %copy-done.8, f32[3,1024]{1,0:T(4,128)S(1)} %copy-done.4, bf16[2,34,16,128]{3,2,1,0:T(8,128)(2,1)S(1)} %bitcast.19, bf16[2,34,16,128]{3,2,1,0:T(8,128)(2,1)S(1)} %collective-permute-done.2.beside_ref), custom_call_target="tpu_custom_call" | custom-call | flops 100000000 | bytes 1200000 | tf_op jit(solution)/shard_map/near2/pallas_call | solution.py:257
  77.2 0.0 collective-permute-done.4.last_mate_ref
  77.2 0.0 copy-done
  77.2 0.0 copy-done.1
  77.2 0.0 copy-done.2
  77.2 0.0 copy-done.3
  77.2 0.0 copy-done.6
  77.2 0.0 copy-done.7
  77.2 0.0 copy-done.9
  77.2 0.0 copy-done.10
  77.2 3.6 %far.1 = bf16[8,1024]{1,0:T(8,128)(2,1)} custom-call(s32[4,16]{1,0:T(4,128)S(1)} %copy-done.7, s32[4]{0:T(128)S(1)} %copy-done.9, s32[1,16]{1,0:T(1,128)S(1)} %copy-done.10, s32[1]{0:T(128)S(6)} %copy.18.coarse_count_ref, s32[1024]{0:T(1024)S(1)} %copy-done.6, bf16[14,16,128]{2,1,0:T(8,128)(2,1)S(1)} %bitcast.23, ...), custom_call_target="tpu_custom_call" | custom-call | tf_op jit(solution)/shard_map/far/pallas_call | solution.py:272
  (12 shorter events, 0.1 us)
Async XLA Ops:
  18.7 24.9 %collective-permute-start = (bf16[2,2,10,16,128]{4,3,2,1,0:T(8,128)(2,1)S(1)}, bf16[2,2,10,16,128]{4,3,2,1,0:T(8,128)(2,1)S(1)}, u32[]{:S(2)}, u32[]{:S(2)}) collective-permute-start(bf16[2,2,10,16,128]{4,3,2,1,0:T(8,128)(2,1)S(1)} %bitcast.27), channel_id=1, source_target_pairs={{1,0},{2,1},{3,2},{4,3},{5,4},{6,5},{7,6},{8,7},{9,8},{10,9},{11,1... | collective-permute-start | bytes 491528 | tf_op jit(solution)/shard_map/ppermute | solution.py:347
  20.0 26.5 %all-to-all-start = ((bf16[32,4,128]{2,1,0:T(4,128)(2,1)}), bf16[32,4,128]{2,1,0:T(4,128)(2,1)S(1)}, u32[]{:S(2)}, u32[]{:S(2)}) async-start(bf16[32,4,128]{2,1,0:T(4,128)(2,1)} %get-tuple-element.19), calls=%async_computation | async-start | bytes 65536 | tf_op jit(solution)/shard_map/all_to_all | solution.py:349
  43.6 2.3 %copy-start.11 = (bf16[2,10,16,128]{3,2,1,0:T(8,128)(2,1)S(1)}, bf16[2,10,16,128]{3,2,1,0:T(8,128)(2,1)}, u32[]{:S(2)}) copy-start(bf16[2,10,16,128]{3,2,1,0:T(8,128)(2,1)} %get-tuple-element.17) | copy-start | bytes 245764
  43.6 10.6 %collective-permute-start.1 = (bf16[2,2,16,128]{3,2,1,0:T(8,128)(2,1)S(1)}, bf16[2,2,16,128]{3,2,1,0:T(8,128)(2,1)S(1)}, u32[]{:S(2)}, u32[]{:S(2)}) collective-permute-start(bf16[2,2,16,128]{3,2,1,0:T(8,128)(2,1)S(1)} %pad_maximum_fusion.4), channel_id=1, source_target_pairs={{2,0},{3,1},{4,2},{5,3},{6,4},{7,5},{8,6},{9,7},{10,8},{11,9},{12,... | collective-permute-start | bytes 49160 | tf_op jit(solution)/shard_map/ppermute | solution.py:353
  47.4 23.2 %all-to-all-start.1 = ((bf16[16,8,16,128]{3,2,1,0:T(8,128)(2,1)}), bf16[16,8,16,128]{3,2,1,0:T(8,128)(2,1)S(1)}, u32[]{:S(2)}, u32[]{:S(2)}) async-start(bf16[16,8,16,128]{3,2,1,0:T(8,128)(2,1)} %broadcast_in_dim.2), calls=%async_computation.1 | async-start | bytes 1048576 | tf_op jit(solution)/shard_map/all_to_all | solution.py:356
  60.3 7.8 %collective-permute-start.2 = (bf16[2,34,16,128]{3,2,1,0:T(8,128)(2,1)S(1)}, bf16[2,34,16,128]{3,2,1,0:T(8,128)(2,1)S(1)}, u32[]{:S(2)}, u32[]{:S(2)}) collective-permute-start(bf16[2,34,16,128]{3,2,1,0:T(8,128)(2,1)S(1)} %bitcast.16), channel_id=1, source_target_pairs={{384,128},{0,256},{640,384},{256,512},{896,640},{512,768},{385,129... | collective-permute-start | bytes 835592 | tf_op jit(solution)/shard_map/ppermute | solution.py:362
  61.6 6.5 %copy-start.4 = (f32[3,1024]{1,0:T(4,128)S(1)}, f32[3,1024]{1,0:T(4,128)}, u32[]{:S(2)}) copy-start(f32[3,1024]{1,0:T(4,128)} %points_ref.3) | copy-start | bytes 36868
  61.6 6.5 %copy-start.5 = (s32[4,8]{1,0:T(4,128)S(1)}, s32[4,8]{1,0:T(4,128)}, u32[]{:S(2)}) copy-start(s32[4,8]{1,0:T(4,128)} %list_ref.3) | copy-start | bytes 388
  61.6 6.4 %copy-start.8 = (s32[4]{0:T(128)S(1)}, s32[4]{0:T(128)}, u32[]{:S(2)}) copy-start(s32[4]{0:T(128)} %count_ref.3) | copy-start | bytes 52
  61.6 9.0 %collective-permute-start.3 = (bf16[14,16,128]{2,1,0:T(8,128)(2,1)S(1)}, bf16[14,16,128]{2,1,0:T(8,128)(2,1)S(1)}, u32[]{:S(2)}, u32[]{:S(2)}) collective-permute-start(bf16[14,16,128]{2,1,0:T(8,128)(2,1)S(1)} %bitcast.22), channel_id=1, source_target_pairs={{640,128},{896,384},{0,512},{256,768},{641,129},{897,385},{1,513},... | collective-permute-start | bytes 172040 | tf_op jit(solution)/shard_map/ppermute | solution.py:364
  70.6 6.6 %copy-start = (bf16[4,16,64,64]{3,2,1,0:T(8,128)(2,1)S(1)}, bf16[4,16,64,64]{3,2,1,0:T(8,128)(2,1)}, u32[]{:S(2)}) copy-start(bf16[4,16,64,64]{3,2,1,0:T(8,128)(2,1)} %leaf_coupling_ref.1) | copy-start | bytes 1572868
  70.7 6.5 %collective-permute-start.4 = (bf16[142,16,128]{2,1,0:T(8,128)(2,1)S(1)}, bf16[142,16,128]{2,1,0:T(8,128)(2,1)S(1)}, u32[]{:S(2)}, u32[]{:S(2)}) collective-permute-start(bf16[142,16,128]{2,1,0:T(8,128)(2,1)S(1)} %pad_maximum_fusion.last_ref), channel_id=1, source_target_pairs={{0,128},{128,0},{1,129},{129,1},{2,130},{130,2},{3,131},{131,3},{4... | collective-permute-start | bytes 1744904 | tf_op jit(solution)/shard_map/ppermute | solution.py:370
  74.5 2.7 %copy-start.1 = (bf16[4,256,64]{1,2,0:T(8,128)(2,1)S(1)}, bf16[4,256,64]{1,2,0:T(8,128)(2,1)}, u32[]{:S(2)}) copy-start(bf16[4,256,64]{1,2,0:T(8,128)(2,1)} %param.15) | copy-start | bytes 393220
  74.5 2.7 %copy-start.2 = (bf16[1,16,64,64]{3,2,1,0:T(8,128)(2,1)S(1)}, bf16[1,16,64,64]{3,2,1,0:T(8,128)(2,1)}, u32[]{:S(2)}) copy-start(bf16[1,16,64,64]{3,2,1,0:T(8,128)(2,1)} %coarse_coupling_ref.1) | copy-start | bytes 393220
  74.5 2.7 %copy-start.3 = (bf16[4,64,64]{2,1,0:T(8,128)(2,1)S(1)}, bf16[4,64,64]{2,1,0:T(8,128)(2,1)}, u32[]{:S(2)}) copy-start(bf16[4,64,64]{2,1,0:T(8,128)(2,1)} %transfer_ref.1) | copy-start | bytes 98308
  74.6 2.7 %copy-start.6 = (s32[1024]{0:T(1024)S(1)}, s32[1024]{0:T(1024)}, u32[]{:S(2)}) copy-start(s32[1024]{0:T(1024)} %owner_ref.1) | copy-start | bytes 12292
  74.6 2.7 %copy-start.7 = (s32[4,16]{1,0:T(4,128)S(1)}, s32[4,16]{1,0:T(4,128)}, u32[]{:S(2)}) copy-start(s32[4,16]{1,0:T(4,128)} %coupling_list_ref.1) | copy-start | bytes 772
  74.6 2.6 %copy-start.9 = (s32[4]{0:T(128)S(1)}, s32[4]{0:T(128)}, u32[]{:S(2)}) copy-start(s32[4]{0:T(128)} %coupling_count_ref.1) | copy-start | bytes 52
  74.6 2.6 %copy-start.10 = (s32[1,16]{1,0:T(1,128)S(1)}, s32[1,16]{1,0:T(1,128)}, u32[]{:S(2)}) copy-start(s32[1,16]{1,0:T(1,128)} %coarse_list_ref.1) | copy-start | bytes 196
